TPU v7x, 32 devices: a whole 2x2x4 slice. The times are simulated.
32 devices in a mesh: dp: 8 (over y, x, core), seq: 4 (over z).
Axes of the slice: x: 2, y: 2, z: 4, core: 2. Of those that a mesh axis runs over, the one named last changes fastest.
Arguments:
- frames: bfloat16 [8, 2, 1024, 1024], P('dp', None, 'seq'), may hold values from -6 to 6
- cotangent: bfloat16 [8, 2, 1024, 1024], P('dp', None, 'seq'), may hold values from -6 to 6
- lengths: int32 [8, 2], replicated, may hold values from 50 to 1024, as said below
- assignment: int32 [8], replicated, may hold values from 0 to 7, each once
- norm_gains: bfloat16 [6, 1024], P(None, 'seq'), may hold values from 0.5 to 1.5
- norm_biases: bfloat16 [6, 1024], P(None, 'seq'), may hold values from -2 to 2
- expand_one: bfloat16 [1024, 4096], P('seq'), may hold values from -0.1875 to 0.1875
- shrink_one: bfloat16 [4096, 1024], P('seq'), may hold values from -0.09375 to 0.09375
- qkv_weight: bfloat16 [1024, 3072], P('seq'), may hold values from -0.25 to 0.25
- pos_weight: bfloat16 [1024, 1024], P(None, 'seq'), may hold values from -0.1875 to 0.1875
- pos_biases: bfloat16 [2, 1024], P(None, 'seq'), may hold values from -3 to 3
- attn_out: bfloat16 [1024, 1024], P('seq'), may hold values from -0.25 to 0.25
- conv_in: bfloat16 [1024, 2048], P('seq'), may hold values from -0.1875 to 0.1875
- conv_depth: bfloat16 [5, 1024], P(None, 'seq'), may hold values from -2.5 to 2.5
- conv_out: bfloat16 [1024, 1024], P('seq'), may hold values from -0.1875 to 0.1875
- expand_two: bfloat16 [1024, 4096], P('seq'), may hold values from -0.1875 to 0.1875
- shrink_two: bfloat16 [4096, 1024], P('seq'), may hold values from -0.25 to 0.25
Outputs:
- encoded: bfloat16 [8, 2, 1024, 1024], P('dp', None, 'seq')
- grad_input: float32 [8, 2, 1024, 1024], P('dp', None, 'seq')
- grad_norm_gains: float32 [6, 1024], P(None, 'seq')
- grad_norm_biases: float32 [6, 1024], P(None, 'seq')
- grad_expand_one: float32 [1024, 4096], P('seq')
- grad_shrink_one: float32 [4096, 1024], P('seq')
- grad_qkv_weight: float32 [1024, 3072], P('seq')
- grad_pos_weight: float32 [1024, 1024], P(None, 'seq')
- grad_pos_biases: float32 [2, 1024], P(None, 'seq')
- grad_attn_out: float32 [1024, 1024], P('seq')
- grad_conv_in: float32 [1024, 2048], P('seq')
- grad_conv_depth: float32 [5, 1024], P(None, 'seq')
- grad_conv_out: float32 [1024, 1024], P('seq')
- grad_expand_two: float32 [1024, 4096], P('seq')
- grad_shrink_two: float32 [4096, 1024], P('seq')
Inputs may be any that keep to these rules, and one draw needn't show every extreme that they name: lengths[b, u] is the number of real frames of utterance u of batch b; in every batch one utterance, which one drawn from the seed, has 1024 frames. A permutation: row g of frames and cotangent is batch assignment[g], whose lengths are row assignment[g] of lengths.
All inputs are finite; a program needn't handle non-finite values.
Results may differ from a plain program's by a relative error of at most 0.024.
Values may be sent and summed in bfloat16 or wider, within the bound.
A program may use at most 320 MiB of HBM per device.

v0:
```python
import math

import jax
import jax.numpy as jnp
from jax import lax
from jax.sharding import PartitionSpec as P

D = 1024
HEADS = 8
HEAD_DIM = 128
KERNEL = 5
UTT = 2
LEN = 1024
QUERY_BLOCK = 512


EPSILON = 1e-05


def with_halo(cells, sides, width):
    for axis, dim in sides:
        count = lax.axis_size(axis)
        ends = count - 1
        head = lax.slice_in_dim(cells, 0, width, axis=dim)
        tail = lax.slice_in_dim(cells, cells.shape[dim] - width, cells.shape[dim], axis=dim)
        cells = jnp.concatenate(
            [
                lax.ppermute(tail, axis, [(i, (i + 1) % count) for i in range(ends)]),
                cells,
                lax.ppermute(head, axis, [((i + 1) % count, i) for i in range(ends)]),
            ],
            axis=dim,
        )
    return cells


def layer_norm(stream, norm_gain, offset):
    average = jnp.mean(stream, axis=-1, keepdims=True)
    centred = stream - average
    spread = jnp.mean(centred * centred, axis=-1, keepdims=True)
    return centred * lax.rsqrt(spread + EPSILON) * norm_gain + offset


def swish(stream):
    return stream * jax.nn.sigmoid(stream)


def norm_swish(stream, norm_gain, offset):
    return swish(layer_norm(stream, norm_gain, offset))


def position_table(length, features):
    indices = jnp.arange(2 * length, dtype=jnp.int32)
    distance = (length - 1 - indices).astype(jnp.float32)
    halves = jnp.arange(features // 2, dtype=jnp.int32).astype(jnp.float32)
    frequency = jnp.exp(halves * (-2.0 * math.log(10000.0) / features))
    angles = distance[:, None] * frequency[None, :]
    return jnp.stack([jnp.sin(angles), jnp.cos(angles)], axis=-1).reshape(2 * length, features)


def skew(placed, block_rows, length):
    leading = placed.shape[:-2]
    span_width = placed.shape[-1]
    flattened = placed.reshape(leading + (block_rows * span_width,))
    flattened = flattened[..., block_rows - 1 : block_rows - 1 + block_rows * (span_width - 1)]
    return flattened.reshape(leading + (block_rows, span_width - 1))[..., :length]


def unskew(graded, block_rows, length):
    leading = graded.shape[:-2]
    span_width = length + block_rows
    untouched = [(0, 0)] * len(leading)
    padded = jnp.pad(graded, untouched + [(0, 0), (0, span_width - 1 - length)])
    flattened = padded.reshape(leading + (block_rows * (span_width - 1),))
    flattened = jnp.pad(flattened, untouched + [(block_rows - 1, 1)])
    return flattened.reshape(leading + (block_rows, span_width))


def ffn_forward(stream, norm_gain, offset, expand_weight, shrink_weight):
    normed, norm_pull = jax.vjp(layer_norm, stream, norm_gain, offset)
    normed = normed.astype(jnp.bfloat16)
    hidden = jnp.einsum("utd,df->utf", normed, expand_weight, preferred_element_type=jnp.float32)
    active = swish(hidden).astype(jnp.bfloat16)
    output = jnp.einsum("utf,fd->utd", active, shrink_weight, preferred_element_type=jnp.float32)
    return (output, (norm_pull, normed, hidden, active))


def ffn_backward(grad_output, kept_values, expand_weight, shrink_weight):
    norm_pull, normed, hidden, active = kept_values
    grad_output = grad_output.astype(jnp.bfloat16)
    grad_shrink = jnp.einsum("utf,utd->fd", active, grad_output, preferred_element_type=jnp.float32)
    grad_active = jnp.einsum(
        "utd,fd->utf", grad_output, shrink_weight, preferred_element_type=jnp.float32
    )
    swish_pull = jax.vjp(swish, hidden)[1]
    grad_hidden = swish_pull(grad_active)[0].astype(jnp.bfloat16)
    grad_expand = jnp.einsum("utd,utf->df", normed, grad_hidden, preferred_element_type=jnp.float32)
    grad_normed = jnp.einsum(
        "utf,df->utd", grad_hidden, expand_weight, preferred_element_type=jnp.float32
    )
    grad_stream, grad_gain, grad_offset = norm_pull(grad_normed)
    return (grad_stream, grad_gain, grad_offset, grad_expand, grad_shrink)


def block_logits(content_query, position_query, keys_heads, projected, keeping, starting):
    span_width = LEN + QUERY_BLOCK
    content_block = lax.slice_in_dim(content_query, starting, starting + QUERY_BLOCK, axis=1)
    position_block = lax.slice_in_dim(position_query, starting, starting + QUERY_BLOCK, axis=1)
    lowest = LEN - QUERY_BLOCK - starting
    window = lax.slice_in_dim(projected, lowest, lowest + span_width, axis=0)
    content = jnp.einsum(
        "uahe,ujhe->uhaj", content_block, keys_heads, preferred_element_type=jnp.float32
    )
    placed = jnp.einsum(
        "uahe,mhe->uham", position_block, window, preferred_element_type=jnp.float32
    )
    scores = content + skew(placed, QUERY_BLOCK, LEN)
    logits = jnp.where(keeping, scores * (1.0 / math.sqrt(HEAD_DIM)), -1000000000.0)
    return (logits, content_block, position_block, window, lowest)


def shards(
    frames,
    cotangent,
    lengths,
    assignment,
    norm_gains,
    norm_biases,
    expand_one,
    shrink_one,
    qkv_weight,
    pos_weight,
    pos_biases,
    attn_out,
    conv_in,
    conv_depth,
    conv_out,
    expand_two,
    shrink_two,
):
    seq_count = lax.axis_size("seq")
    seq_index = lax.axis_index("seq")
    local_len = frames.shape[2]
    heads_here = HEADS // seq_count
    margin = (KERNEL - 1) // 2
    span_width = LEN + QUERY_BLOCK
    block_count = LEN // QUERY_BLOCK
    batch_index = assignment[lax.axis_index("dp")]
    lengths_row = lengths[batch_index]
    frame_ids = seq_index * local_len + jnp.arange(local_len, dtype=jnp.int32)
    validity = (frame_ids[None, :] < lengths_row[:, None]).astype(jnp.float32)
    keeping = (jnp.arange(LEN, dtype=jnp.int32)[None, :] < lengths_row[:, None])[:, None, None, :]
    (
        gains_all,
        biases_all,
        depth_all,
        expand_a,
        shrink_a,
        qkv_all,
        attn_all,
        conv_in_all,
        conv_out_all,
        expand_b,
        shrink_b,
    ) = (
        lax.all_gather(norm_gains, "seq", axis=1, tiled=True),
        lax.all_gather(norm_biases, "seq", axis=1, tiled=True),
        lax.all_gather(conv_depth, "seq", axis=1, tiled=True),
        lax.all_gather(expand_one, "seq", axis=0, tiled=True),
        lax.all_gather(shrink_one, "seq", axis=0, tiled=True),
        lax.all_gather(qkv_weight, "seq", axis=0, tiled=True),
        lax.all_gather(attn_out, "seq", axis=0, tiled=True),
        lax.all_gather(conv_in, "seq", axis=0, tiled=True),
        lax.all_gather(conv_out, "seq", axis=0, tiled=True),
        lax.all_gather(expand_two, "seq", axis=0, tiled=True),
        lax.all_gather(shrink_two, "seq", axis=0, tiled=True),
    )
    gain_values = gains_all.astype(jnp.float32)
    bias_values = biases_all.astype(jnp.float32)
    depth_values = depth_all.astype(jnp.float32)
    stream_in = frames[0].astype(jnp.float32)
    ffn_first, kept_first = ffn_forward(
        stream_in, gain_values[0], bias_values[0], expand_a, shrink_a
    )
    section_one = stream_in + 0.5 * ffn_first
    normed, attn_pull = jax.vjp(layer_norm, section_one, gain_values[1], bias_values[1])
    attn_normed = normed.astype(jnp.bfloat16)
    packed = jnp.einsum(
        "utd,de->ute", attn_normed, qkv_all, preferred_element_type=jnp.float32
    ).astype(jnp.bfloat16)
    packed = packed.reshape(UTT, local_len, 3, HEADS, HEAD_DIM)
    head_major = lax.all_to_all(packed, "seq", split_axis=3, concat_axis=1, tiled=True)
    queries = head_major[:, :, 0]
    keys_heads = head_major[:, :, 1]
    values_heads = head_major[:, :, 2]
    sinusoid = position_table(LEN, D).astype(jnp.bfloat16)
    projected = jnp.dot(sinusoid, pos_weight, preferred_element_type=jnp.float32).astype(
        jnp.bfloat16
    )
    projected = projected.reshape(2 * LEN, heads_here, HEAD_DIM)
    bias_pair = pos_biases.astype(jnp.float32).reshape(2, heads_here, HEAD_DIM)
    query_float = queries.astype(jnp.float32)
    content_query = (query_float + bias_pair[0]).astype(jnp.bfloat16)
    position_query = (query_float + bias_pair[1]).astype(jnp.bfloat16)
    pieces = []
    normalizers = []
    for block_index in range(block_count):
        starting = block_index * QUERY_BLOCK
        logits = block_logits(
            content_query, position_query, keys_heads, projected, keeping, starting
        )[0]
        maximum = jnp.max(logits, axis=-1, keepdims=True)
        exponent = jnp.exp(logits - maximum)
        denominator = jnp.sum(exponent, axis=-1, keepdims=True)
        weights = (exponent / denominator).astype(jnp.bfloat16)
        pieces.append(
            jnp.einsum("uhaj,ujhe->uahe", weights, values_heads, preferred_element_type=jnp.float32)
        )
        normalizers.append(maximum + jnp.log(denominator))
    attn_heads = jnp.concatenate(pieces, axis=1).astype(jnp.bfloat16)
    attn_time = lax.all_to_all(attn_heads, "seq", split_axis=1, concat_axis=2, tiled=True).reshape(
        UTT, local_len, D
    )
    attn_delta = jnp.einsum("ute,ed->utd", attn_time, attn_all, preferred_element_type=jnp.float32)
    section_two = section_one + attn_delta
    normed, conv_pull = jax.vjp(layer_norm, section_two, gain_values[2], bias_values[2])
    conv_normed = normed.astype(jnp.bfloat16)
    doubled = jnp.einsum(
        "utd,de->ute", conv_normed, conv_in_all, preferred_element_type=jnp.float32
    )

    def gate_rows(doubled_in):
        return doubled_in[..., :D] * jax.nn.sigmoid(doubled_in[..., D:]) * validity[..., None]

    gated_rows, gate_pull = jax.vjp(gate_rows, doubled)
    gated_rows = gated_rows.astype(jnp.bfloat16)
    rimmed = with_halo(gated_rows, (("seq", 1),), margin)
    depthwise = depth_values[0] * rimmed[:, 0:local_len]
    for shift_index in range(1, KERNEL):
        depthwise = (
            depthwise + depth_values[shift_index] * rimmed[:, shift_index : shift_index + local_len]
        )
    conv_active, inner_pull = jax.vjp(norm_swish, depthwise, gain_values[3], bias_values[3])
    conv_active = conv_active.astype(jnp.bfloat16)
    conv_delta = jnp.einsum(
        "utd,de->ute", conv_active, conv_out_all, preferred_element_type=jnp.float32
    )
    section_three = section_two + conv_delta
    ffn_second, kept_second = ffn_forward(
        section_three, gain_values[4], bias_values[4], expand_b, shrink_b
    )
    section_four = section_three + 0.5 * ffn_second
    encoded, final_pull = jax.vjp(layer_norm, section_four, gain_values[5], bias_values[5])
    grad_four, grad_gain_last, grad_bias_last = final_pull(cotangent[0].astype(jnp.float32))
    back_second = ffn_backward(0.5 * grad_four, kept_second, expand_b, shrink_b)
    grad_three = grad_four + back_second[0]
    grad_delta = grad_three.astype(jnp.bfloat16)
    grad_conv_out = jnp.einsum(
        "utd,ute->de", conv_active, grad_delta, preferred_element_type=jnp.float32
    )
    grad_active = jnp.einsum(
        "ute,de->utd", grad_delta, conv_out_all, preferred_element_type=jnp.float32
    )
    grad_depthwise, grad_gain_inner, grad_bias_inner = inner_pull(grad_active)
    grad_depthwise = grad_depthwise.astype(jnp.bfloat16)
    grad_rimmed = with_halo(grad_depthwise, (("seq", 1),), margin)
    grad_gated = depth_values[0] * grad_rimmed[:, KERNEL - 1 : KERNEL - 1 + local_len]
    for shift_index in range(1, KERNEL):
        lead_at = KERNEL - 1 - shift_index
        grad_gated = (
            grad_gated + depth_values[shift_index] * grad_rimmed[:, lead_at : lead_at + local_len]
        )
    grad_depth = jnp.stack(
        [
            jnp.einsum(
                "utd,utd->d",
                grad_depthwise,
                rimmed[:, shift_index : shift_index + local_len],
                preferred_element_type=jnp.float32,
            )
            for shift_index in range(KERNEL)
        ]
    )
    grad_doubled = gate_pull(grad_gated)[0].astype(jnp.bfloat16)
    grad_conv_in = jnp.einsum(
        "utd,ute->de", conv_normed, grad_doubled, preferred_element_type=jnp.float32
    )
    grad_normed = jnp.einsum(
        "ute,de->utd", grad_doubled, conv_in_all, preferred_element_type=jnp.float32
    )
    grad_conv_stream, grad_gain_conv, grad_bias_conv = conv_pull(grad_normed)
    grad_two = grad_three + grad_conv_stream
    grad_attn = grad_two.astype(jnp.bfloat16)
    grad_attn_out = jnp.einsum(
        "ute,utd->ed", attn_time, grad_attn, preferred_element_type=jnp.float32
    )
    grad_time = jnp.einsum("utd,ed->ute", grad_attn, attn_all, preferred_element_type=jnp.float32)
    grad_time = grad_time.astype(jnp.bfloat16).reshape(UTT, local_len, HEADS, HEAD_DIM)
    grad_heads = lax.all_to_all(grad_time, "seq", split_axis=2, concat_axis=1, tiled=True)
    grad_keys = jnp.zeros((UTT, LEN, heads_here, HEAD_DIM), jnp.float32)
    grad_values = jnp.zeros((UTT, LEN, heads_here, HEAD_DIM), jnp.float32)
    grad_table = jnp.zeros((2 * LEN, heads_here, HEAD_DIM), jnp.float32)
    content_sum = jnp.zeros((heads_here, HEAD_DIM), jnp.float32)
    position_sum = jnp.zeros((heads_here, HEAD_DIM), jnp.float32)
    query_grads = []
    for block_index in range(block_count):
        starting = block_index * QUERY_BLOCK
        logits, content_block, position_block, window, lowest = block_logits(
            content_query, position_query, keys_heads, projected, keeping, starting
        )
        probability = jnp.exp(logits - normalizers[block_index])
        grad_block = lax.slice_in_dim(grad_heads, starting, starting + QUERY_BLOCK, axis=1)
        grad_prob = jnp.einsum(
            "uahe,ujhe->uhaj", grad_block, values_heads, preferred_element_type=jnp.float32
        )
        grad_logits = probability * (
            grad_prob - jnp.sum(probability * grad_prob, axis=-1, keepdims=True)
        )
        grad_scores = (grad_logits * (1.0 / math.sqrt(HEAD_DIM))).astype(jnp.bfloat16)
        grad_values = grad_values + jnp.einsum(
            "uhaj,uahe->ujhe",
            probability.astype(jnp.bfloat16),
            grad_block,
            preferred_element_type=jnp.float32,
        )
        grad_keys = grad_keys + jnp.einsum(
            "uhaj,uahe->ujhe", grad_scores, content_block, preferred_element_type=jnp.float32
        )
        grad_content = jnp.einsum(
            "uhaj,ujhe->uahe", grad_scores, keys_heads, preferred_element_type=jnp.float32
        )
        grad_placed = unskew(grad_scores, QUERY_BLOCK, LEN)
        grad_position = jnp.einsum(
            "uham,mhe->uahe", grad_placed, window, preferred_element_type=jnp.float32
        )
        grad_window = jnp.einsum(
            "uham,uahe->mhe", grad_placed, position_block, preferred_element_type=jnp.float32
        )
        grad_table = grad_table + jnp.pad(
            grad_window, ((lowest, 2 * LEN - lowest - span_width), (0, 0), (0, 0))
        )
        content_sum = content_sum + jnp.sum(grad_content, axis=(0, 1))
        position_sum = position_sum + jnp.sum(grad_position, axis=(0, 1))
        query_grads.append(grad_content + grad_position)
    grad_queries = jnp.concatenate(query_grads, axis=1).astype(jnp.bfloat16)
    grad_stack = jnp.stack(
        [grad_queries, grad_keys.astype(jnp.bfloat16), grad_values.astype(jnp.bfloat16)], axis=2
    )
    grad_packed = lax.all_to_all(
        grad_stack, "seq", split_axis=1, concat_axis=3, tiled=True
    ).reshape(UTT, local_len, 3 * D)
    grad_qkv = jnp.einsum(
        "utd,ute->de", attn_normed, grad_packed, preferred_element_type=jnp.float32
    )
    grad_normed = jnp.einsum(
        "ute,de->utd", grad_packed, qkv_all, preferred_element_type=jnp.float32
    )
    grad_attn_stream, grad_gain_attn, grad_bias_attn = attn_pull(grad_normed)
    grad_one = grad_two + grad_attn_stream
    grad_pos = jnp.einsum(
        "rd,re->de",
        sinusoid,
        grad_table.astype(jnp.bfloat16).reshape(2 * LEN, heads_here * HEAD_DIM),
        preferred_element_type=jnp.float32,
    )
    grad_pos_bias = jnp.stack([content_sum, position_sum]).reshape(2, heads_here * HEAD_DIM)
    back_first = ffn_backward(0.5 * grad_one, kept_first, expand_a, shrink_a)
    grad_input = grad_one + back_first[0]
    grad_gains_rows = jnp.stack(
        [
            back_first[1],
            grad_gain_attn,
            grad_gain_conv,
            grad_gain_inner,
            back_second[1],
            grad_gain_last,
        ]
    ).T
    grad_biases_rows = jnp.stack(
        [
            back_first[2],
            grad_bias_attn,
            grad_bias_conv,
            grad_bias_inner,
            back_second[2],
            grad_bias_last,
        ]
    ).T
    grad_depth_rows = grad_depth.T
    (
        part_gains,
        part_biases,
        part_depth,
        part_expand_one,
        part_shrink_one,
        part_qkv,
        part_attn_out,
        part_conv_in,
        part_conv_out,
        part_expand_two,
        part_shrink_two,
    ) = (
        lax.psum_scatter(
            grad_gains_rows.astype(jnp.bfloat16), "seq", scatter_dimension=0, tiled=True
        ).astype(jnp.float32),
        lax.psum_scatter(
            grad_biases_rows.astype(jnp.bfloat16), "seq", scatter_dimension=0, tiled=True
        ).astype(jnp.float32),
        lax.psum_scatter(
            grad_depth_rows.astype(jnp.bfloat16), "seq", scatter_dimension=0, tiled=True
        ).astype(jnp.float32),
        lax.psum_scatter(
            back_first[3].astype(jnp.bfloat16), "seq", scatter_dimension=0, tiled=True
        ).astype(jnp.float32),
        lax.psum_scatter(
            back_first[4].astype(jnp.bfloat16), "seq", scatter_dimension=0, tiled=True
        ).astype(jnp.float32),
        lax.psum_scatter(
            grad_qkv.astype(jnp.bfloat16), "seq", scatter_dimension=0, tiled=True
        ).astype(jnp.float32),
        lax.psum_scatter(
            grad_attn_out.astype(jnp.bfloat16), "seq", scatter_dimension=0, tiled=True
        ).astype(jnp.float32),
        lax.psum_scatter(
            grad_conv_in.astype(jnp.bfloat16), "seq", scatter_dimension=0, tiled=True
        ).astype(jnp.float32),
        lax.psum_scatter(
            grad_conv_out.astype(jnp.bfloat16), "seq", scatter_dimension=0, tiled=True
        ).astype(jnp.float32),
        lax.psum_scatter(
            back_second[3].astype(jnp.bfloat16), "seq", scatter_dimension=0, tiled=True
        ).astype(jnp.float32),
        lax.psum_scatter(
            back_second[4].astype(jnp.bfloat16), "seq", scatter_dimension=0, tiled=True
        ).astype(jnp.float32),
    )
    (
        sum_gains,
        sum_biases,
        sum_depth,
        sum_expand_one,
        sum_shrink_one,
        sum_qkv,
        sum_attn_out,
        sum_conv_in,
        sum_conv_out,
        sum_expand_two,
        sum_shrink_two,
        sum_pos,
        sum_pos_bias,
    ) = (
        lax.psum(part_gains.astype(jnp.bfloat16), "dp").astype(jnp.float32),
        lax.psum(part_biases.astype(jnp.bfloat16), "dp").astype(jnp.float32),
        lax.psum(part_depth.astype(jnp.bfloat16), "dp").astype(jnp.float32),
        lax.psum(part_expand_one.astype(jnp.bfloat16), "dp").astype(jnp.float32),
        lax.psum(part_shrink_one.astype(jnp.bfloat16), "dp").astype(jnp.float32),
        lax.psum(part_qkv.astype(jnp.bfloat16), "dp").astype(jnp.float32),
        lax.psum(part_attn_out.astype(jnp.bfloat16), "dp").astype(jnp.float32),
        lax.psum(part_conv_in.astype(jnp.bfloat16), "dp").astype(jnp.float32),
        lax.psum(part_conv_out.astype(jnp.bfloat16), "dp").astype(jnp.float32),
        lax.psum(part_expand_two.astype(jnp.bfloat16), "dp").astype(jnp.float32),
        lax.psum(part_shrink_two.astype(jnp.bfloat16), "dp").astype(jnp.float32),
        lax.psum(grad_pos.astype(jnp.bfloat16), "dp").astype(jnp.float32),
        lax.psum(grad_pos_bias.astype(jnp.bfloat16), "dp").astype(jnp.float32),
    )
    return (
        encoded.astype(jnp.bfloat16)[None],
        grad_input[None],
        sum_gains.T,
        sum_biases.T,
        sum_expand_one,
        sum_shrink_one,
        sum_qkv,
        sum_pos,
        sum_pos_bias,
        sum_attn_out,
        sum_conv_in,
        sum_depth.T,
        sum_conv_out,
        sum_expand_two,
        sum_shrink_two,
    )


def solution(mesh):
    placed = (
        P("dp", None, "seq", None),
        P("dp", None, "seq", None),
        P(),
        P(),
        P(None, "seq"),
        P(None, "seq"),
        P("seq", None),
        P("seq", None),
        P("seq", None),
        P(None, "seq"),
        P(None, "seq"),
        P("seq", None),
        P("seq", None),
        P(None, "seq"),
        P("seq", None),
        P("seq", None),
        P("seq", None),
    )
    return jax.shard_map(
        shards,
        mesh=mesh,
        in_specs=placed,
        out_specs=(
            P("dp", None, "seq", None),
            P("dp", None, "seq", None),
            P(None, "seq"),
            P(None, "seq"),
            P("seq", None),
            P("seq", None),
            P("seq", None),
            P(None, "seq"),
            P(None, "seq"),
            P("seq", None),
            P("seq", None),
            P(None, "seq"),
            P("seq", None),
            P("seq", None),
            P("seq", None),
        ),
        check_vma=False,
    )
```

profile of v0, /device:TPU:0, one launch (start us, length us, event | category | flops | bytes accessed | tf_op | source)
XLA Modules:
  0.0 2239.0 jit_solution(3996493236263545410)
XLA Ops:
  11.9 14.8 all_gather.33
  26.8 14.2 all_gather.34
  43.4 118.8 %all-gather.9.cloned.1.call-done = bf16[1024,4096]{1,0:T(8,128)(2,1)} async-done(((bf16[256,4096]{1,0:T(8,128)(2,1)}), bf16[1024,4096]{1,0:T(8,128)(2,1)}) %all-gather.9.cloned.1.call-update) | async-done | bytes 8388624 | tf_op jit(solution)/shard_map/all_gather | solution.py:169
  162.2 10.3 fusion.26
  172.5 139.2 %all-gather.11.cloned.1.call-done = bf16[4096,1024]{1,0:T(8,128)(2,1)} async-done(((bf16[1024,1024]{1,0:T(8,128)(2,1)}), bf16[4096,1024]{1,0:T(8,128)(2,1)}) %all-gather.11.cloned.1.call-update) | async-done | bytes 8388624 | tf_op jit(solution)/shard_map/all_gather | solution.py:170
  311.7 10.6 fusion.204
  322.7 104.2 %all-gather.13.cloned.1.call-done = bf16[1024,3072]{1,0:T(8,128)(2,1)} async-done(((bf16[256,3072]{1,0:T(8,128)(2,1)}), bf16[1024,3072]{1,0:T(8,128)(2,1)}) %all-gather.13.cloned.1.call-update) | async-done | bytes 6291472 | tf_op jit(solution)/shard_map/all_gather | solution.py:171
  426.9 6.6 fusion.46
  444.2 15.8 multiply_sine_fusion
  462.4 11.3 copy.172
  473.6 7.2 convert_element_type.326
  486.3 97.4 %all-to-all-done = bf16[2,256,3,8,128]{4,1,2,0,3:T(8,128)(2,1)} async-done(((bf16[2,256,3,8,128]{4,1,2,0,3:T(8,128)(2,1)}), bf16[2,256,3,8,128]{4,1,2,0,3:T(8,128)(2,1)}, u32[]{:S(2)}, u32[]{:S(2)}) %all-to-all-start) | async-done | bytes 3145760 | tf_op jit(solution)/shard_map/all_to_all | solution.py:192
  588.5 6.4 convolution_bitcast_fusion.1
  594.9 12.6 copy.175
  607.5 21.7 reshape.561
  629.2 16.2 slice.241
  645.4 26.5 %reshape.562 = f32[2,2,512,1535]{3,2,1,0:T(8,128)} reshape(f32[2,2,785920]{2,1,0:T(2,128)} %slice.241) | data formatting | bytes 25149440 | tf_op jit(solution)/shard_map/reshape | solution.py:66
  672.0 6.4 convolution_bitcast_fusion
  678.4 12.7 copy.179
  691.1 22.1 reshape.563
  713.1 16.2 slice.246
  729.4 26.2 %reshape.564 = f32[2,2,512,1535]{3,2,1,0:T(8,128)} reshape(f32[2,2,785920]{2,1,0:T(2,128)} %slice.246) | data formatting | bytes 25149440 | tf_op jit(solution)/shard_map/reshape | solution.py:66
  755.6 5.6 fusion.206
  787.7 42.1 %all_gather.39 = bf16[5,1024]{1,0:T(8,128)(2,1)S(1)} all-gather(bf16[5,256]{1,0:T(8,128)(2,1)S(1)} %copy-done.86), channel_id=1, replica_groups=mesh['dp'=8,'seq'=4] {'seq'}, dimensions={1}, use_global_device_ids=true | all-gather | bytes 12800 | tf_op jit(solution)/shard_map/all_gather | solution.py:168
  840.5 5.3 fusion.55
  865.8 11.9 fusion.18
  877.7 93.0 %all-gather.23.cloned.1.call-done = bf16[4096,1024]{1,0:T(8,128)(2,1)} async-done(((bf16[1024,1024]{1,0:T(8,128)(2,1)}), bf16[4096,1024]{1,0:T(8,128)(2,1)}) %all-gather.23.cloned.1.call-update) | async-done | bytes 8388624 | tf_op jit(solution)/shard_map/all_gather | solution.py:176
  970.7 11.1 fusion.209
  984.2 13.5 fusion.4
  997.6 9.1 fusion.188
  1015.0 5.0 fusion.189
  1021.7 8.0 fusion.89
  1051.5 7.4 bitcast_convert_fusion.5
  1059.3 12.9 bitcast_convert_fusion
  1072.2 10.8 bitcast_convert_fusion.1
  1092.4 38.4 %all-to-all-done.2 = bf16[2,256,8,128]{3,1,0,2:T(8,128)(2,1)} async-done(((bf16[2,256,8,128]{3,1,0,2:T(8,128)(2,1)}), bf16[2,256,8,128]{3,1,0,2:T(8,128)(2,1)}, u32[]{:S(2)}, u32[]{:S(2)}) %all-to-all-start.2) | async-done | bytes 1048608 | tf_op jit(solution)/shard_map/all_to_all | solution.py:299
  1133.4 12.5 multiply_convert_fusion
  1145.8 5.3 pad.32
  1151.1 14.2 reshape.569
  1165.3 10.7 pad.33
  1176.1 9.7 reshape.612
  1185.7 12.6 multiply_convert_fusion.1
  1198.3 5.3 pad.30
  1203.6 14.1 reshape.567
  1217.7 10.7 pad.31
  1228.4 9.8 reshape.611
  1260.7 8.7 copy.195
  1269.3 145.2 %all_to_all.66 = bf16[2,1024,3,2,128]{4,3,0,2,1:T(2,128)(2,1)S(1)} all-to-all(bf16[2,1024,3,2,128]{4,3,0,2,1:T(2,128)(2,1)} %copy.195), channel_id=1, replica_groups=mesh['dp'=8,'seq'=4] {'seq'}, dimensions={1} | all-to-all | bytes 6291456 | tf_op jit(solution)/shard_map/all_to_all | solution.py:349
  1418.4 8.0 reshape.571
  1426.4 8.9 bitcast_convert_fusion.4
  1435.9 8.2 fusion.190
  1447.9 10.9 bitcast_convert_fusion.2
  1459.1 10.4 fusion.7
  1471.6 7.3 bitcast_convert_fusion.3
  1492.2 6.0 fusion.191
  1506.6 55.5 %reduce-scatter.30.cloned.1.call-done = bf16[256,4096]{1,0:T(8,128)(2,1)} async-done(((bf16[1024,4096]{1,0:T(8,128)(2,1)}), bf16[256,4096]{1,0:T(8,128)(2,1)}) %reduce-scatter.30.cloned.1.call-update) | async-done | bytes 2097168 | tf_op jit(solution)/shard_map/reduce_scatter | solution.py:430
  1562.2 113.8 %reduce-scatter.20.cloned.1.call-done = bf16[256,3072]{1,0:T(8,128)(2,1)} async-done(((bf16[1024,3072]{1,0:T(8,128)(2,1)}), bf16[256,3072]{1,0:T(8,128)(2,1)}) %reduce-scatter.20.cloned.1.call-update) | async-done | bytes 1572880 | tf_op jit(solution)/shard_map/reduce_scatter | solution.py:418
  1675.9 147.4 %reduce-scatter.18.cloned.1.call-done = bf16[1024,1024]{1,0:T(8,128)(2,1)} async-done(((bf16[4096,1024]{1,0:T(8,128)(2,1)}), bf16[1024,1024]{1,0:T(8,128)(2,1)}) %reduce-scatter.18.cloned.1.call-update) | async-done | bytes 2097168 | tf_op jit(solution)/shard_map/reduce_scatter | solution.py:415
  1823.3 147.6 %reduce-scatter.16.cloned.1.call-done = bf16[256,4096]{1,0:T(8,128)(2,1)} async-done(((bf16[1024,4096]{1,0:T(8,128)(2,1)}), bf16[256,4096]{1,0:T(8,128)(2,1)}) %reduce-scatter.16.cloned.1.call-update) | async-done | bytes 2097168 | tf_op jit(solution)/shard_map/reduce_scatter | solution.py:412
  1975.2 18.1 reduce-scatter.26.cloned.1.call-done
  1993.2 19.7 reduce-scatter.14.cloned.1.call-done
  2013.0 20.0 reduce-scatter.12.cloned.1.call-done
  2032.9 23.7 %all-reduce.8 = (bf16[6,256]{1,0:T(8,128)(2,1)S(1)}, bf16[6,256]{1,0:T(8,128)(2,1)S(1)}, bf16[2,256]{1,0:T(2,128)(2,1)S(1)}, bf16[5,256]{1,0:T(8,128)(2,1)S(1)}) all-reduce(bf16[6,256]{1,0:T(8,128)(2,1)} %bitcast.453, bf16[6,256]{1,0:T(8,128)(2,1)} %bitcast.452, ...), channel_id=1, replica_groups=mesh['dp'=8,'seq'=4] {'dp'}, use_global_device_ids=true, to_apply=%region_37.38 | all-reduce | flops 4864 | bytes 19456 | tf_op jit(solution)/shard_map/psum | solution.py:452
  2059.0 153.4 %all-reduce.12.cloned.1.call-done = (bf16[256,4096]{1,0:T(8,128)(2,1)}, bf16[1024,1024]{1,0:T(8,128)(2,1)}, bf16[256,3072]{1,0:T(8,128)(2,1)}, bf16[1024,256]{1,...) async-done(((bf16[256,4096]{1,0:T(8,128)(2,1)}, ...) | async-done | bytes 12582928 | tf_op jit(solution)/shard_map/psum | solution.py:455
  (430 shorter events, 212.0 us)
Async XLA Ops:
  7.2 474.6 %copy-start = (bf16[1024,256]{1,0:T(8,128)(2,1)S(1)}, bf16[1024,256]{1,0:T(8,128)(2,1)}, u32[]{:S(2)}) copy-start(bf16[1024,256]{1,0:T(8,128)(2,1)} %param.26) | copy-start | bytes 1572868
  7.2 155.0 %all-gather.9.cloned.1.call-start = ((), (), s32[]{:S(2)}) async-start(), calls=%async_computation.15 | async-start | bytes 10485760 | tf_op jit(solution)/shard_map/all_gather | solution.py:169
  7.9 303.7 %all-gather.11.cloned.1.call-start = ((), (), s32[]{:S(2)}) async-start(), calls=%async_computation.16 | async-start | bytes 10485760 | tf_op jit(solution)/shard_map/all_gather | solution.py:170
  8.7 418.2 %all-gather.13.cloned.1.call-start = ((), (), s32[]{:S(2)}) async-start(), calls=%async_computation.17 | async-start | bytes 7864320 | tf_op jit(solution)/shard_map/all_gather | solution.py:171
  9.4 17.3 copy-start.85
  9.4 31.5 %copy-start.21 = (bf16[1,2,256,1024]{3,2,1,0:T(8,128)(2,1)S(1)}, bf16[1,2,256,1024]{3,2,1,0:T(8,128)(2,1)}, u32[]{:S(2)}) copy-start(bf16[1,2,256,1024]{3,2,1,0:T(8,128)(2,1)} %param.17) | copy-start | bytes 3145732
  9.4 826.1 %all-gather.15.cloned.1.call-start = ((), (), s32[]{:S(2)}) async-start(), calls=%async_computation.18 | async-start | bytes 2621440 | tf_op jit(solution)/shard_map/all_gather | solution.py:172
  10.0 830.5 %all-gather.17.cloned.1.call-start = ((), (), s32[]{:S(2)}) async-start(), calls=%async_computation.19 | async-start | bytes 5242880 | tf_op jit(solution)/shard_map/all_gather | solution.py:173
  10.6 849.6 %all-gather.19.cloned.1.call-start = ((), (), s32[]{:S(2)}) async-start(), calls=%async_computation.20 | async-start | bytes 2621440 | tf_op jit(solution)/shard_map/all_gather | solution.py:174
  11.2 854.6 %all-gather.21.cloned.1.call-start = ((), (), s32[]{:S(2)}) async-start(), calls=%async_computation.21 | async-start | bytes 10485760 | tf_op jit(solution)/shard_map/all_gather | solution.py:175
  41.2 131.3 %copy-start.64 = (f32[2,256]{1,0:T(2,128)}, f32[2,256]{1,0:T(2,128)S(1)}, u32[]{:S(2)}) copy-start(f32[2,256]{1,0:T(2,128)S(1)} %broadcast_multiply_fusion.5) | copy-start | bytes 6148
  42.2 130.3 %copy-start.72 = (f32[2,256]{1,0:T(2,128)}, f32[2,256]{1,0:T(2,128)S(1)}, u32[]{:S(2)}) copy-start(f32[2,256]{1,0:T(2,128)S(1)} %fusion.170) | copy-start | bytes 6148
  42.8 129.7 %copy-start.52 = (f32[1,1024]{1,0:T(1,128)}, f32[1,1024]{1,0:T(1,128)S(1)}, u32[]{:S(2)}) copy-start(f32[1,1024]{1,0:T(1,128)S(1)} %get-tuple-element.86) | copy-start | bytes 12292
  42.8 384.1 %copy-start.54 = (f32[1,1024]{1,0:T(1,128)}, f32[1,1024]{1,0:T(1,128)S(1)}, u32[]{:S(2)}) copy-start(f32[1,1024]{1,0:T(1,128)S(1)} %get-tuple-element.85) | copy-start | bytes 12292
  43.4 129.1 %copy-start.87 = (f32[1,1024]{1,0:T(1,128)}, f32[1,1024]{1,0:T(1,128)S(1)}, u32[]{:S(2)}) copy-start(f32[1,1024]{1,0:T(1,128)S(1)} %get-tuple-element.92) | copy-start | bytes 12292
  43.4 383.4 %copy-start.89 = (f32[1,1024]{1,0:T(1,128)}, f32[1,1024]{1,0:T(1,128)S(1)}, u32[]{:S(2)}) copy-start(f32[1,1024]{1,0:T(1,128)S(1)} %get-tuple-element.91) | copy-start | bytes 12292
  322.3 513.2 %copy-start.11 = (f32[2,256,1024]{2,1,0:T(8,128)}, f32[2,256,1024]{2,1,0:T(8,128)S(1)}, u32[]{:S(2)}) copy-start(f32[2,256,1024]{2,1,0:T(8,128)S(1)} %get-tuple-element.105) | copy-start | bytes 6291460
  322.3 111.2 %copy-start.58 = (f32[2,256]{1,0:T(2,128)}, f32[2,256]{1,0:T(2,128)S(1)}, u32[]{:S(2)}) copy-start(f32[2,256]{1,0:T(2,128)S(1)} %broadcast_multiply_fusion.4) | copy-start | bytes 6148
  322.7 110.8 %copy-start.70 = (f32[2,256]{1,0:T(2,128)}, f32[2,256]{1,0:T(2,128)S(1)}, u32[]{:S(2)}) copy-start(f32[2,256]{1,0:T(2,128)S(1)} %multiply_reduce_fusion.14) | copy-start | bytes 6148
  322.7 110.8 %copy-start.66 = (f32[2,256]{1,0:T(2,128)}, f32[2,256]{1,0:T(2,128)S(1)}, u32[]{:S(2)}) copy-start(f32[2,256]{1,0:T(2,128)S(1)} %fusion.171) | copy-start | bytes 6148
  436.8 146.9 %all-to-all-start = ((bf16[2,256,3,8,128]{4,1,2,0,3:T(8,128)(2,1)}), bf16[2,256,3,8,128]{4,1,2,0,3:T(8,128)(2,1)}, u32[]{:S(2)}, u32[]{:S(2)}) async-start(bf16[2,256,3,8,128]{4,1,2,0,3:T(8,128)(2,1)} %copy.170), calls=%async_computation | async-start | bytes 6291456 | tf_op jit(solution)/shard_map/all_to_all | solution.py:192
  441.5 529.2 %all-gather.23.cloned.1.call-start = ((), (), s32[]{:S(2)}) async-start(), calls=%async_computation.22 | async-start | bytes 10485760 | tf_op jit(solution)/shard_map/all_gather | solution.py:176
  473.6 8.1 copy-start.94
  486.3 102.2 %copy-start.31 = (bf16[1536,256]{0,1:T(8,128)(2,1)}, bf16[1536,256]{0,1:T(8,128)(2,1)S(1)}, u32[]{:S(2)}) copy-start(bf16[1536,256]{0,1:T(8,128)(2,1)S(1)} %get-tuple-element.79) | copy-start | bytes 2359300
  645.4 26.5 %copy-start.33 = (bf16[1536,256]{0,1:T(8,128)(2,1)S(1)}, bf16[1536,256]{0,1:T(8,128)(2,1)}, u32[]{:S(2)}) copy-start(bf16[1536,256]{0,1:T(8,128)(2,1)} %get-tuple-element.80) | copy-start | bytes 2359300
  755.6 9.8 copy-start.6
  761.2 10.1 copy-start.2
  761.2 10.1 copy-start.47
  783.4 46.5 %all-to-all-start.1 = ((bf16[2,1024,2,128]{3,2,0,1:T(2,128)(2,1)}), bf16[2,1024,2,128]{3,2,0,1:T(2,128)(2,1)}, u32[]{:S(2)}, u32[]{:S(2)}) async-start(bf16[2,1024,2,128]{3,2,0,1:T(2,128)(2,1)} %copy.181), calls=%async_computation.1 | async-start | bytes 2097152 | tf_op jit(solution)/shard_map/all_to_all | solution.py:221
  787.7 718.9 %reduce-scatter.28.cloned.1.call-start = ((), (), s32[]{:S(2)}) async-start(), calls=%async_computation.31 | async-start | bytes 2621440 | tf_op jit(solution)/shard_map/reduce_scatter | solution.py:427
  847.9 12.3 copy-start.24
  847.9 5.0 collective-permute-start
  851.6 6.2 collective-permute-start.1
  877.7 104.1 %copy-start.51 = (f32[1,1024]{1,0:T(1,128)S(1)}, f32[1,1024]{1,0:T(1,128)}, u32[]{:S(2)}) copy-start(f32[1,1024]{1,0:T(1,128)} %get-tuple-element.81) | copy-start | bytes 12292
  970.7 11.1 copy-start.23
  981.7 26.5 %copy-start.18 = (f32[2,256,1024]{2,1,0:T(8,128)}, f32[2,256,1024]{2,1,0:T(8,128)S(1)}, u32[]{:S(2)}) copy-start(f32[2,256,1024]{2,1,0:T(8,128)S(1)} %get-tuple-element.115) | copy-start | bytes 6291460
  984.2 13.5 copy-start.17
  1021.6 485.0 %reduce-scatter.22.cloned.1.call-start = ((), (), s32[]{:S(2)}) async-start(), calls=%async_computation.28 | async-start | bytes 2621440 | tf_op jit(solution)/shard_map/reduce_scatter | solution.py:421
  1021.7 15.3 copy-start.8
  1029.7 5.9 collective-permute-start.2
  1031.0 5.9 collective-permute-start.3
  1051.5 455.1 %reduce-scatter.24.cloned.1.call-start = ((), (), s32[]{:S(2)}) async-start(), calls=%async_computation.29 | async-start | bytes 5242880 | tf_op jit(solution)/shard_map/reduce_scatter | solution.py:424
  1059.0 447.6 %reduce-scatter.32.cloned.1.call-start = ((), (), s32[]{:S(2)}) async-start(), calls=%async_computation.33 | async-start | bytes 10485760 | tf_op jit(solution)/shard_map/reduce_scatter | solution.py:433
  1072.2 490.0 %reduce-scatter.30.cloned.1.call-start = ((), (), s32[]{:S(2)}) async-start(), calls=%async_computation.32 | async-start | bytes 10485760 | tf_op jit(solution)/shard_map/reduce_scatter | solution.py:430
  1087.6 43.2 %all-to-all-start.2 = ((bf16[2,256,8,128]{3,1,0,2:T(8,128)(2,1)}), bf16[2,256,8,128]{3,1,0,2:T(8,128)(2,1)}, u32[]{:S(2)}, u32[]{:S(2)}) async-start(bf16[2,256,8,128]{3,1,0,2:T(8,128)(2,1)} %bitcast.386), calls=%async_computation.2 | async-start | bytes 2097152 | tf_op jit(solution)/shard_map/all_to_all | solution.py:299
  1091.9 584.0 %reduce-scatter.20.cloned.1.call-start = ((), (), s32[]{:S(2)}) async-start(), calls=%async_computation.27 | async-start | bytes 7864320 | tf_op jit(solution)/shard_map/reduce_scatter | solution.py:418
  1418.4 8.0 copy-start.55
  1418.4 8.0 copy-start.59
  1418.4 8.0 copy-start.67
  1418.4 8.0 copy-start.90
  1435.3 8.7 copy-start.71
  1435.3 387.9 %reduce-scatter.18.cloned.1.call-start = ((), (), s32[]{:S(2)}) async-start(), calls=%async_computation.26 | async-start | bytes 10485760 | tf_op jit(solution)/shard_map/reduce_scatter | solution.py:415
  1435.9 8.2 copy-start.12
  1458.8 12.7 copy-start.22
  1458.8 12.7 copy-start.53
  1458.9 12.7 copy-start.65
  1458.9 12.7 copy-start.73
  1458.9 12.7 copy-start.88
  1458.9 511.9 %reduce-scatter.16.cloned.1.call-start = ((), (), s32[]{:S(2)}) async-start(), calls=%async_computation.25 | async-start | bytes 10485760 | tf_op jit(solution)/shard_map/reduce_scatter | solution.py:412
  1479.0 514.3 %reduce-scatter.26.cloned.1.call-start = ((), (), s32[]{:S(2)}) async-start(), calls=%async_computation.30 | async-start | bytes 20480 | tf_op jit(solution)/shard_map/reduce_scatter | solution.py:409
  1481.4 531.5 %reduce-scatter.14.cloned.1.call-start = ((), (), s32[]{:S(2)}) async-start(), calls=%async_computation.24 | async-start | bytes 20480 | tf_op jit(solution)/shard_map/reduce_scatter | solution.py:406
  1481.7 8.5 slice-start.8
  1498.9 534.0 %reduce-scatter.12.cloned.1.call-start = ((), (), s32[]{:S(2)}) async-start(), calls=%async_computation.23 | async-start | bytes 20480 | tf_op jit(solution)/shard_map/reduce_scatter | solution.py:403
  1502.3 710.1 %all-reduce.12.cloned.1.call-start = ((), (), s32[]{:S(2)}) async-start(), calls=%async_computation.34 | async-start | bytes 25165824 | tf_op jit(solution)/shard_map/psum | solution.py:455
  (77 other events, 243.2 us)
Sparse Core Ops, SparseCore 0:
  9.6 152.5 all-gather.8
  163.8 147.8 all-gather.10
  313.3 113.5 all-gather.12
  428.3 74.3 all-gather.14
  504.1 103.0 all-gather.16
  608.6 44.8 all-gather.18
  655.1 165.8 all-gather.20
  822.6 148.0 all-gather.22
  1021.7 42.2 reduce-scatter.27
  1066.3 54.8 reduce-scatter.21
  1124.0 77.5 reduce-scatter.23
  1204.0 195.6 reduce-scatter.31
  1402.2 159.9 reduce-scatter.29
  1564.4 111.4 reduce-scatter.19
  1678.2 144.9 reduce-scatter.17
  1825.6 145.1 reduce-scatter.15
  1973.6 19.6 reduce-scatter.25
  1995.9 17.0 reduce-scatter.13
  2015.8 17.0 reduce-scatter.11
  2038.6 173.7 all-reduce.11
where the time goes:
time: 2250 us; the launch traced here: 2240 us
  waiting for transfers between devices  1280 us (57%)
  local copies, waits for them, and re-layouts  322 us (14%)
  matrix products  271 us (12%)
  blocking collectives  240 us (11%)
  other arithmetic  84.1 us (4%)
  starting transfers between devices  26.8 us (1%)
    psum x1, waiting for transfers between devices, shards(): lax.psum(part_expand_one.astype(jnp.bfloat16), 'dp').astype(jnp.float32)  153 us
    reduce_scatter x1, waiting for transfers between devices, shards(): lax.psum_scatter(back_first[3].astype(jnp.bfloat16), 'seq', scatter_dimen...  148 us
    reduce_scatter x1, waiting for transfers between devices, shards(): lax.psum_scatter(back_first[4].astype(jnp.bfloat16), 'seq', scatter_dimen...  147 us
    all_to_all x1, blocking collectives, shards(): lax.all_to_all(grad_stack, 'seq', split_axis=1, concat_axis=3, tiled=True)  145 us
    all_gather x1, waiting for transfers between devices, shards(): lax.all_gather(shrink_one, 'seq', axis=0, tiled=True)  139 us
    all_gather x1, waiting for transfers between devices, shards(): lax.all_gather(expand_one, 'seq', axis=0, tiled=True)  119 us
    reduce_scatter x1, waiting for transfers between devices, shards(): lax.psum_scatter(grad_qkv.astype(jnp.bfloat16), 'seq', scatter_dimension=...  114 us
    all_gather x1, waiting for transfers between devices, shards(): lax.all_gather(qkv_weight, 'seq', axis=0, tiled=True)  104 us
  transfers between devices with their start and end apart: 27, of which 16 were waited for; matrix products, arithmetic and copies ran while one was open for 26% of the time, Pallas kernels for 0%

commit v1 on v0

v1 whole, which is shorter than its diff:
```python
import functools
import math

import jax
import jax.numpy as jnp
from jax import lax
from jax.experimental import pallas as pl
from jax.experimental.pallas import tpu as pltpu
from jax.sharding import PartitionSpec as P

D = 1024
KERNEL = 5
EPSILON = 1e-05
MESH=pl.DeviceIdType.MESH

def place():
    dp=lax.axis_index("dp"); z=lax.axis_index("seq")
    c=dp%2; p=(dp//2)%4
    bx=p%2; by=p//2
    return dict(dp=dp,z=z,c=c,p=p,px=p+1-2*bx,py=p+2-4*by,
                core=dp+1-2*c, xn=dp+2-4*bx, yn=dp+4-8*by)

def gather_kernel(nw, nz, *refs):
    ins=refs[:nw]; small,fr,ct=refs[nw:nw+3]
    outs=refs[nw+3:2*nw+3]; small_o,fr_o,ct_o=refs[2*nw+3:2*nw+6]
    (zr,xr,yr,ar,br,cr,zsr,zsl,xs,ys,as_,bs,cs,loc,fs,frv)=refs[2*nw+6:]
    k=place(); dp,z,c,p=k["dp"],k["z"],k["c"],k["p"]
    here=lambda zz:(dp,zz)
    tcore=z//2; tdp=dp-c+tcore
    bar=pltpu.get_barrier_semaphore()
    def sig(dev): pl.semaphore_signal(bar,inc=1,device_id=dev,device_id_type=MESH)
    for n in ("core","xn","yn"): sig((k[n],z))
    for ok,zz in ((z>0,z-1),(z<nz-1,z+1)):
        @pl.when(ok)
        def _(): sig((dp,zz))
    for u in range(2):
        @pl.when(jnp.logical_or(tcore!=c, 2*c+u!=z))
        def _(): sig((tdp,2*c+u))
    one=lambda b: jnp.where(b,1,0)
    pl.semaphore_wait(bar,3+one(z>0)+one(z<nz-1)+2-one(tcore==c))
    def rc(src,dst,s,r,dev):
        return pltpu.make_async_remote_copy(src_ref=src,dst_ref=dst,send_sem=s,recv_sem=r,device_id=dev,device_id_type=MESH)
    allin=list(ins)+[small]; allout=list(outs)+[small_o]
    def piece(w,t,pp=None,half=None):
        if w==nw: return small_o.at[t]
        r=outs[w].at[t,p if pp is None else pp,c]
        if half is None: return r
        h=outs[w].shape[3]//2
        return r.at[pl.ds(half*h,h)]
    def own(w):
        return small if w==nw else ins[w].at[p,c]
    def zright(w,t,src=None): return rc(piece(w,t) if src is None else src,piece(w,t),zsr.at[w,t],zr.at[w,t],(dp,z+1))
    def zleft(w,t,src=None): return rc(piece(w,t) if src is None else src,piece(w,t),zsl.at[w,t],zr.at[w,t],(dp,z-1))
    def xsend(w,t): return rc(piece(w,t),piece(w,t),xs.at[w,t],xr.at[w,t],(k["xn"],z))
    def ysend(w,t): return rc(piece(w,t),piece(w,t),ys.at[w,t],yr.at[w,t],(k["yn"],z))
    def asend(w,t): return rc(piece(w,t,k["px"],0),piece(w,t,k["px"],0),as_.at[w,t],ar.at[w,t],(k["yn"],z))
    def bsend(w,t): return rc(piece(w,t,k["py"],1),piece(w,t,k["py"],1),bs.at[w,t],br.at[w,t],(k["xn"],z))
    def csend(w,t): return rc(outs[w].at[t,:,c],outs[w].at[t,:,c],cs.at[w,t],cr.at[w,t],(k["core"],z))
    def local(w): return pltpu.make_async_copy(allin[w],allout[w].at[z],loc.at[w])
    redo=[(fr,fr_o,0),(ct,ct_o,1)]
    def move(a,u):
        s,d,i=redo[a]
        return rc(s.at[u],d.at[z%2],fs.at[i,u],frv.at[i,z%2],(tdp,2*c+u))
    def keep(a):
        s,d,i=redo[a]
        return pltpu.make_async_copy(s.at[z%2],d.at[z%2],loc.at[nw+1+i])
    def moves(a,f_remote,f_local):
        for u in range(2):
            @pl.when(jnp.logical_or(tcore!=c,2*c+u!=z))
            def _(): f_remote(a,u)
        @pl.when(tcore==c)
        def _(): f_local(a)
    def away(f):
        for d in range(1,nz):
            @pl.when(z-d>=0)
            def _(): f(z-d,True)
            @pl.when(z+d<nz)
            def _(): f(z+d,False)
    moves(0,lambda a,u:move(a,u).start(),lambda a:keep(a).start())
    def go(w):
        @pl.when(z<nz-1)
        def _(): zright(w,z,own(w)).start()
        @pl.when(z>0)
        def _(): zleft(w,z,own(w)).start()
    def f1(w,t,fromleft):
        zright(w,t).wait_recv()
        if fromleft:
            @pl.when(z<nz-1)
            def _(): zright(w,t).start()
        else:
            @pl.when(z>0)
            def _(): zleft(w,t).start()
        if w<nw:
            xsend(w,t).start(); ysend(w,t).start()
    def f2(w,t,_):
        xsend(w,t).wait_recv(); asend(w,t).start()
        ysend(w,t).wait_recv(); bsend(w,t).start()
    def f3(w,t,_):
        asend(w,t).wait_recv(); bsend(w,t).wait_recv(); csend(w,t).start()
    def at(f,w,d):
        @pl.when(z-d>=0)
        def _(): f(w,z-d,True)
        @pl.when(z+d<nz)
        def _(): f(w,z+d,False)
    if True:
        for w in ([nw]+list(range(nw)))[:2]: go(w)
        for w in range(nw+1): local(w).start()
        for d in range(1,nz): at(f1,nw,d)
        for s in range(nw+2):
            for ww in (s+1,):
                if ww<nw: go(ww)
            if s==4: moves(1,lambda a,u:move(a,u).start(),lambda a:keep(a).start())
            for f,ww in ((f1,s),(f2,s-1),(f3,s-2)):
                if 0<=ww<nw:
                    for d in range(1,nz): at(f,ww,d)
    def away(f):
        for d in range(1,nz):
            @pl.when(z-d>=0)
            def _(): f(z-d,True)
            @pl.when(z+d<nz)
            def _(): f(z+d,False)
    for w in range(nw+1):
        local(w).wait()
        @pl.when(z<nz-1)
        def _(): zright(w,z,own(w)).wait_send()
        @pl.when(z>0)
        def _(): zleft(w,z,own(w)).wait_send()
        def f(t,fromleft):
            if fromleft:
                @pl.when(z<nz-1)
                def _(): zright(w,t).wait_send()
            else:
                @pl.when(z>0)
                def _(): zleft(w,t).wait_send()
            if w<nw:
                for g in (xsend,ysend,asend,bsend): g(w,t).wait_send()
                csend(w,t).wait()
        away(f)
    for a in range(2):
        moves(a,lambda a,u:move(a,u).wait_send(),lambda a:keep(a).wait())
        for pos in range(2):
            @pl.when(jnp.logical_or(tcore!=c,2*c+pos!=z))
            def _():
                s,d,i=redo[a]
                rc(s.at[pos],d.at[pos],fs.at[i,pos],frv.at[i,pos],(tdp,2*c+pos)).wait_recv()

def gather(ws,small,fr,ct,nz,cid=0):
    nw=len(ws)
    ins=[w.reshape(4,2,w.shape[0]//8,w.shape[1]) for w in ws]
    any_=pl.BlockSpec(memory_space=pl.ANY)
    shp=[jax.ShapeDtypeStruct((nz,)+w.shape,w.dtype) for w in ins]+[jax.ShapeDtypeStruct((nz,)+small.shape,small.dtype),jax.ShapeDtypeStruct(fr.shape,fr.dtype),jax.ShapeDtypeStruct(ct.shape,ct.dtype)]
    S=pltpu.SemaphoreType.DMA
    o=pl.pallas_call(functools.partial(gather_kernel,nw,nz),out_shape=shp,in_specs=[any_]*(nw+3),out_specs=[any_]*(nw+3),
        scratch_shapes=[S((nw+1,nz))]+[S((nw,nz))]*5+[S((nw+1,nz))]*2+[S((nw,nz))]*5+[S((nw+3,)),S((2,2)),S((2,2))],
        compiler_params=pltpu.CompilerParams(collective_id=cid,has_side_effects=True,vmem_limit_bytes=2**20),
        cost_estimate=pl.CostEstimate(flops=0,bytes_accessed=2*48*2**20,transcendentals=0),
    )(*ins,small,fr,ct)
    full=[x.reshape(nz*w.shape[0],w.shape[1]) for x,w in zip(o[:nw],ws)]
    return full,o[nw],o[nw+1],o[nw+2]

HD=128; SCALE=1.0/math.sqrt(128)
BLK=256
NT=(((1,),(1,)),((),()))
TN=(((0,),(0,)),((),()))
def dot(a,b,dims=(((1,),(0,)),((),()))):
    return lax.dot_general(a,b,dims,preferred_element_type=jnp.float32)

def order(first, own, oth):
    return jnp.concatenate([jnp.where(first, own, oth), jnp.where(first, oth, own)], axis=0)

def attn_fwd_kernel(sc_ref, q_ref, k_ref, v_ref, ko_ref, vo_ref, pt_ref, pb_ref, o_ref, p_ref):
    T=q_ref.shape[0]; L2=2*T
    first=sc_ref[0]==0; length=sc_ref[1]
    q=q_ref[...].astype(jnp.float32)
    pb=pb_ref[...].astype(jnp.float32)
    qu=(q+pb[0:1]).astype(jnp.bfloat16); qv=(q+pb[1:2]).astype(jnp.bfloat16)
    k=order(first,k_ref[...],ko_ref[...]); v=order(first,v_ref[...],vo_ref[...])
    W=BLK+L2
    keep=lax.broadcasted_iota(jnp.int32,(BLK,L2),1)<length
    for b in range(T//BLK):
        i0=b*BLK; w0=T-i0-BLK
        s=dot(qu[i0:i0+BLK],k,NT)
        pl_=dot(qv[i0:i0+BLK],pt_ref[w0:w0+W,:],NT)
        s=s+pltpu.roll(pl_,W-(BLK-1),1,stride=1,stride_axis=0)[:,:L2]
        s=jnp.where(keep,s*SCALE,-1e9)
        m=jnp.max(s,axis=-1,keepdims=True)
        e=jnp.exp(s-m)
        p=(e*(1.0/jnp.sum(e,axis=-1,keepdims=True))).astype(jnp.bfloat16)
        p_ref[0,i0:i0+BLK,:]=p
        o_ref[i0:i0+BLK,:]=dot(p,v).astype(jnp.bfloat16)

def attn_bwd_kernel(sc_ref, q_ref, k_ref, v_ref, ko_ref, vo_ref, pt_ref, pb_ref, g_ref, p_ref,
                    gq_ref, gk_ref, gv_ref, gko_ref, gvo_ref, gpt_ref, gb_ref, gpt_acc):
    T=q_ref.shape[0]; L2=2*T
    first=sc_ref[0]==0
    q=q_ref[...].astype(jnp.float32)
    pb=pb_ref[...].astype(jnp.float32)
    qu=(q+pb[0:1]).astype(jnp.bfloat16); qv=(q+pb[1:2]).astype(jnp.bfloat16)
    k=order(first,k_ref[...],ko_ref[...]); v=order(first,v_ref[...],vo_ref[...])
    W=BLK+L2
    flip=(lax.broadcasted_iota(jnp.int32,(BLK,BLK),0)+lax.broadcasted_iota(jnp.int32,(BLK,BLK),1)==BLK-1).astype(jnp.float32).astype(jnp.bfloat16)
    gpt_acc[...]=jnp.zeros_like(gpt_acc)
    gk=gv=None; su=sv=None
    for b in range(T//BLK):
        i0=b*BLK; w0=T-i0-BLK
        g=g_ref[i0:i0+BLK,:]
        pbf=p_ref[0,i0:i0+BLK,:]
        p=pbf.astype(jnp.float32)
        t=p*dot(g,v,NT)
        gl=t-p*jnp.sum(t,axis=-1,keepdims=True)
        gr=gl*SCALE
        grb=gr.astype(jnp.bfloat16)
        gvb=dot(pbf,g,TN); gkb=dot(grb,qu[i0:i0+BLK],TN)
        gv=gvb if gv is None else gv+gvb
        gk=gkb if gk is None else gk+gkb
        gqu=dot(grb,k)
        pad=jnp.concatenate([dot(flip,grb),jnp.zeros((BLK,BLK),jnp.float32)],axis=1)
        gp=pltpu.roll(pad,0,1,stride=1,stride_axis=0).astype(jnp.bfloat16)
        gpt_acc[w0:w0+W,:]+=dot(gp,dot(flip,qv[i0:i0+BLK]).astype(jnp.bfloat16),TN)
        gqv=lax.dot_general(flip.astype(jnp.float32),dot(gp,pt_ref[w0:w0+W,:]),(((1,),(0,)),((),())),precision=lax.Precision.HIGHEST,preferred_element_type=jnp.float32)
        gq_ref[i0:i0+BLK,:]=(gqu+gqv).astype(jnp.bfloat16)
        a=jnp.sum(gqu,axis=0,keepdims=True); c=jnp.sum(gqv,axis=0,keepdims=True)
        su=a if su is None else su+a; sv=c if sv is None else sv+c
    gpt_ref[...]=gpt_acc[...].astype(jnp.bfloat16)
    gk_ref[...]=jnp.where(first,gk[:T],gk[T:]); gv_ref[...]=jnp.where(first,gv[:T],gv[T:])
    gko_ref[...]=jnp.where(first,gk[T:],gk[:T]).astype(jnp.bfloat16); gvo_ref[...]=jnp.where(first,gv[T:],gv[:T]).astype(jnp.bfloat16)
    gb_ref[...]=jnp.concatenate([su,sv,jnp.zeros((6,su.shape[1]),jnp.float32)],axis=0)

def col(rows,off=0): return pl.BlockSpec((rows,HD),lambda h,off=off:(0,h+off))
def attn_fwd(sc,qkv,kvo,pt,pb):
    T=qkv.shape[0]; D=qkv.shape[1]//3; H=D//HD
    return pl.pallas_call(attn_fwd_kernel,grid=(H,),
        in_specs=[pl.BlockSpec(memory_space=pltpu.SMEM),col(T),col(T,H),col(T,2*H),col(T),col(T,H),col(3*T),col(pb.shape[0])],
        out_specs=[col(T),pl.BlockSpec((1,T,2*T),lambda h:(h,0,0))],
        out_shape=[jax.ShapeDtypeStruct((T,D),jnp.bfloat16),jax.ShapeDtypeStruct((H,T,2*T),jnp.bfloat16)],
        compiler_params=pltpu.CompilerParams(vmem_limit_bytes=48*2**20),
        cost_estimate=pl.CostEstimate(flops=H*T*2*T*HD*2*3,bytes_accessed=20*2**20,transcendentals=H*T*2*T),
    )(sc,qkv,qkv,qkv,kvo,kvo,pt,pb)
def attn_bwd(sc,qkv,kvo,pt,pb,g,p):
    T=qkv.shape[0]; D=qkv.shape[1]//3; H=D//HD
    f32=jnp.float32; bf=jnp.bfloat16
    return pl.pallas_call(attn_bwd_kernel,grid=(H,),
        in_specs=[pl.BlockSpec(memory_space=pltpu.SMEM),col(T),col(T,H),col(T,2*H),col(T),col(T,H),col(3*T),col(pb.shape[0]),col(T),pl.BlockSpec((1,T,2*T),lambda h:(h,0,0))],
        out_specs=[col(T)]*5+[col(3*T),col(8)],
        out_shape=[jax.ShapeDtypeStruct((T,D),bf),jax.ShapeDtypeStruct((T,D),f32),jax.ShapeDtypeStruct((T,D),f32),jax.ShapeDtypeStruct((T,D),bf),jax.ShapeDtypeStruct((T,D),bf),jax.ShapeDtypeStruct((3*T,D),bf),jax.ShapeDtypeStruct((8,D),f32)],
        scratch_shapes=[pltpu.VMEM((3*T,HD),f32)],
        compiler_params=pltpu.CompilerParams(vmem_limit_bytes=48*2**20),
        cost_estimate=pl.CostEstimate(flops=H*T*2*T*HD*2*6,bytes_accessed=30*2**20,transcendentals=0),
    )(sc,qkv,qkv,qkv,kvo,kvo,pt,pb,g,p)

def reduce_all(grads, g_small):
    outs = []
    for g in grads:
        part = lax.psum_scatter(g, ("seq", "dp"), scatter_dimension=0, tiled=True)
        outs.append(lax.all_gather(part, "dp", axis=0, tiled=True).astype(jnp.float32))
    width = g_small.shape[1] // lax.axis_size("seq")
    total = lax.psum(g_small.astype(jnp.bfloat16), ("dp", "seq")).astype(jnp.float32)
    return (*outs, lax.dynamic_slice_in_dim(total, lax.axis_index("seq") * width, width, axis=1))

def layer_norm(stream, gain, offset):
    average = jnp.mean(stream, axis=-1, keepdims=True)
    centred = stream - average
    spread = jnp.mean(centred * centred, axis=-1, keepdims=True)
    return centred * lax.rsqrt(spread + EPSILON) * gain + offset


def layer_norm_back(stream, gain, grad):
    average = jnp.mean(stream, axis=-1, keepdims=True)
    centred = stream - average
    spread = jnp.mean(centred * centred, axis=-1, keepdims=True)
    inverse = lax.rsqrt(spread + EPSILON)
    unit = centred * inverse
    scaled = grad * gain
    grad_stream = inverse * (
        scaled
        - jnp.mean(scaled, axis=-1, keepdims=True)
        - unit * jnp.mean(scaled * unit, axis=-1, keepdims=True)
    )
    return grad_stream, jnp.sum(grad * unit, axis=0), jnp.sum(grad, axis=0)


def swish(value):
    return value * jax.nn.sigmoid(value)


def swish_back(value, grad):
    gate = jax.nn.sigmoid(value)
    return grad * gate * (1.0 + value * (1.0 - gate))


def position_rows(first_row, rows, length, features):
    fine = 32
    column = lax.broadcasted_iota(jnp.int32, (1, features), 1)
    odd = column % 2 == 1
    frequency = jnp.exp((column // 2).astype(jnp.float32) * (-2.0 * math.log(10000.0) / features))
    coarse_at = (length - 1 - first_row - fine * jnp.arange(rows // fine, dtype=jnp.int32)).astype(jnp.float32)
    fine_at = jnp.arange(fine, dtype=jnp.int32).astype(jnp.float32)
    coarse = coarse_at[:, None] * frequency
    small = fine_at[:, None] * frequency
    coarse_sin, coarse_cos = jnp.sin(coarse), jnp.cos(coarse)
    lead = jnp.where(odd, coarse_cos, coarse_sin)[:, None, :]
    quarter = jnp.where(odd, -coarse_sin, coarse_cos)[:, None, :]
    table = lead * jnp.cos(small)[None] - quarter * jnp.sin(small)[None]
    return table.reshape(rows, features).astype(jnp.bfloat16)


def mm(left, right):
    return jnp.dot(left, right, preferred_element_type=jnp.float32)


def mm_nt(left, right):
    return lax.dot_general(left, right, NT, preferred_element_type=jnp.float32)


def mm_tn(left, right):
    return lax.dot_general(left, right, TN, preferred_element_type=jnp.float32).astype(jnp.bfloat16)


def pair_swap(value):
    count = lax.axis_size("dp")
    return lax.ppermute(value, "dp", [(i, i + 1 - 2 * (i % 2)) for i in range(count)])


def redistribute(value):
    dp_count, seq_count = lax.axis_size("dp"), lax.axis_size("seq")
    z = lax.axis_index("seq")
    routes = ([], [])
    for dp in range(dp_count):
        for zz in range(seq_count):
            a, b, c = zz // 2, zz % 2, dp % 2
            for which in range(2):
                routes[which].append(
                    (dp * seq_count + zz, (dp - c + a) * seq_count + 2 * c + (b + which) % 2)
                )
    low = z % 2 == 0
    straight = lax.ppermute(jnp.where(low, value[0], value[1]), ("dp", "seq"), routes[0])
    crossed = lax.ppermute(jnp.where(low, value[1], value[0]), ("dp", "seq"), routes[1])
    return jnp.stack([jnp.where(low, straight, crossed), jnp.where(low, crossed, straight)])


def with_halo(rows, core):
    margin = (KERNEL - 1) // 2
    got = pair_swap(jnp.where(core == 0, rows[-margin:], rows[:margin]))
    none = jnp.zeros_like(got)
    return jnp.concatenate([jnp.where(core == 1, got, none), rows, jnp.where(core == 0, got, none)], axis=0)


def shards(
    frames, cotangent, lengths, assignment, norm_gains, norm_biases, expand_one, shrink_one, qkv_weight,
    pos_weight, pos_biases, attn_out, conv_in, conv_depth, conv_out, expand_two, shrink_two,
):
    seq_count = lax.axis_size("seq")
    dp, z = lax.axis_index("dp"), lax.axis_index("seq")
    core = dp % 2
    own_length = lengths[assignment[dp - core + z // 2], z % 2]
    small = jnp.concatenate(
        [norm_gains, norm_biases, conv_depth, pos_biases, jnp.zeros((13, norm_gains.shape[1]), jnp.bfloat16)], axis=0
    )
    weights, small_all, x_in, cot = gather(
        [expand_one, shrink_one, qkv_weight, pos_weight, attn_out, conv_in, conv_out, expand_two, shrink_two],
        small, frames[0], cotangent[0], seq_count,
    )
    w1, w2, wqkv, wpos, wo, wci, wco, w3, w4 = weights
    wpos = wpos.reshape(seq_count, D, D // seq_count).transpose(1, 0, 2).reshape(D, D)
    vectors = small_all.transpose(1, 0, 2).reshape(32, D).astype(jnp.float32)
    gains, biases, depth, pos_pair = vectors[0:6], vectors[6:12], vectors[12:17], vectors[16:24]
    pos_pair = jnp.concatenate([vectors[17:19], jnp.zeros((6, D), jnp.float32)], axis=0)
    rows = 2 * frames.shape[2]
    x0 = x_in.reshape(rows, D).astype(jnp.float32)
    cot = cot.reshape(rows, D).astype(jnp.float32)
    valid = (core * rows + jnp.arange(rows, dtype=jnp.int32) < own_length).astype(jnp.float32)[:, None]

    h1 = layer_norm(x0, gains[0], biases[0]).astype(jnp.bfloat16)
    a1 = mm(h1, w1)
    s1 = swish(a1).astype(jnp.bfloat16)
    x1 = x0 + 0.5 * mm(s1, w2)
    ha = layer_norm(x1, gains[1], biases[1]).astype(jnp.bfloat16)
    qkv = mm(ha, wqkv).astype(jnp.bfloat16)
    kv_other = pair_swap(qkv[:, D:])
    sinusoid = position_rows((1 - core) * rows, 3 * rows, 2 * rows, D)
    ptab = mm(sinusoid, wpos).astype(jnp.bfloat16)
    scalars = jnp.stack([core, own_length]).astype(jnp.int32)
    attn, prob = attn_fwd(scalars, qkv, kv_other, ptab, pos_pair)
    x2 = x1 + mm(attn, wo)
    hc = layer_norm(x2, gains[2], biases[2]).astype(jnp.bfloat16)
    dbl = mm(hc, wci)
    gate = jax.nn.sigmoid(dbl[:, D:])
    m = (dbl[:, :D] * gate * valid).astype(jnp.bfloat16)
    rim = with_halo(m, core)
    cv = depth[0] * rim[0:rows]
    for tap in range(1, KERNEL):
        cv = cv + depth[tap] * rim[tap : tap + rows]
    sc = swish(layer_norm(cv, gains[3], biases[3])).astype(jnp.bfloat16)
    x3 = x2 + mm(sc, wco)
    h2 = layer_norm(x3, gains[4], biases[4]).astype(jnp.bfloat16)
    a2 = mm(h2, w3)
    s2 = swish(a2).astype(jnp.bfloat16)
    x4 = x3 + 0.5 * mm(s2, w4)
    encoded = layer_norm(x4, gains[5], biases[5]).astype(jnp.bfloat16)
    encoded = redistribute(encoded.reshape(2, rows // 2, D))

    gx4, gg5, gb5 = layer_norm_back(x4, gains[5], cot)
    go2 = (0.5 * gx4).astype(jnp.bfloat16)
    g_w4 = mm_tn(s2, go2)
    ga2 = swish_back(a2, mm_nt(go2, w4)).astype(jnp.bfloat16)
    g_w3 = mm_tn(h2, ga2)
    back, gg4, gb4 = layer_norm_back(x3, gains[4], mm_nt(ga2, w3))
    gx3 = gx4 + back
    gco = gx3.astype(jnp.bfloat16)
    g_wco = mm_tn(sc, gco)
    inner = layer_norm(cv, gains[3], biases[3])
    gcv, gg3, gb3 = layer_norm_back(cv, gains[3], swish_back(inner, mm_nt(gco, wco)))
    gcv = gcv.astype(jnp.bfloat16)
    grim = with_halo(gcv, core)
    gm = depth[0] * grim[KERNEL - 1 : KERNEL - 1 + rows]
    for tap in range(1, KERNEL):
        gm = gm + depth[tap] * grim[KERNEL - 1 - tap : KERNEL - 1 - tap + rows]
    g_depth = jnp.stack([
        jnp.sum(gcv.astype(jnp.float32) * rim[tap : tap + rows].astype(jnp.float32), axis=0) for tap in range(KERNEL)
    ])
    gm = gm * valid
    gdbl = jnp.concatenate(
        [(gm * gate).astype(jnp.bfloat16), (gm * dbl[:, :D] * gate * (1.0 - gate)).astype(jnp.bfloat16)], axis=1
    )
    g_wci = mm_tn(hc, gdbl)
    back, gg2, gb2 = layer_norm_back(x2, gains[2], mm_nt(gdbl, wci))
    gx2 = gx3 + back
    gao = gx2.astype(jnp.bfloat16)
    g_wo = mm_tn(attn, gao)
    gattn = mm_nt(gao, wo).astype(jnp.bfloat16)
    gq, gk, gv, gk_other, gv_other, gptab, g_pair = attn_bwd(scalars, qkv, kv_other, ptab, pos_pair, gattn, prob)
    got = pair_swap(jnp.concatenate([gk_other, gv_other], axis=1))
    gk = (gk + got[:, :D]).astype(jnp.bfloat16)
    gv = (gv + got[:, D:]).astype(jnp.bfloat16)
    gqkv = jnp.concatenate([gq, gk, gv], axis=1)
    g_wpos = mm_tn(sinusoid, gptab)
    g_wpos = g_wpos.reshape(D, seq_count, D // seq_count).transpose(1, 0, 2).reshape(seq_count * D, D // seq_count)
    g_wqkv = mm_tn(ha, gqkv)
    back, gg1, gb1 = layer_norm_back(x1, gains[1], mm_nt(gqkv, wqkv))
    gx1 = gx2 + back
    go1 = (0.5 * gx1).astype(jnp.bfloat16)
    g_w2 = mm_tn(s1, go1)
    ga1 = swish_back(a1, mm_nt(go1, w2)).astype(jnp.bfloat16)
    g_w1 = mm_tn(h1, ga1)
    back, gg0, gb0 = layer_norm_back(x0, gains[0], mm_nt(ga1, w1))
    gx0 = gx1 + back
    grad_input = redistribute(gx0.astype(jnp.bfloat16).reshape(2, rows // 2, D)).astype(jnp.float32)

    g_small = jnp.concatenate(
        [jnp.stack([gg0, gg1, gg2, gg3, gg4, gg5, gb0, gb1, gb2, gb3, gb4, gb5]), g_depth, g_pair[:2]], axis=0
    )
    outs = reduce_all([g_w1, g_w2, g_wqkv, g_wpos, g_wo, g_wci, g_wco, g_w3, g_w4], g_small)
    s_w1, s_w2, s_wqkv, s_wpos, s_wo, s_wci, s_wco, s_w3, s_w4, s_small = outs
    return (
        encoded[None], grad_input[None], s_small[0:6], s_small[6:12], s_w1, s_w2, s_wqkv, s_wpos, s_small[17:19],
        s_wo, s_wci, s_small[12:17], s_wco, s_w3, s_w4,
    )


def solution(mesh):
    rows, columns = P("seq", None), P(None, "seq")
    act = P("dp", None, "seq", None)
    return jax.shard_map(
        shards,
        mesh=mesh,
        in_specs=(act, act, P(), P(), columns, columns, rows, rows, rows, columns, columns, rows, rows, columns, rows, rows, rows),
        out_specs=(act, act, columns, columns, rows, rows, rows, columns, columns, rows, rows, columns, rows, rows, rows),
        check_vma=False,
    )
```

time: 2250 us -> 1830 us (0.81)
  local copies, waits for them, and re-layouts: 322 us -> 46.9 us
  Pallas kernels: 0 us -> 271 us
  blocking collectives: 240 us -> 76.1 us
  waiting for transfers between devices: 1280 us -> 1170 us
  matrix products: 271 us -> 174 us
  other arithmetic: 84.1 us -> 58.2 us
    reduce_scatter x11 -> x9, waiting for transfers between devices: 522 us -> 1010 us  [reduce_all(): part = lax.psum_scatter(g, ('seq', 'dp'), scatter_dimension=0, tiled=True)]
    all_gather x8 -> x6, waiting for transfers between devices: 455 us -> 137 us  [reduce_all(): lax.all_gather(part, 'dp', axis=0, tiled=True).astype(jnp.float32)]
    pallas_call x0 -> x3, Pallas kernels: none -> 271 us  [the longest x1 215 us: gather(): pl.pallas_call(functools.partial(gather_kernel, nw, nz), out_shape=shp, i...]
    reshape x12 -> x0, local copies, waits for them, and re-layouts: 159 us -> none  [the longest x2 52.7 us: skew(): flattened.reshape(leading + (block_rows, span_width - 1))[..., :length]]
    psum x1 -> x0, waiting for transfers between devices: 153 us -> none  [shards(): lax.psum(part_expand_one.astype(jnp.bfloat16), 'dp').astype(jnp.float32)]
    all_to_all x1 -> x0, blocking collectives: 145 us -> none  [shards(): lax.all_to_all(grad_stack, 'seq', split_axis=1, concat_axis=3, tiled=True)]
    all_to_all x3 -> x0, waiting for transfers between devices: 136 us -> none  [the longest x1 97.4 us: shards(): lax.all_to_all(packed, 'seq', split_axis=3, concat_axis=1, tiled=True)]
    dot_general x42 -> x26, matrix products: 246 us -> 174 us  [the longest x9 67.3 us: mm_tn(): lax.dot_general(left, right, TN, preferred_element_type=jnp.float32)]
  transfers between devices with their start and end apart: 27 -> 23, of which waited for: 16 -> 18; matrix products, arithmetic and copies ran while one was open for 26% -> 8% of each run, Pallas kernels for 0% -> 2%
where the time goes in v1:
time: 1830 us; the launch traced here: 1820 us
  waiting for transfers between devices  1170 us (64%)
  Pallas kernels  271 us (15%)
  matrix products  174 us (10%)
  blocking collectives  76.1 us (4%)
  other arithmetic  58.2 us (3%)
  local copies, waits for them, and re-layouts  46.9 us (3%)
    reduce_scatter x9, waiting for transfers between devices, reduce_all(): part = lax.psum_scatter(g, ('seq', 'dp'), scatter_dimension=0, tiled=True)  1010 us
    pallas_call x1, Pallas kernels, gather(): pl.pallas_call(functools.partial(gather_kernel, nw, nz), out_shape=shp, i...  215 us
    all_gather x6, waiting for transfers between devices, reduce_all(): lax.all_gather(part, 'dp', axis=0, tiled=True).astype(jnp.float32)  137 us
    dot_general x9, matrix products, mm_tn(): lax.dot_general(left, right, TN, preferred_element_type=jnp.float32)  67.3 us
    dot_general x8, matrix products, mm_nt(): return lax.dot_general(left, right, NT, preferred_element_type=jnp.float32)  60.3 us
    psum x1, blocking collectives, reduce_all(): lax.psum(g_small.astype(jnp.bfloat16), ('dp', 'seq')).astype(jnp.float32)  46.9 us
    dot_general x9, matrix products, mm(): return jnp.dot(left, right, preferred_element_type=jnp.float32)  46.5 us
  transfers between devices with their start and end apart: 23, of which 18 were waited for; matrix products, arithmetic and copies ran while one was open for 8% of the time, Pallas kernels for 2%

profile of v1, /device:TPU:0, one launch (start us, length us, event | category | flops | bytes accessed | tf_op | source)
XLA Modules:
  0.0 1817.9 jit_solution(7413502090053579466)
XLA Ops:
  7.2 3.0 concatenate.44.refs_9_
  24.9 215.2 %shard_map.280 = (bf16[4,4,2,32,4096]{4,3,2,1,0:T(8,128)(2,1)S(1)}, bf16[4,4,2,128,1024]{4,3,2,1,0:T(8,128)(2,1)S(1)}, bf16[4,4,2,32,3072]{4,3,2,1,0:T(8,128)(2,...) custom-call(bf16[4,2,32,4096]{3,2,1,0:T(8,128)(2,1)S(1)} %bitcast.14, ...), custom_call_target="tpu_custom_call" | custom-call | bytes 100663296 | tf_op jit(solution)/shard_map/pallas_call | solution.py:153
  241.4 2.0 copy-done.20
  249.6 7.6 fusion.86
  257.3 7.5 fusion.82
  265.2 4.0 convolution_convert_fusion.5.q_ref.k_ref.v_ref
  269.2 1.7 slice.256
  273.8 4.0 copy.33
  283.0 4.9 convolution_convert_fusion.7.pt_ref
  288.0 20.8 %shard_map.281 = (bf16[512,1024]{1,0:T(8,128)(2,1)S(1)}, bf16[8,512,1024]{2,1,0:T(8,128)(2,1)}) custom-call(s32[2]{0:T(128)S(1)} %pad_add_fusion.sc_ref, bf16[512,3072]{1,0:T(8,128)(2,1)} %copy-done.29, bf16[512,3072]{1,0:T(8,128)(2,1)} %copy-done.29, bf16[512,3072]{1,0:T(8,128)(2,1)} %copy-done.29, ...), custom_call_target="tpu_custom_call" | custom-call | flops 3221225472 | bytes 20971520 | tf_op jit(solution)/shard_map/pallas_call | solution.py:232
  312.0 2.5 fusion.75
  317.8 1.8 fusion.78
  322.6 2.0 slice-done.1
  324.6 7.0 fusion.76
  331.6 10.0 fusion.85
  343.4 1.8 fusion.19
  345.1 12.4 multiply_convert_fusion.1
  357.5 9.6 multiply_reduce_fusion
  367.9 2.9 multiply_reduce_fusion.1
  370.8 4.3 fusion.12
  376.4 2.9 multiply_convert_fusion.6
  381.1 4.6 convolution_convert_fusion.6
  386.3 6.3 multiply_reduce_fusion.2
  395.5 34.6 %shard_map.282 = (bf16[512,1024]{1,0:T(8,128)(2,1)S(1)}, f32[512,1024]{1,0:T(8,128)}, f32[512,1024]{1,0:T(8,128)}, bf16[512,1024]{1,0:T(8,128)(2,1)S(1)}, bf16[5...) custom-call(s32[2]{0:T(128)S(1)} %pad_add_fusion.sc_ref, bf16[512,3072]{1,0:T(8,128)(2,1)} %copy-done.29, ...), custom_call_target="tpu_custom_call" | custom-call | flops 6442450944 | bytes 31457280 | tf_op jit(solution)/shard_map/pallas_call | solution.py:242
  430.5 4.0 collective-permute-done.5
  436.2 6.2 convolution_convert_fusion.4
  442.6 10.8 convolution_convert_fusion.1
  453.4 12.1 convolution_convert_fusion
  465.6 7.6 multiply_reduce_fusion.3
  474.0 11.6 convolution_convert_fusion.2
  486.4 10.4 multiply_convert_fusion
  496.9 9.8 fusion.39
  506.7 6.8 convolution_convert_fusion.3
  515.0 4.5 convolution_convert_fusion.8
  519.8 6.3 convolution_convert_fusion.10
  526.1 2.6 copy.34
  529.9 4.3 convolution_convert_fusion.9
  535.0 104.9 %reduce-scatter.14.cloned.1.call-done = bf16[32,3072]{1,0:T(8,128)(2,1)} async-done(((bf16[1024,3072]{1,0:T(8,128)(2,1)}), bf16[32,3072]{1,0:T(8,128)(2,1)}) %reduce-scatter.14.cloned.1.call-update) | async-done | bytes 196624 | tf_op jit(solution)/shard_map/reduce_scatter | solution.py:254
  640.0 150.4 %reduce-scatter.24.cloned.1.call-done = bf16[32,4096]{1,0:T(8,128)(2,1)} async-done(((bf16[1024,4096]{1,0:T(8,128)(2,1)}), bf16[32,4096]{1,0:T(8,128)(2,1)}) %reduce-scatter.24.cloned.1.call-update) | async-done | bytes 262160 | tf_op jit(solution)/shard_map/reduce_scatter | solution.py:254
  790.4 147.0 %reduce-scatter.26.cloned.1.call-done = bf16[128,1024]{1,0:T(8,128)(2,1)} async-done(((bf16[4096,1024]{1,0:T(8,128)(2,1)}), bf16[128,1024]{1,0:T(8,128)(2,1)}) %reduce-scatter.26.cloned.1.call-update) | async-done | bytes 262160 | tf_op jit(solution)/shard_map/reduce_scatter | solution.py:254
  937.5 146.9 %reduce-scatter.12.cloned.1.call-done = bf16[128,1024]{1,0:T(8,128)(2,1)} async-done(((bf16[4096,1024]{1,0:T(8,128)(2,1)}), bf16[128,1024]{1,0:T(8,128)(2,1)}) %reduce-scatter.12.cloned.1.call-update) | async-done | bytes 262160 | tf_op jit(solution)/shard_map/reduce_scatter | solution.py:254
  1084.4 147.0 %reduce-scatter.10.cloned.1.call-done = bf16[32,4096]{1,0:T(8,128)(2,1)} async-done(((bf16[1024,4096]{1,0:T(8,128)(2,1)}), bf16[32,4096]{1,0:T(8,128)(2,1)}) %reduce-scatter.10.cloned.1.call-update) | async-done | bytes 262160 | tf_op jit(solution)/shard_map/reduce_scatter | solution.py:254
  1234.1 2.3 fusion.38
  1237.2 2.1 collective-permute-start.7
  1239.3 17.7 collective-permute-done.3
  1258.3 46.9 %psum.7 = bf16[19,1024]{1,0:T(8,128)(2,1)S(1)} all-reduce(bf16[19,1024]{1,0:T(8,128)(2,1)S(1)} %concatenate.53), channel_id=1, replica_groups=mesh['dp'=8,'seq'=4] {'dp','seq'}, use_global_device_ids=true, to_apply=%region_41.42 | all-reduce | flops 19456 | bytes 77824 | tf_op jit(solution)/shard_map/psum | solution.py:257
  1308.6 60.4 %reduce-scatter.22.cloned.1.call-done = bf16[32,1024]{1,0:T(8,128)(2,1)} async-done(((bf16[1024,1024]{1,0:T(8,128)(2,1)}), bf16[32,1024]{1,0:T(8,128)(2,1)}) %reduce-scatter.22.cloned.1.call-update) | async-done | bytes 65552 | tf_op jit(solution)/shard_map/reduce_scatter | solution.py:254
  1369.0 9.2 all_gather.33
  1379.3 124.8 %reduce-scatter.16.cloned.1.call-done = bf16[128,256]{1,0:T(8,128)(2,1)} async-done(((bf16[4096,256]{1,0:T(8,128)(2,1)}), bf16[128,256]{1,0:T(8,128)(2,1)}) %reduce-scatter.16.cloned.1.call-update) | async-done | bytes 65552 | tf_op jit(solution)/shard_map/reduce_scatter | solution.py:254
  1504.1 9.2 all_gather.30
  1514.4 125.1 %reduce-scatter.18.cloned.1.call-done = bf16[32,1024]{1,0:T(8,128)(2,1)} async-done(((bf16[1024,1024]{1,0:T(8,128)(2,1)}), bf16[32,1024]{1,0:T(8,128)(2,1)}) %reduce-scatter.18.cloned.1.call-update) | async-done | bytes 65552 | tf_op jit(solution)/shard_map/reduce_scatter | solution.py:254
  1639.4 10.7 all_gather.31
  1651.2 9.4 all-gather.13.cloned.1.call-done
  1660.6 2.8 convert_element_type.332
  1663.4 24.8 %all-gather.11.cloned.1.call-done = bf16[256,3072]{1,0:T(8,128)(2,1)} async-done(((bf16[32,3072]{1,0:T(8,128)(2,1)}), bf16[256,3072]{1,0:T(8,128)(2,1)}) %all-gather.11.cloned.1.call-update) | async-done | bytes 1572880 | tf_op jit(solution)/shard_map/all_gather | solution.py:255
  1688.2 3.4 convert_element_type.326
  1691.7 26.2 %all-gather.15.cloned.1.call-done = bf16[256,4096]{1,0:T(8,128)(2,1)} async-done(((bf16[32,4096]{1,0:T(8,128)(2,1)}), bf16[256,4096]{1,0:T(8,128)(2,1)}) %all-gather.15.cloned.1.call-update) | async-done | bytes 2097168 | tf_op jit(solution)/shard_map/all_gather | solution.py:255
  1717.9 4.1 convert_element_type.336
  1722.0 25.7 %all-gather.17.cloned.1.call-done = bf16[1024,1024]{1,0:T(8,128)(2,1)} async-done(((bf16[128,1024]{1,0:T(8,128)(2,1)}), bf16[1024,1024]{1,0:T(8,128)(2,1)}) %all-gather.17.cloned.1.call-update) | async-done | bytes 2097168 | tf_op jit(solution)/shard_map/all_gather | solution.py:255
  1747.7 4.1 convert_element_type.338
  1751.8 25.6 %all-gather.9.cloned.1.call-done = bf16[1024,1024]{1,0:T(8,128)(2,1)} async-done(((bf16[128,1024]{1,0:T(8,128)(2,1)}), bf16[1024,1024]{1,0:T(8,128)(2,1)}) %all-gather.9.cloned.1.call-update) | async-done | bytes 2097168 | tf_op jit(solution)/shard_map/all_gather | solution.py:255
  1777.4 4.1 convert_element_type.324
  1781.5 25.6 %all-gather.7.cloned.1.call-done = bf16[256,4096]{1,0:T(8,128)(2,1)} async-done(((bf16[32,4096]{1,0:T(8,128)(2,1)}), bf16[256,4096]{1,0:T(8,128)(2,1)}) %all-gather.7.cloned.1.call-update) | async-done | bytes 2097168 | tf_op jit(solution)/shard_map/all_gather | solution.py:255
  1807.1 4.1 convert_element_type.322
  (290 shorter events, 65.5 us)
Async XLA Ops:
  7.2 527.2 %reduce-scatter.20.cloned.1.call-start = ((), (), s32[]{:S(2)}) async-start(), calls=%async_computation.17 | async-start | bytes 4325376 | tf_op jit(solution)/shard_map/reduce_scatter | solution.py:254
  246.1 11.1 copy-start.17
  246.1 11.1 copy-start.1
  246.1 11.1 copy-start.18
  246.1 19.0 %copy-start.19 = (bf16[4,4,2,32,3072]{4,3,2,1,0:T(8,128)(2,1)}, bf16[4,4,2,32,3072]{4,3,2,1,0:T(8,128)(2,1)S(1)}, u32[]{:S(2)}) copy-start(bf16[4,4,2,32,3072]{4,3,2,1,0:T(8,128)(2,1)S(1)} %get-tuple-element.40) | copy-start | bytes 18874372
  246.1 97.2 %copy-start.3 = (bf16[2,256,1024]{2,1,0:T(8,128)(2,1)}, bf16[2,256,1024]{2,1,0:T(8,128)(2,1)S(1)}, u32[]{:S(2)}) copy-start(bf16[2,256,1024]{2,1,0:T(8,128)(2,1)S(1)} %get-tuple-element.48) | copy-start | bytes 3145732
  246.2 11.0 copy-start.54
  246.2 11.0 copy-start.56
  264.8 4.4 copy-start.39
  271.5 16.4 collective-permute-start
  273.8 4.6 copy-start.70
  283.0 5.0 copy-start.49
  287.9 20.9 %copy-start.23 = (bf16[4,4,2,32,1024]{4,3,2,1,0:T(8,128)(2,1)S(1)}, bf16[4,4,2,32,1024]{4,3,2,1,0:T(8,128)(2,1)}, u32[]{:S(2)}) copy-start(bf16[4,4,2,32,1024]{4,3,2,1,0:T(8,128)(2,1)} %copy-done.22) | copy-start | bytes 6291460
  287.9 20.9 %copy-start.40 = (f32[512,1024]{1,0:T(8,128)S(1)}, f32[512,1024]{1,0:T(8,128)}, u32[]{:S(2)}) copy-start(f32[512,1024]{1,0:T(8,128)} %copy-done.39) | copy-start | bytes 6291460
  288.0 20.8 %copy-start = (bf16[512,2048]{1,0:T(8,128)(2,1)}, bf16[512,2048]{1,0:T(8,128)(2,1)S(1)}, u32[]{:S(2)}) copy-start(bf16[512,2048]{1,0:T(8,128)(2,1)S(1)} %collective-permute-done.ko_ref.vo_ref) | copy-start | bytes 6291460
  308.8 3.2 copy-start.21
  310.2 4.3 copy-start.46
  316.6 1.2 collective-permute-start.1
  319.7 51.1 %copy-start.32 = (f32[512,1024]{1,0:T(8,128)}, f32[512,1024]{1,0:T(8,128)S(1)}, u32[]{:S(2)}) copy-start(f32[512,1024]{1,0:T(8,128)S(1)} %get-tuple-element.90) | copy-start | bytes 6291460
  320.1 4.5 slice-start.1
  321.7 45.4 %copy-start.45 = (f32[512,1024]{1,0:T(8,128)}, f32[512,1024]{1,0:T(8,128)S(1)}, u32[]{:S(2)}) copy-start(f32[512,1024]{1,0:T(8,128)S(1)} %get-tuple-element.140) | copy-start | bytes 6291460
  345.1 22.0 %copy-start.38 = (f32[512,1024]{1,0:T(8,128)}, f32[512,1024]{1,0:T(8,128)S(1)}, u32[]{:S(2)}) copy-start(f32[512,1024]{1,0:T(8,128)S(1)} %get-tuple-element.91) | copy-start | bytes 6291460
  370.8 5.6 copy-start.31
  375.2 1.2 collective-permute-start.4
  385.8 6.8 copy-start.35
  385.8 254.1 %reduce-scatter.14.cloned.1.call-start = ((), (), s32[]{:S(2)}) async-start(), calls=%async_computation.13 | async-start | bytes 6488064 | tf_op jit(solution)/shard_map/reduce_scatter | solution.py:254
  386.3 6.3 copy-start.48
  430.1 4.5 copy-start.51
  430.1 4.5 copy-start.52
  430.3 4.3 collective-permute-start.5
  442.3 348.0 %reduce-scatter.24.cloned.1.call-start = ((), (), s32[]{:S(2)}) async-start(), calls=%async_computation.20 | async-start | bytes 8650752 | tf_op jit(solution)/shard_map/reduce_scatter | solution.py:254
  453.4 484.1 %reduce-scatter.26.cloned.1.call-start = ((), (), s32[]{:S(2)}) async-start(), calls=%async_computation.22 | async-start | bytes 8650752 | tf_op jit(solution)/shard_map/reduce_scatter | solution.py:254
  465.6 618.8 %reduce-scatter.12.cloned.1.call-start = ((), (), s32[]{:S(2)}) async-start(), calls=%async_computation.11 | async-start | bytes 8650752 | tf_op jit(solution)/shard_map/reduce_scatter | solution.py:254
  465.6 7.7 copy-start.37
  465.6 7.7 copy-start.42
  474.0 12.3 copy-start.43
  485.7 745.7 %reduce-scatter.10.cloned.1.call-start = ((), (), s32[]{:S(2)}) async-start(), calls=%async_computation.9 | async-start | bytes 8650752 | tf_op jit(solution)/shard_map/reduce_scatter | solution.py:254
  486.4 10.5 copy-start.2
  486.4 10.5 copy-start.55
  486.4 10.5 copy-start.57
  513.5 855.6 %reduce-scatter.22.cloned.1.call-start = ((), (), s32[]{:S(2)}) async-start(), calls=%async_computation.19 | async-start | bytes 2162688 | tf_op jit(solution)/shard_map/reduce_scatter | solution.py:254
  519.6 984.5 %reduce-scatter.16.cloned.1.call-start = ((), (), s32[]{:S(2)}) async-start(), calls=%async_computation.15 | async-start | bytes 2162688 | tf_op jit(solution)/shard_map/reduce_scatter | solution.py:254
  528.7 1110.7 %reduce-scatter.18.cloned.1.call-start = ((), (), s32[]{:S(2)}) async-start(), calls=%async_computation.16 | async-start | bytes 2162688 | tf_op jit(solution)/shard_map/reduce_scatter | solution.py:254
  534.2 697.2 %copy-start.4 = (bf16[2,256,1024]{2,1,0:T(8,128)(2,1)S(1)}, bf16[2,256,1024]{2,1,0:T(8,128)(2,1)}, u32[]{:S(2)}) copy-start(bf16[2,256,1024]{2,1,0:T(8,128)(2,1)} %copy-done.3) | copy-start | bytes 3145732
  534.2 697.4 %copy-start.63 = (bf16[1024]{0:T(1024)(128)(2,1)S(1)}, bf16[1024]{0:T(1024)(128)(2,1)}, u32[]{:S(2)}) copy-start(bf16[1024]{0:T(1024)(128)(2,1)} %get-tuple-element.65) | copy-start | bytes 6148
  534.2 697.4 %copy-start.68 = (bf16[1024]{0:T(1024)(128)(2,1)S(1)}, bf16[1024]{0:T(1024)(128)(2,1)}, u32[]{:S(2)}) copy-start(bf16[1024]{0:T(1024)(128)(2,1)} %get-tuple-element.57) | copy-start | bytes 6148
  534.2 697.4 %copy-start.67 = (bf16[1024]{0:T(1024)(128)(2,1)S(1)}, bf16[1024]{0:T(1024)(128)(2,1)}, u32[]{:S(2)}) copy-start(bf16[1024]{0:T(1024)(128)(2,1)} %get-tuple-element.81) | copy-start | bytes 6148
  534.2 697.5 %copy-start.69 = (bf16[1024]{0:T(1024)(128)(2,1)S(1)}, bf16[1024]{0:T(1024)(128)(2,1)}, u32[]{:S(2)}) copy-start(bf16[1024]{0:T(1024)(128)(2,1)} %get-tuple-element.59) | copy-start | bytes 6148
  534.2 697.5 %copy-start.62 = (bf16[1024]{0:T(1024)(128)(2,1)S(1)}, bf16[1024]{0:T(1024)(128)(2,1)}, u32[]{:S(2)}) copy-start(bf16[1024]{0:T(1024)(128)(2,1)} %get-tuple-element.74) | copy-start | bytes 6148
  534.3 697.5 %copy-start.61 = (bf16[1024]{0:T(1024)(128)(2,1)S(1)}, bf16[1024]{0:T(1024)(128)(2,1)}, u32[]{:S(2)}) copy-start(bf16[1024]{0:T(1024)(128)(2,1)} %get-tuple-element.75) | copy-start | bytes 6148
  534.3 697.5 %copy-start.60 = (bf16[1024]{0:T(1024)(128)(2,1)S(1)}, bf16[1024]{0:T(1024)(128)(2,1)}, u32[]{:S(2)}) copy-start(bf16[1024]{0:T(1024)(128)(2,1)} %get-tuple-element.78) | copy-start | bytes 6148
  534.3 697.5 %copy-start.59 = (bf16[1024]{0:T(1024)(128)(2,1)S(1)}, bf16[1024]{0:T(1024)(128)(2,1)}, u32[]{:S(2)}) copy-start(bf16[1024]{0:T(1024)(128)(2,1)} %get-tuple-element.79) | copy-start | bytes 6148
  534.3 697.5 %copy-start.58 = (bf16[1024]{0:T(1024)(128)(2,1)S(1)}, bf16[1024]{0:T(1024)(128)(2,1)}, u32[]{:S(2)}) copy-start(bf16[1024]{0:T(1024)(128)(2,1)} %get-tuple-element.80) | copy-start | bytes 6148
  534.3 697.5 %copy-start.66 = (bf16[1024]{0:T(1024)(128)(2,1)S(1)}, bf16[1024]{0:T(1024)(128)(2,1)}, u32[]{:S(2)}) copy-start(bf16[1024]{0:T(1024)(128)(2,1)} %get-tuple-element.82) | copy-start | bytes 6148
  534.3 1126.3 %all-gather.13.cloned.1.call-start = ((), (), s32[]{:S(2)}) async-start(), calls=%async_computation.18 | async-start | bytes 1179648 | tf_op jit(solution)/shard_map/all_gather | solution.py:255
  534.9 1153.3 %all-gather.11.cloned.1.call-start = ((), (), s32[]{:S(2)}) async-start(), calls=%async_computation.14 | async-start | bytes 1769472 | tf_op jit(solution)/shard_map/all_gather | solution.py:255
  639.9 1078.0 %all-gather.15.cloned.1.call-start = ((), (), s32[]{:S(2)}) async-start(), calls=%async_computation.21 | async-start | bytes 2359296 | tf_op jit(solution)/shard_map/all_gather | solution.py:255
  790.4 957.4 %all-gather.17.cloned.1.call-start = ((), (), s32[]{:S(2)}) async-start(), calls=%async_computation.23 | async-start | bytes 2359296 | tf_op jit(solution)/shard_map/all_gather | solution.py:255
  937.4 840.0 %all-gather.9.cloned.1.call-start = ((), (), s32[]{:S(2)}) async-start(), calls=%async_computation.12 | async-start | bytes 2359296 | tf_op jit(solution)/shard_map/all_gather | solution.py:255
  1084.4 722.7 %all-gather.7.cloned.1.call-start = ((), (), s32[]{:S(2)}) async-start(), calls=%async_computation.10 | async-start | bytes 2359296 | tf_op jit(solution)/shard_map/all_gather | solution.py:255
  1233.3 6.0 collective-permute-start.2
  1234.0 23.0 %collective-permute-start.3 = (bf16[256,1024]{1,0:T(8,128)(2,1)S(1)}, bf16[256,1024]{1,0:T(8,128)(2,1)S(1)}, u32[]{:S(2)}, u32[]{:S(2)}) collective-permute-start(bf16[256,1024]{1,0:T(8,128)(2,1)S(1)} %get-tuple-element.103), channel_id=1, source_target_pairs={{0,1},{1,0},{2,5},{3,4},{4,3},{5,2},{6,7},{7,6},{8,9},{9,8},{10,13... | collective-permute-start | bytes 1572872 | tf_op jit(solution)/shard_map/ppermute | solution.py:337
  1236.5 70.6 %collective-permute-start.6 = (bf16[256,1024]{1,0:T(8,128)(2,1)S(1)}, bf16[256,1024]{1,0:T(8,128)(2,1)S(1)}, u32[]{:S(2)}, u32[]{:S(2)}) collective-permute-start(bf16[256,1024]{1,0:T(8,128)(2,1)S(1)} %get-tuple-element.98), channel_id=1, source_target_pairs={{0,0},{1,1},{2,4},{3,5},{4,2},{5,3},{6,6},{7,7},{8,8},{9,9},{10,12... | collective-permute-start | bytes 1572872 | tf_op jit(solution)/shard_map/ppermute | solution.py:336
  1237.2 69.9 %collective-permute-start.7 = (bf16[256,1024]{1,0:T(8,128)(2,1)S(1)}, bf16[256,1024]{1,0:T(8,128)(2,1)S(1)}, u32[]{:S(2)}, u32[]{:S(2)}) collective-permute-start(bf16[256,1024]{1,0:T(8,128)(2,1)S(1)} %get-tuple-element.99), channel_id=1, source_target_pairs={{0,1},{1,0},{2,5},{3,4},{4,3},{5,2},{6,7},{7,6},{8,9},{9,8},{10,13... | collective-permute-start | bytes 1572872 | tf_op jit(solution)/shard_map/ppermute | solution.py:337
  (33 other events, 53.3 us)
Sparse Core Ops, SparseCore 0:
  385.9 138.0 reduce-scatter.19
  529.7 110.2 reduce-scatter.13
  642.3 147.9 reduce-scatter.23
  792.6 144.7 reduce-scatter.25
  939.7 144.6 reduce-scatter.11
  1086.6 144.7 reduce-scatter.9
  1234.3 134.6 reduce-scatter.21
  1371.9 132.1 reduce-scatter.15
  1507.0 132.3 reduce-scatter.17
  1641.2 19.4 all-gather.12
  1662.5 25.6 all-gather.10
  1690.0 27.8 all-gather.14
  1719.8 27.8 all-gather.16
  1749.5 27.8 all-gather.8
  1779.1 27.8 all-gather.6

commit v2 on v1

--- a/solution.py
+++ b/solution.py
@@ -248,14 +248,199 @@
         cost_estimate=pl.CostEstimate(flops=H*T*2*T*HD*2*6,bytes_accessed=30*2**20,transcendentals=0),
     )(sc,qkv,qkv,qkv,kvo,kvo,pt,pb,g,p)
 
-def reduce_all(grads, g_small):
-    outs = []
-    for g in grads:
-        part = lax.psum_scatter(g, ("seq", "dp"), scatter_dimension=0, tiled=True)
-        outs.append(lax.all_gather(part, "dp", axis=0, tiled=True).astype(jnp.float32))
-    width = g_small.shape[1] // lax.axis_size("seq")
-    total = lax.psum(g_small.astype(jnp.bfloat16), ("dp", "seq")).astype(jnp.float32)
-    return (*outs, lax.dynamic_slice_in_dim(total, lax.axis_index("seq") * width, width, axis=1))
+def reduce_kernel(chunks, nz, ng, *refs):
+    n=len(chunks)
+    gs=refs[:ng]; gi=refs[ng]; outs=refs[ng+1:2*ng+1]; gi_o=refs[2*ng+1]; cbig=refs[2*ng+2:2*ng+2+n]
+    rest=list(refs[2*ng+2+n:])
+    t1=rest[:2]; cin=rest[2:4]; rest=rest[4:]
+    x1=rest[:n]; y1=rest[n:2*n]; x2=rest[2*n:3*n]; y2=rest[3*n:4*n]; zb=rest[4*n:5*n]
+    (cs,cr,x1s,x1r,y1s,y1r,x2s,x2r,y2s,y2r,axs,axr,ays,ayr,aas,aar,abs_,abr,acs,acr,zrs,zrr,zls,zlr,own,cld,loc,fs,frv,keeps)=rest[5*n:]
+    k=place(); dp,z,c=k["dp"],k["z"],k["c"]
+    bx=k["p"]%2; by=k["p"]//2
+    tcore=z//2; tdp=dp-c+tcore
+    bar=pltpu.get_barrier_semaphore()
+    def sig(dev): pl.semaphore_signal(bar,inc=1,device_id=dev,device_id_type=MESH)
+    for a in ("core","xn","yn"): sig((k[a],z))
+    for ok,zz in ((z>0,z-1),(z<nz-1,z+1)):
+        @pl.when(ok)
+        def _(): sig((dp,zz))
+    for u in range(2):
+        @pl.when(jnp.logical_or(tcore!=c, 2*c+u!=z))
+        def _(): sig((tdp,2*c+u))
+    one=lambda b: jnp.where(b,1,0)
+    pl.semaphore_wait(bar,3+one(z>0)+one(z<nz-1)+2-one(tcore==c))
+    def rc(src,dst,s,r,dev):
+        return pltpu.make_async_remote_copy(src_ref=src,dst_ref=dst,send_sem=s,recv_sem=r,device_id=dev,device_id_type=MESH)
+    xn=(k["xn"],z); yn=(k["yn"],z); cn=(k["core"],z)
+    ns=t1[0].shape[0]; nc=cin[0].shape[0]
+    def tb(i): return t1[0].at[i%ns] if chunks[i][4]==1024 else t1[1].at[0]
+    def cb(i): return cin[0].at[i%nc] if chunks[i][4]==1024 else cin[1].at[0]
+    def sl(i): return pl.ds(chunks[i][1],chunks[i][2]),pl.ds(chunks[i][3],chunks[i][4])
+    def g(i,cc): return gs[chunks[i][0]].at[(slice(None),slice(None),slice(None),cc)+sl(i)]
+    def o(i,yy,xx,half=None):
+        r0,q,c0,cc=chunks[i][1:]
+        if half is not None: q=q//2; r0=r0+half*q
+        return outs[chunks[i][0]].at[yy,xx,c,pl.ds(r0,q),pl.ds(c0,cc)]
+    def oc(i): return outs[chunks[i][0]].at[(slice(None),slice(None),c)+sl(i)]
+    H=lambda i: chunks[i][2]//2
+    A=lambda i: pl.ds(0,H(i))
+    B=lambda i: pl.ds(H(i),H(i))
+    send_c=lambda i: rc(g(i,1-c),cbig[i],cs.at[i],cr.at[i],cn)
+    load_own=lambda i: pltpu.make_async_copy(g(i,c),tb(i),own.at[i])
+    load_c=lambda i: pltpu.make_async_copy(cbig[i],cb(i),cld.at[i])
+    send_x1=lambda i: rc(tb(i).at[:,:,1-bx,A(i)],x1[i],x1s.at[i],x1r.at[i],xn)
+    send_y1=lambda i: rc(tb(i).at[:,1-by,:,B(i)],y1[i],y1s.at[i],y1r.at[i],yn)
+    send_x2=lambda i: rc(tb(i).at[:,1-by,bx,A(i)],x2[i],x2s.at[i],x2r.at[i],yn)
+    send_y2=lambda i: rc(tb(i).at[:,by,1-bx,B(i)],y2[i],y2s.at[i],y2r.at[i],xn)
+    send_r=lambda i,t: rc(tb(i).at[t,by,bx],zb[i].at[t],zrs.at[i,t],zrr.at[i,t],(dp,z+1))
+    def send_l(i,t,last): return rc(tb(i).at[t,by,bx],zb[i].at[nz if last else t],zls.at[i,t],zlr.at[i,t],(dp,z-1))
+    send_ax=lambda i: rc(tb(i).at[z,by,bx],o(i,by,bx),axs.at[i],axr.at[i],xn)
+    send_ay=lambda i: rc(tb(i).at[z,by,bx],o(i,by,bx),ays.at[i],ayr.at[i],yn)
+    keep_a=lambda i: pltpu.make_async_copy(tb(i).at[z,by,bx],o(i,by,bx),loc.at[i])
+    send_aa=lambda i: rc(o(i,by,1-bx,0),o(i,by,1-bx,0),aas.at[i],aar.at[i],yn)
+    send_ab=lambda i: rc(o(i,1-by,bx,1),o(i,1-by,bx,1),abs_.at[i],abr.at[i],xn)
+    send_ac=lambda i: rc(oc(i),oc(i),acs.at[i],acr.at[i],cn)
+    def add(dst,src):
+        dst[...]=(dst[...].astype(jnp.float32)+src[...].astype(jnp.float32)).astype(jnp.bfloat16)
+    def loop(m,f):
+        lax.fori_loop(0,m,lambda j,_: (f(j),0)[1],0)
+    def move(u): return rc(gi.at[u],gi_o.at[z%2],fs.at[u],frv.at[z%2],(tdp,2*c+u))
+    keep=pltpu.make_async_copy(gi.at[z%2],gi_o.at[z%2],keeps.at[0])
+    for u in range(2):
+        @pl.when(jnp.logical_or(tcore!=c,2*c+u!=z))
+        def _(): move(u).start()
+    @pl.when(tcore==c)
+    def _(): keep.start()
+    def drain(i):
+        for f in (send_x1,send_y1,send_x2,send_y2,send_ax,send_ay): f(i).wait_send()
+        for t in range(nz):
+            @pl.when(z<t)
+            def _(): send_r(i,t).wait_send()
+            @pl.when(z>t)
+            def _(): send_l(i,t,False).wait_send()
+    def s0(i):
+        if chunks[i][4]==1024 and i>=ns: drain(i-ns)
+        send_c(i).start(); load_own(i).start()
+    def s1a(i):
+        send_c(i).wait_recv(); load_c(i).start()
+    def s1(i):
+        load_own(i).wait(); load_c(i).wait()
+        T=tb(i); C=cb(i)
+        loop(nz*4,lambda j: add(T.at[j//4,(j//2)%2,j%2],C.at[j//4,(j//2)%2,j%2]))
+        send_x1(i).start(); send_y1(i).start()
+    def s2(i):
+        T=tb(i)
+        send_x1(i).wait_recv()
+        loop(nz*2,lambda j: add(T.at[j//2,j%2,bx,A(i)],x1[i].at[j//2,j%2]))
+        send_x2(i).start()
+        send_y1(i).wait_recv()
+        loop(nz*2,lambda j: add(T.at[j//2,by,j%2,B(i)],y1[i].at[j//2,j%2]))
+        send_y2(i).start()
+    def s3(i):
+        T=tb(i)
+        send_x2(i).wait_recv()
+        loop(nz,lambda j: add(T.at[j,by,bx,A(i)],x2[i].at[j]))
+        send_y2(i).wait_recv()
+        loop(nz,lambda j: add(T.at[j,by,bx,B(i)],y2[i].at[j]))
+        for t in range(1,nz):
+            @pl.when(z==0)
+            def _(): send_r(i,t).start()
+        for t in range(nz-1):
+            @pl.when(z==nz-1)
+            def _(): send_l(i,t,t==nz-2).start()
+    def hop(i,h):
+        T=tb(i)
+        @pl.when(z==h)
+        def _():
+            for t in range(h+1,nz):
+                send_r(i,t).wait_recv()
+                add(T.at[t,by,bx],zb[i].at[t])
+                send_r(i,t).start()
+        @pl.when(z==nz-1-h)
+        def _():
+            for t in range(nz-1-h):
+                send_l(i,t,False).wait_recv()
+                add(T.at[t,by,bx],zb[i].at[t])
+                send_l(i,t,t==nz-2-h).start()
+    def s6(i):
+        T=tb(i)
+        @pl.when(z>0)
+        def _():
+            send_r(i,z).wait_recv()
+            add(T.at[z,by,bx],zb[i].at[z])
+        @pl.when(z<nz-1)
+        def _():
+            send_l(i,z,False).wait_recv()
+            add(T.at[z,by,bx],zb[i].at[nz])
+        send_ax(i).start(); send_ay(i).start(); keep_a(i).start()
+    def s7(i):
+        send_ax(i).wait_recv(); send_aa(i).start()
+        send_ay(i).wait_recv(); send_ab(i).start()
+    def s8(i):
+        keep_a(i).wait()
+        send_aa(i).wait_recv(); send_ab(i).wait_recv(); send_ac(i).start()
+    stages=[(s0,0),(s1a,LAGS[0]),(s1,LAGS[1]),(s2,LAGS[2]),(s3,LAGS[3])]
+    lag=LAGS[3]
+    for h in range(1,nz-1):
+        lag+=1; stages.append((functools.partial(lambda h,i: hop(i,h),h),lag))
+    for f in (s6,s7,s8):
+        lag+=1; stages.append((f,lag))
+    for s in range(n+lag):
+        for f,l in reversed(stages):
+            if 0<=s-l<n: f(s-l)
+    for i in range(n):
+        if chunks[i][4]!=1024 or i+ns>=n or not any(j==i+ns and chunks[j][4]==1024 for j in range(n)): drain(i)
+        send_c(i).wait_send()
+        for f in (send_aa,send_ab): f(i).wait_send()
+        send_ac(i).wait()
+    for u in range(2):
+        @pl.when(jnp.logical_or(tcore!=c,2*c+u!=z))
+        def _():
+            move(u).wait_send()
+            rc(gi.at[u],gi_o.at[u],fs.at[u],frv.at[u],(tdp,2*c+u)).wait_recv()
+    @pl.when(tcore==c)
+    def _(): keep.wait()
+LAGS=(2,3,4,5)
+SLOTS=12
+
+def reduce_call(grads,gi,nz,cid):
+    views=[x.reshape(nz,2,2,2,x.shape[0]//(8*nz),x.shape[1]) for x in grads]
+    chunks=[]
+    for w,v in enumerate(views):
+        r,cc=v.shape[4:]
+        wide=min(cc,1024)
+        for r0 in range(0,r,32):
+            for c0 in range(0,cc,wide): chunks.append((w,r0,32,c0,wide))
+    n=len(chunks); bf=jnp.bfloat16
+    any_=pl.BlockSpec(memory_space=pl.ANY)
+    outs=[jax.ShapeDtypeStruct((2,2,2)+v.shape[4:],bf) for v in views]+[jax.ShapeDtypeStruct(gi.shape,gi.dtype)]+[jax.ShapeDtypeStruct((nz,2,2,q,cc),bf) for _,_,q,_,cc in chunks]
+    V=pltpu.VMEM; S=pltpu.SemaphoreType.DMA
+    scratch=[V((SLOTS,nz,2,2,32,1024),bf),V((1,nz,2,2,32,128),bf),V((2,nz,2,2,32,1024),bf),V((1,nz,2,2,32,128),bf)]
+    scratch+=[V((nz,2,q//2,cc),bf) for _,_,q,_,cc in chunks]*1+[V((nz,2,q//2,cc),bf) for _,_,q,_,cc in chunks]
+    scratch+=[V((nz,q//2,cc),bf) for _,_,q,_,cc in chunks]+[V((nz,q//2,cc),bf) for _,_,q,_,cc in chunks]
+    scratch+=[V((nz+1,q,cc),bf) for _,_,q,_,cc in chunks]
+    scratch+=[S((n,))]*20+[S((n,nz))]*4+[S((n,))]*3+[S((2,)),S((2,)),S((1,))]
+    ng=len(grads)
+    o=pl.pallas_call(functools.partial(reduce_kernel,chunks,nz,ng),out_shape=outs,in_specs=[any_]*(ng+1),out_specs=[any_]*len(outs),
+        scratch_shapes=scratch,
+        compiler_params=pltpu.CompilerParams(collective_id=cid,has_side_effects=True,vmem_limit_bytes=58*2**20),
+        cost_estimate=pl.CostEstimate(flops=0,bytes_accessed=3*48*2**20,transcendentals=0),
+    )(*views,gi)
+    return [x.reshape(-1,x.shape[-1]) for x in o[:ng]],o[ng]
+
+def reduce_all(grads, g_small, grad_input, seq_count):
+    width = D // seq_count
+    small = g_small.reshape(32, seq_count, width // 128, 128).transpose(1, 2, 0, 3).reshape(seq_count, width // 4, 128)
+    small = jnp.pad(small, ((0, 0), (0, 256 - width // 4), (0, 0))).reshape(seq_count * 256, 128)
+    sums, grad_input = reduce_call(grads + [small], grad_input, seq_count, 1)
+    count = lax.axis_size("dp")
+    if count > 8:
+        groups = [[i + 8 * quad for quad in range(count // 8)] for i in range(8)]
+        sums = [lax.psum(x, "dp", axis_index_groups=groups) for x in sums]
+    sums = [x.astype(jnp.float32) for x in sums]
+    small = sums[-1][: width // 4].reshape(width // 128, 32, 128).transpose(1, 0, 2).reshape(32, width)
+    pos = sums[3].reshape(D, width)
+    return (*sums[:3], pos, *sums[4:-1], small), grad_input
 
 def layer_norm(stream, gain, offset):
     average = jnp.mean(stream, axis=-1, keepdims=True)
@@ -434,7 +619,7 @@
     gv = (gv + got[:, D:]).astype(jnp.bfloat16)
     gqkv = jnp.concatenate([gq, gk, gv], axis=1)
     g_wpos = mm_tn(sinusoid, gptab)
-    g_wpos = g_wpos.reshape(D, seq_count, D // seq_count).transpose(1, 0, 2).reshape(seq_count * D, D // seq_count)
+    g_wpos = g_wpos.reshape(D, seq_count, D // seq_count).transpose(1, 0, 2).reshape(D, D)
     g_wqkv = mm_tn(ha, gqkv)
     back, gg1, gb1 = layer_norm_back(x1, gains[1], mm_nt(gqkv, wqkv))
     gx1 = gx2 + back
@@ -444,13 +629,16 @@
     g_w1 = mm_tn(h1, ga1)
     back, gg0, gb0 = layer_norm_back(x0, gains[0], mm_nt(ga1, w1))
     gx0 = gx1 + back
-    grad_input = redistribute(gx0.astype(jnp.bfloat16).reshape(2, rows // 2, D)).astype(jnp.float32)
-
     g_small = jnp.concatenate(
-        [jnp.stack([gg0, gg1, gg2, gg3, gg4, gg5, gb0, gb1, gb2, gb3, gb4, gb5]), g_depth, g_pair[:2]], axis=0
+        [jnp.stack([gg0, gg1, gg2, gg3, gg4, gg5, gb0, gb1, gb2, gb3, gb4, gb5]), g_depth, g_pair[:2], jnp.zeros((13, D), jnp.float32)],
+        axis=0,
+    ).astype(jnp.bfloat16)
+    sums, grad_input = reduce_all(
+        [g_w1, g_w2, g_wqkv, g_wpos, g_wo, g_wci, g_wco, g_w3, g_w4],
+        g_small, gx0.astype(jnp.bfloat16).reshape(2, rows // 2, D), seq_count,
     )
-    outs = reduce_all([g_w1, g_w2, g_wqkv, g_wpos, g_wo, g_wci, g_wco, g_w3, g_w4], g_small)
-    s_w1, s_w2, s_wqkv, s_wpos, s_wo, s_wci, s_wco, s_w3, s_w4, s_small = outs
+    s_w1, s_w2, s_wqkv, s_wpos, s_wo, s_wci, s_wco, s_w3, s_w4, s_small = sums
+    grad_input = grad_input.astype(jnp.float32)
     return (
         encoded[None], grad_input[None], s_small[0:6], s_small[6:12], s_w1, s_w2, s_wqkv, s_wpos, s_small[17:19],
         s_wo, s_wci, s_small[12:17], s_wco, s_w3, s_w4,

time: 1830 us -> 847 us (0.46)
  waiting for transfers between devices: 1170 us -> 0.02 us
  Pallas kernels: 271 us -> 562 us
  blocking collectives: 76.1 us -> 0 us
    reduce_scatter x9 -> x0, waiting for transfers between devices: 1010 us -> none  [reduce_all(): part = lax.psum_scatter(g, ('seq', 'dp'), scatter_dimension=0, tiled=True)]
    pallas_call x0 -> x1, Pallas kernels: none -> 291 us  [reduce_call(): pl.pallas_call(functools.partial(reduce_kernel, chunks, nz, ng), out_shap...]
    all_gather x6 -> x0, waiting for transfers between devices: 137 us -> none  [reduce_all(): lax.all_gather(part, 'dp', axis=0, tiled=True).astype(jnp.float32)]
    psum x1 -> x0, blocking collectives: 46.9 us -> none  [reduce_all(): lax.psum(g_small.astype(jnp.bfloat16), ('dp', 'seq')).astype(jnp.float32)]
    all_gather x3 -> x0, blocking collectives: 29.1 us -> none  [reduce_all(): lax.all_gather(part, 'dp', axis=0, tiled=True).astype(jnp.float32)]
  transfers between devices with their start and end apart: 23 -> 6, of which waited for: 18 -> 0; matrix products, arithmetic and copies ran while one was open for 8% -> 7% of each run, Pallas kernels for 2% -> 4%
where the time goes in v2:
time: 847 us; the launch traced here: 840 us
  Pallas kernels  562 us (66%)
  matrix products  159 us (19%)
  local copies, waits for them, and re-layouts  55.6 us (7%)
  other arithmetic  53.3 us (6%)
    pallas_call x1, Pallas kernels, reduce_call(): pl.pallas_call(functools.partial(reduce_kernel, chunks, nz, ng), out_shap...  291 us
    pallas_call x1, Pallas kernels, gather(): pl.pallas_call(functools.partial(gather_kernel, nw, nz), out_shape=shp, i...  215 us
    dot_general x9, matrix products, mm_tn(): lax.dot_general(left, right, TN, preferred_element_type=jnp.float32)  63.8 us
    dot_general x8, matrix products, mm_nt(): return lax.dot_general(left, right, NT, preferred_element_type=jnp.float32)  49.5 us
    dot_general x9, matrix products, mm(): return jnp.dot(left, right, preferred_element_type=jnp.float32)  45.4 us
    pallas_call x1, Pallas kernels, attn_bwd(): pl.pallas_call(attn_bwd_kernel, grid=(H,), in_specs=[pl.BlockSpec(memory_...  34.5 us
    unnamed x194, local copies, waits for them, and re-layouts  33.5 us
    pallas_call x1, Pallas kernels, attn_fwd(): pl.pallas_call(attn_fwd_kernel, grid=(H,), in_specs=[pl.BlockSpec(memory_...  20.9 us
  transfers between devices with their start and end apart: 6, of which 0 were waited for; matrix products, arithmetic and copies ran while one was open for 7% of the time, Pallas kernels for 4%

profile of v2, /device:TPU:0, one launch (start us, length us, event | category | flops | bytes accessed | tf_op | source)
XLA Modules:
  0.0 840.1 jit_solution(13256452617877070429)
XLA Ops:
  0.7 3.0 concatenate.74.refs_9_
  3.7 1.6 copy-done.4
  5.3 1.6 copy-done.5
  6.9 1.6 copy-done.6
  8.5 1.6 copy-done.7
  10.1 1.4 copy-done.8
  18.3 215.2 %shard_map.280 = (bf16[4,4,2,32,4096]{4,3,2,1,0:T(8,128)(2,1)S(1)}, bf16[4,4,2,128,1024]{4,3,2,1,0:T(8,128)(2,1)S(1)}, bf16[4,4,2,32,3072]{4,3,2,1,0:T(8,128)(2,...) custom-call(bf16[4,2,32,4096]{3,2,1,0:T(8,128)(2,1)S(1)} %bitcast.22, ...), custom_call_target="tpu_custom_call" | custom-call | bytes 100663296 | tf_op jit(solution)/shard_map/pallas_call | solution.py:153
  233.5 1.3 copy-done.3
  234.8 2.0 copy-done.18
  236.8 1.3 copy-done.21
  238.2 1.3 copy-done.24
  241.0 7.8 fusion.85
  248.8 8.3 fusion.81
  257.6 4.0 convolution_convert_fusion.5.q_ref.k_ref.v_ref
  261.6 1.6 slice.265
  266.2 4.0 copy.35
  275.4 4.9 convolution_convert_fusion.7.pt_ref
  280.4 20.9 %shard_map.281 = (bf16[512,1024]{1,0:T(8,128)(2,1)S(1)}, bf16[8,512,1024]{2,1,0:T(8,128)(2,1)}) custom-call(s32[2]{0:T(128)S(1)} %pad_add_fusion.sc_ref, bf16[512,3072]{1,0:T(8,128)(2,1)} %copy-done.28, bf16[512,3072]{1,0:T(8,128)(2,1)} %copy-done.28, bf16[512,3072]{1,0:T(8,128)(2,1)} %copy-done.28, ...), custom_call_target="tpu_custom_call" | custom-call | flops 3221225472 | bytes 20971520 | tf_op jit(solution)/shard_map/pallas_call | solution.py:232
  301.3 1.3 fusion.82
  303.0 1.5 copy-done.19
  304.5 2.5 fusion.75
  307.6 1.4 copy-done.29
  311.1 1.8 fusion.78
  313.4 1.6 fusion.83
  315.6 1.3 slice-done.7
  316.8 7.1 fusion.76
  323.9 7.9 fusion.84
  333.8 11.7 %multiply_convert_fusion.1 = bf16[512,4096]{1,0:T(8,128)(2,1)} fusion(f32[512,4096]{1,0:T(8,128)} %fusion.76, bf16[4096,1024]{1,0:T(8,128)(2,1)} %bitcast.352, f32[512,1024]{1,0:T(8,128)S(1)} %get-tuple-element.113), kind=kOutput, calls=%fused_computation.1 | convolution fusion | flops 4314890240 | bytes 23068672 | tf_op jit(solution)/shard_map/dot_general | solution.py:497
  345.4 10.9 %convolution_convert_fusion = bf16[4096,1024]{1,0:T(8,128)(2,1)} fusion(f32[512,1024]{1,0:T(8,128)S(1)} %get-tuple-element.113, f32[512,4096]{1,0:T(8,128)} %fusion.76), kind=kOutput, calls=%fused_computation.6 | convolution fusion | flops 4310695936 | bytes 18874368 | tf_op jit(solution)/shard_map/dot_general | solution.py:501
  356.3 9.0 %multiply_reduce_fusion = (bf16[1024]{0:T(1024)(128)(2,1)S(1)}, f32[512]{0:T(512)S(1)}, f32[512]{0:T(512)S(1)}, bf16[1024]{0:T(1024)(128)(2,1)S(1)}, f32[512,1024]{1,0:T(8,128)S(1)}) fusion(f32[512,1024]{1,0:T(8,128)S(1)} %get-tuple-element.159, f32[512]{0:T(512)S(1)} %add_rsqrt_fusion.1, f32[512]{0:T(512)S(1)} %broadcast_multiply_fusion.12, ...), kind=kOutput, calls=%fused_computation.83 | convolution fusion | flops 4299682816 | bytes 16793600 | tf_op jit(solution)/shard_map/dot_general | solution.py:497
  366.1 2.4 multiply_reduce_fusion.1
  368.5 2.9 convolution_convert_fusion.8
  371.5 7.4 convolution_convert_fusion.1
  378.8 3.7 fusion.12
  384.2 5.4 collective-permute-start.2
  389.6 3.1 multiply_convert_fusion.6
  393.9 1.8 copy-done.20
  395.7 2.9 multiply_reduce_fusion.2
  400.2 1.3 convolution_convert_fusion.11.g_ref
  401.5 34.5 %shard_map.282 = (bf16[512,1024]{1,0:T(8,128)(2,1)S(1)}, f32[512,1024]{1,0:T(8,128)}, f32[512,1024]{1,0:T(8,128)}, bf16[512,1024]{1,0:T(8,128)(2,1)S(1)}, bf16[5...) custom-call(s32[2]{0:T(128)S(1)} %pad_add_fusion.sc_ref, bf16[512,3072]{1,0:T(8,128)(2,1)} %copy-done.28, ...), custom_call_target="tpu_custom_call" | custom-call | flops 6442450944 | bytes 31457280 | tf_op jit(solution)/shard_map/pallas_call | solution.py:242
  436.0 1.5 pad_maximum_fusion.2
  438.7 7.0 convolution_convert_fusion.10
  445.6 2.7 convolution_convert_fusion.9
  448.3 4.1 copy.36
  452.4 4.3 reshape_reshape.10.refs_3_
  456.8 6.9 convolution_convert_fusion.6
  463.7 1.4 select_bitcast_fusion.1
  466.3 2.6 add_convert_fusion.1
  469.0 5.1 multiply_reduce_fusion.3
  474.2 2.3 multiply_add_fusion
  476.5 10.8 %multiply_convert_fusion = bf16[512,4096]{1,0:T(8,128)(2,1)} fusion(f32[512,4096]{1,0:T(8,128)} %fusion.85, bf16[4096,1024]{1,0:T(8,128)(2,1)S(1)} %bitcast.243, f32[512,1024]{1,0:T(8,128)S(1)} %multiply_add_fusion), kind=kOutput, calls=%fused_computation | convolution fusion | flops 4314890240 | bytes 23068672 | tf_op jit(solution)/shard_map/dot_general | solution.py:497
  487.3 11.1 %convolution_convert_fusion.2 = bf16[4096,1024]{1,0:T(8,128)(2,1)} fusion(f32[512,1024]{1,0:T(8,128)S(1)} %multiply_add_fusion, f32[512,4096]{1,0:T(8,128)} %fusion.85), kind=kOutput, calls=%fused_computation.8 | convolution fusion | flops 4310695936 | bytes 18874368 | tf_op jit(solution)/shard_map/dot_general | solution.py:501
  498.5 8.0 convolution_convert_fusion.4
  506.6 6.4 fusion.37
  514.2 3.6 fusion.41
  517.8 6.9 convolution_convert_fusion.3
  524.7 291.1 %shard_map.283 = (bf16[2,2,2,32,4096]{4,3,2,1,0:T(8,128)(2,1)}, bf16[2,2,2,128,1024]{4,3,2,1,0:T(8,128)(2,1)}, bf16[2,2,2,32,3072]{4,3,2,1,0:T(8,128)(2,1)}, bf1...) custom-call(bf16[4,2,2,2,32,4096]{5,4,3,2,1,0:T(8,128)(2,1)} %bitcas, ...), custom_call_target="tpu_custom_call" | custom-call | bytes 150994944 | tf_op jit(solution)/shard_map/pallas_call | solution.py:424
  819.0 2.8 bitcast_convert_fusion.6
  825.3 1.6 bitcast_convert_fusion.5
  827.0 2.1 bitcast_convert_fusion.4
  829.1 2.6 bitcast_convert_fusion.3
  831.7 2.6 bitcast_convert_fusion.2
  834.4 2.6 bitcast_convert_fusion.1
  837.0 2.6 bitcast_convert_fusion
  (284 shorter events, 36.0 us)
Async XLA Ops:
  239.5 9.3 %copy-start.15 = (bf16[4,4,2,32,4096]{4,3,2,1,0:T(8,128)(2,1)}, bf16[4,4,2,32,4096]{4,3,2,1,0:T(8,128)(2,1)S(1)}, u32[]{:S(2)}) copy-start(bf16[4,4,2,32,4096]{4,3,2,1,0:T(8,128)(2,1)S(1)} %get-tuple-element.49) | copy-start | bytes 25165828
  239.5 9.3 %copy-start.1 = (bf16[2,256,1024]{2,1,0:T(8,128)(2,1)}, bf16[2,256,1024]{2,1,0:T(8,128)(2,1)S(1)}, u32[]{:S(2)}) copy-start(bf16[2,256,1024]{2,1,0:T(8,128)(2,1)S(1)} %get-tuple-element.47) | copy-start | bytes 3145732
  239.5 9.3 %copy-start.16 = (bf16[4,4,2,128,1024]{4,3,2,1,0:T(8,128)(2,1)}, bf16[4,4,2,128,1024]{4,3,2,1,0:T(8,128)(2,1)S(1)}, u32[]{:S(2)}) copy-start(bf16[4,4,2,128,1024]{4,3,2,1,0:T(8,128)(2,1)S(1)} %get-tuple-element.50) | copy-start | bytes 25165828
  239.5 18.0 %copy-start.17 = (bf16[4,4,2,32,3072]{4,3,2,1,0:T(8,128)(2,1)}, bf16[4,4,2,32,3072]{4,3,2,1,0:T(8,128)(2,1)S(1)}, u32[]{:S(2)}) copy-start(bf16[4,4,2,32,3072]{4,3,2,1,0:T(8,128)(2,1)S(1)} %get-tuple-element.51) | copy-start | bytes 18874372
  239.6 9.2 %copy-start.60 = (f32[1,4,256]{2,0,1:T(1,128)}, f32[1,4,256]{2,0,1:T(1,128)S(1)}, u32[]{:S(2)}) copy-start(f32[1,4,256]{2,0,1:T(1,128)S(1)} %get-tuple-element.138) | copy-start | bytes 12292
  239.6 9.2 %copy-start.62 = (f32[1,4,256]{2,0,1:T(1,128)}, f32[1,4,256]{2,0,1:T(1,128)S(1)}, u32[]{:S(2)}) copy-start(f32[1,4,256]{2,0,1:T(1,128)S(1)} %get-tuple-element.139) | copy-start | bytes 12292
  239.6 17.9 %copy-start.66 = (f32[1,4,256]{2,0,1:T(1,128)}, f32[1,4,256]{2,0,1:T(1,128)S(1)}, u32[]{:S(2)}) copy-start(f32[1,4,256]{2,0,1:T(1,128)S(1)} %get-tuple-element.137) | copy-start | bytes 12292
  239.6 17.9 %copy-start.73 = (f32[1,4,256]{2,0,1:T(1,128)}, f32[1,4,256]{2,0,1:T(1,128)S(1)}, u32[]{:S(2)}) copy-start(f32[1,4,256]{2,0,1:T(1,128)S(1)} %get-tuple-element.136) | copy-start | bytes 12292
  239.6 63.4 %copy-start.75 = (f32[1,4,256]{2,0,1:T(1,128)}, f32[1,4,256]{2,0,1:T(1,128)S(1)}, u32[]{:S(2)}) copy-start(f32[1,4,256]{2,0,1:T(1,128)S(1)} %get-tuple-element.133) | copy-start | bytes 12292
  257.1 4.4 copy-start.35
  257.1 4.4 copy-start.64
  257.5 4.1 copy-start.69
  261.6 2.7 copy-start.78
  263.9 16.4 %collective-permute-start = (bf16[512,2048]{1,0:T(8,128)(2,1)}, bf16[512,2048]{1,0:T(8,128)(2,1)S(1)}, u32[]{:S(2)}, u32[]{:S(2)}) collective-permute-start(bf16[512,2048]{1,0:T(8,128)(2,1)} %slice.265), channel_id=1, source_target_pairs={{0,4},{4,0},{8,12},{12,8},{16,20},{20,16},{24,28},{28,24},{1,5},{5... | collective-permute-start | bytes 6291464 | tf_op jit(solution)/shard_map/ppermute | solution.py:506
  266.2 4.6 copy-start.77
  275.4 5.0 copy-start.40
  280.4 20.9 %copy-start.22 = (bf16[4,4,2,32,1024]{4,3,2,1,0:T(8,128)(2,1)S(1)}, bf16[4,4,2,32,1024]{4,3,2,1,0:T(8,128)(2,1)}, u32[]{:S(2)}) copy-start(bf16[4,4,2,32,1024]{4,3,2,1,0:T(8,128)(2,1)} %copy-done.21) | copy-start | bytes 6291460
  280.4 20.9 %copy-start.36 = (f32[512,1024]{1,0:T(8,128)S(1)}, f32[512,1024]{1,0:T(8,128)}, u32[]{:S(2)}) copy-start(f32[512,1024]{1,0:T(8,128)} %copy-done.35) | copy-start | bytes 6291460
  280.4 20.9 %copy-start = (bf16[512,2048]{1,0:T(8,128)(2,1)}, bf16[512,2048]{1,0:T(8,128)(2,1)S(1)}, u32[]{:S(2)}) copy-start(bf16[512,2048]{1,0:T(8,128)(2,1)S(1)} %collective-permute-done.ko_ref.vo_ref) | copy-start | bytes 6291460
  301.3 3.2 copy-start.19
  302.6 4.3 copy-start.38
  309.0 2.1 collective-permute-start.1
  313.4 3.5 slice-start.7
  313.4 10.5 %slice-start.8 = ((s8[8388608]{0:T(1024)(128)(4,1)}), s8[4194304]{0:T(1024)(128)(4,1)S(1)}, s32[]{:S(2)}) async-start(s8[8388608]{0:T(1024)(128)(4,1)} %bitcast.353), calls=%async_computation.8 | async-start | bytes 8388608
  315.0 8.9 %slice-start.9 = ((s8[8388608]{0:T(1024)(128)(4,1)}), s8[4194304]{0:T(1024)(128)(4,1)S(1)}, s32[]{:S(2)}) async-start(s8[8388608]{0:T(1024)(128)(4,1)} %bitcast.353), calls=%async_computation.9 | async-start | bytes 8388608
  368.5 3.0 copy-start.81
  378.8 10.8 %copy-start.30 = (f32[512,2048]{1,0:T(8,128)S(1)}, f32[512,2048]{1,0:T(8,128)}, u32[]{:S(2)}) copy-start(f32[512,2048]{1,0:T(8,128)} %copy-done.29) | copy-start | bytes 12582916
  382.6 7.0 collective-permute-start.4
  384.2 79.5 %collective-permute-start.2 = (bf16[256,1024]{1,0:T(8,128)(2,1)}, bf16[256,1024]{1,0:T(8,128)(2,1)}, u32[]{:S(2)}, u32[]{:S(2)}) collective-permute-start(bf16[256,1024]{1,0:T(8,128)(2,1)} %get-tuple-element.121), channel_id=1, source_target_pairs={{0,0},{1,1},{2,4},{3,5},{4,2},{5,3},{6,6},{7,7},{8,8},{9,9},{10,12... | collective-permute-start | bytes 1572872 | tf_op jit(solution)/shard_map/ppermute | solution.py:521
  389.6 74.1 %collective-permute-start.3 = (bf16[256,1024]{1,0:T(8,128)(2,1)}, bf16[256,1024]{1,0:T(8,128)(2,1)}, u32[]{:S(2)}, u32[]{:S(2)}) collective-permute-start(bf16[256,1024]{1,0:T(8,128)(2,1)} %get-tuple-element.122), channel_id=1, source_target_pairs={{0,1},{1,0},{2,5},{3,4},{4,3},{5,2},{6,7},{7,6},{8,9},{9,8},{10,13... | collective-permute-start | bytes 1572872 | tf_op jit(solution)/shard_map/ppermute | solution.py:522
  392.7 2.9 copy-start.20
  393.6 5.0 copy-start.52
  400.2 45.4 %copy-start.31 = (f32[512,1024]{1,0:T(8,128)}, f32[512,1024]{1,0:T(8,128)S(1)}, u32[]{:S(2)}) copy-start(f32[512,1024]{1,0:T(8,128)S(1)} %multiply_add_fusion.1) | copy-start | bytes 6291460
  437.5 28.7 %collective-permute-start.5 = (bf16[512,2048]{1,0:T(8,128)(2,1)}, bf16[512,2048]{1,0:T(8,128)(2,1)}, u32[]{:S(2)}, u32[]{:S(2)}) collective-permute-start(bf16[512,2048]{1,0:T(8,128)(2,1)} %pad_maximum_fusion.2), channel_id=1, source_target_pairs={{0,4},{4,0},{8,12},{12,8},{16,20},{20,16},{24,28},{28,24},{1,5},{5... | collective-permute-start | bytes 6291464 | tf_op jit(solution)/shard_map/ppermute | solution.py:506
  438.7 7.0 copy-start.27
  448.3 20.6 %slice-start.4 = ((s8[6291456]{0:T(1024)(128)(4,1)}), s8[2097152]{0:T(1024)(128)(4,1)S(1)}, s32[]{:S(2)}) async-start(s8[6291456]{0:T(1024)(128)(4,1)} %bitcast.245), calls=%async_computation.4 | async-start | bytes 4194304
  452.4 4.4 copy-start.76
  456.8 12.1 %slice-start.5 = ((s8[6291456]{0:T(1024)(128)(4,1)}), s8[4194304]{0:T(1024)(128)(4,1)S(1)}, s32[]{:S(2)}) async-start(s8[6291456]{0:T(1024)(128)(4,1)} %bitcast.245), calls=%async_computation.5 | async-start | bytes 8388608
  466.3 2.7 copy-start.67
  466.3 2.7 copy-start.70
  466.3 10.2 %slice-start.2 = ((s8[8388608]{0:T(1024)(128)(4,1)}), s8[4194304]{0:T(1024)(128)(4,1)S(1)}, s32[]{:S(2)}) async-start(s8[8388608]{0:T(1024)(128)(4,1)} %bitcast.241), calls=%async_computation.2 | async-start | bytes 8388608
  468.9 5.3 copy-start.53
  468.9 5.2 copy-start.55
  469.0 5.2 copy-start.32
  469.0 7.5 slice-start.3
  476.5 10.8 %copy-start.33 = (f32[512,1024]{1,0:T(8,128)}, f32[512,1024]{1,0:T(8,128)S(1)}, u32[]{:S(2)}) copy-start(f32[512,1024]{1,0:T(8,128)S(1)} %multiply_add_fusion) | copy-start | bytes 6291460
  476.5 30.0 %slice-start = ((s8[8388608]{0:T(1024)(128)(4,1)}), s8[4194304]{0:T(1024)(128)(4,1)S(1)}, s32[]{:S(2)}) async-start(s8[8388608]{0:T(1024)(128)(4,1)} %bitcast.237), calls=%async_computation | async-start | bytes 8388608
  487.3 11.1 %copy-start.54 = (bf16[512,1024]{1,0:T(8,128)(2,1)S(1)}, bf16[512,1024]{1,0:T(8,128)(2,1)}, u32[]{:S(2)}) copy-start(bf16[512,1024]{1,0:T(8,128)(2,1)} %copy-done.53) | copy-start | bytes 3145732
  487.3 11.1 %copy-start.56 = (bf16[512,1024]{1,0:T(8,128)(2,1)S(1)}, bf16[512,1024]{1,0:T(8,128)(2,1)}, u32[]{:S(2)}) copy-start(bf16[512,1024]{1,0:T(8,128)(2,1)} %copy-done.55) | copy-start | bytes 3145732
  487.3 11.1 %copy-start.74 = (f32[1,4,256]{2,0,1:T(1,128)S(1)}, f32[1,4,256]{2,0,1:T(1,128)}, u32[]{:S(2)}) copy-start(f32[1,4,256]{2,0,1:T(1,128)} %copy-done.73) | copy-start | bytes 12292
  487.3 19.2 %slice-start.1 = ((s8[8388608]{0:T(1024)(128)(4,1)}), s8[4194304]{0:T(1024)(128)(4,1)S(1)}, s32[]{:S(2)}) async-start(s8[8388608]{0:T(1024)(128)(4,1)} %bitcast.237), calls=%async_computation.1 | async-start | bytes 8388608
  498.4 8.1 copy-start.2
  498.4 8.1 copy-start.63
  498.5 8.1 copy-start.71
  498.5 8.1 copy-start.72
  498.5 8.1 copy-start.79
  506.6 6.5 copy-start.68
  506.6 7.5 copy-start.34
  506.6 7.5 copy-start.61
  514.2 3.6 copy-start.80
  815.8 6.1 copy-start.59
  819.0 4.1 copy-start.58
  821.8 3.5 copy-start.51
  824.2 2.8 copy-start.49
  (34 other events, 63.3 us)

commit v3 on v1

v3 whole, which is shorter than its diff:
```python
import functools
import math

import jax
import jax.numpy as jnp
from jax import lax
from jax.experimental import pallas as pl
from jax.experimental.pallas import tpu as pltpu
from jax.sharding import PartitionSpec as P

D = 1024
KERNEL = 5
EPSILON = 1e-05
MESH=pl.DeviceIdType.MESH

def place():
    dp=lax.axis_index("dp"); z=lax.axis_index("seq")
    c=dp%2; p=(dp//2)%4
    bx=p%2; by=p//2
    return dict(dp=dp,z=z,c=c,p=p,px=p+1-2*bx,py=p+2-4*by,
                core=dp+1-2*c, xn=dp+2-4*bx, yn=dp+4-8*by)

def rows_norm(value, gain, offset):
    centred=value-jnp.mean(value,axis=-1,keepdims=True)
    return centred*lax.rsqrt(jnp.mean(centred*centred,axis=-1,keepdims=True)+EPSILON)*gain+offset

def gather_kernel(items, order, nw, nz, *refs):
    ni=len(items)
    refs=list(refs)
    take=lambda m: [refs.pop(0) for _ in range(m)]
    ins=take(nw); vecs=take(4); fr,ct,length,lead,quarter,fine_c,fine_s=take(7)
    outs=take(nw); small_o,fr_o,ct_o,h1_o,a1_o,s1_o,x1_o,ha_o,qkv_o,kvo_o,pe_o,pt_o,p_o,at_o=take(14)
    stage=take(nw)
    x0,sv,h1,acc,ha,qkv,kvo,pe,pt,at,w1b,w2b,ab,sb,wqb,wpb,pb,x1b,small,small_f=take(20)
    (zr,xr,yr,ar,br,cr,zsr,zsl,xs,ys,as_,bs,cs,loc,lod,fs,frv,one_sem,in_sem,out_sem,kv_s,kv_r)=refs
    k=place(); dp,z,c,p=k["dp"],k["z"],k["c"],k["p"]
    here=lambda zz:(dp,zz)
    tcore=z//2; tdp=dp-c+tcore
    small_f[...]=jnp.zeros_like(small_f)
    row=0
    for part in vecs:
        small_f[row:row+part.shape[0],:]=part[...].astype(jnp.float32); row+=part.shape[0]
    small[...]=small_f[...].astype(jnp.bfloat16)
    bar=pltpu.get_barrier_semaphore()
    def sig(dev): pl.semaphore_signal(bar,inc=1,device_id=dev,device_id_type=MESH)
    for n in ("core","xn","yn"): sig((k[n],z))
    for ok,zz in ((z>0,z-1),(z<nz-1,z+1)):
        @pl.when(ok)
        def _(): sig((dp,zz))
    for u in range(2):
        @pl.when(jnp.logical_or(tcore!=c, 2*c+u!=z))
        def _(): sig((tdp,2*c+u))
    one=lambda b: jnp.where(b,1,0)
    pl.semaphore_wait(bar,3+one(z>0)+one(z<nz-1)+2-one(tcore==c))
    def rc(src,dst,s,r,dev):
        return pltpu.make_async_remote_copy(src_ref=src,dst_ref=dst,send_sem=s,recv_sem=r,device_id=dev,device_id_type=MESH)
    allin=list(ins)+[small]; allout=list(outs)+[small_o]
    def piece(i,t,pp=None,half=None):
        if i==ni: return small_o.at[t]
        w,r0,q,c0,cc=items[i]
        if half is not None: q=q//2; r0=r0+half*q
        return outs[w].at[t,p if pp is None else pp,c,pl.ds(r0,q),pl.ds(c0,cc)]
    def own(i):
        if i==ni: return small
        w,r0,q,c0,cc=items[i]
        return ins[w].at[p,c,pl.ds(r0,q),pl.ds(c0,cc)]
    def zright(w,t,src=None): return rc(piece(w,t) if src is None else src,piece(w,t),zsr.at[w,t],zr.at[w,t],(dp,z+1))
    def zleft(w,t,src=None): return rc(piece(w,t) if src is None else src,piece(w,t),zsl.at[w,t],zr.at[w,t],(dp,z-1))
    def xsend(w,t): return rc(piece(w,t),piece(w,t),xs.at[w,t],xr.at[w,t],(k["xn"],z))
    def ysend(w,t): return rc(piece(w,t),piece(w,t),ys.at[w,t],yr.at[w,t],(k["yn"],z))
    def asend(w,t): return rc(piece(w,t,k["px"],0),piece(w,t,k["px"],0),as_.at[w,t],ar.at[w,t],(k["yn"],z))
    def bsend(w,t): return rc(piece(w,t,k["py"],1),piece(w,t,k["py"],1),bs.at[w,t],br.at[w,t],(k["xn"],z))
    def csend(i,t):
        w,r0,q,c0,cc=items[i]
        four=outs[w].at[t,:,c,pl.ds(r0,q),pl.ds(c0,cc)]
        return rc(four,four,cs.at[i,t],cr.at[i,t],(k["core"],z))
    def load(w): return pltpu.make_async_copy(allin[w],stage[w],lod.at[w])
    from_vmem=lambda w: small if w==nw else stage[w]
    def local(w): return pltpu.make_async_copy(from_vmem(w),allout[w].at[z],loc.at[w])
    redo=[(fr,fr_o,0),(ct,ct_o,1)]
    def move(a,u):
        s,d,i=redo[a]
        return rc(s.at[u],d.at[z%2],fs.at[i,u],frv.at[i,z%2],(tdp,2*c+u))
    def keep(a):
        s,d,i=redo[a]
        return pltpu.make_async_copy(s.at[z%2],d.at[z%2],loc.at[nw+1+i])
    def moves(a,f_remote,f_local):
        for u in range(2):
            @pl.when(jnp.logical_or(tcore!=c,2*c+u!=z))
            def _(): f_remote(a,u)
        @pl.when(tcore==c)
        def _(): f_local(a)
    def away(f):
        for d in range(1,nz):
            @pl.when(z-d>=0)
            def _(): f(z-d,True)
            @pl.when(z+d<nz)
            def _(): f(z+d,False)
    moves(0,lambda a,u:move(a,u).start(),lambda a:keep(a).start())
    def go(w):
        @pl.when(z<nz-1)
        def _(): zright(w,z,own(w)).start()
        @pl.when(z>0)
        def _(): zleft(w,z,own(w)).start()
    def f1(w,t,fromleft):
        zright(w,t).wait_recv()
        if fromleft:
            @pl.when(z<nz-1)
            def _(): zright(w,t).start()
        else:
            @pl.when(z>0)
            def _(): zleft(w,t).start()
        if w<ni:
            xsend(w,t).start(); ysend(w,t).start()
    def f2(w,t,_):
        xsend(w,t).wait_recv(); asend(w,t).start()
        ysend(w,t).wait_recv(); bsend(w,t).start()
    def f3(w,t,_):
        asend(w,t).wait_recv(); bsend(w,t).wait_recv(); csend(w,t).start()
    def at_(f,w,d):
        @pl.when(z-d>=0)
        def _(): f(w,z-d,True)
        @pl.when(z+d<nz)
        def _(): f(w,z+d,False)
    def arrived(i):
        for d in range(1,nz): at_(lambda i,t,_: csend(i,t).wait_recv(),i,d)
    got=set(); laid=set()
    def ensure(w):
        for i in range(ni):
            if items[i][0]==w: arrived(i); got.add(i)
        local(w).wait(); laid.add(w)
    rows=x0.shape[0]; quarter_rows=rows//4
    def landed(a):
        for pos in range(2):
            @pl.when(jnp.logical_or(tcore!=c,2*c+pos!=z))
            def _():
                s,d,i=redo[a]
                rc(s.at[pos],d.at[pos],fs.at[i,pos],frv.at[i,pos],(tdp,2*c+pos)).wait_recv()
        @pl.when(tcore==c)
        def _(): keep(a).wait()
    vec=lambda r: jnp.concatenate([sv[t,r:r+1,:] for t in range(nz)],axis=1).astype(jnp.float32)
    def copy_now(src,dst,sem):
        cp=pltpu.make_async_copy(src,dst,sem); cp.start(); return cp
    pending=[]
    def store(src,dst,key):
        pending.append(copy_now(src,dst,out_sem.at[key]))
    def u_norm0():
        landed(0); local(nw).wait(); laid.add(nw)
        cps=[copy_now(fr_o.at[j],x0.at[pl.ds(j*rows//2,rows//2)],one_sem.at[j]) for j in range(2)]+[copy_now(small_o,sv,one_sem.at[2])]
        for cp in cps: cp.wait()
        gain,off=vec(0),vec(6)
        def f(j):
            at_rows=pl.ds(pl.multiple_of(j*quarter_rows,quarter_rows),quarter_rows)
            h1[at_rows,:]=rows_norm(x0[at_rows,:].astype(jnp.float32),gain,off).astype(jnp.bfloat16)
        loop(4,f)
        acc[...]=jnp.zeros_like(acc)
        store(h1,h1_o,0)
    def u_table():
        n_fine=fine_c.shape[0]
        def f(j):
            row=pl.ds(j,1)
            block=lead[row,:]*fine_c[...]-quarter[row,:]*fine_s[...]
            pe[pl.ds(pl.multiple_of(j*n_fine,n_fine),n_fine),:]=block.astype(jnp.bfloat16)
        loop(lead.shape[0],f)
        store(pe,pe_o,1)
    def u_ptab(t):
        if t==0: ensure(3)
        copy_now(outs[3].at[t],wpb,one_sem.at[0]).wait()
        width=wpb.shape[3]
        pt[:,width*t:width*t+width]=mmv(pe[...],wpb[...].reshape(-1,width)).astype(jnp.bfloat16)
        if t==nz-1: store(pt,pt_o,2)
    mmv=lambda l,r: jnp.dot(l,r,preferred_element_type=jnp.float32)
    fcols=w1b.shape[-1]; nf=outs[0].shape[-1]//fcols
    per_z=outs[1].shape[3]*8; zb_rows=per_z//fcols
    lows=4//zb_rows
    a_load=lambda j: copy_now(outs[0].at[:,:,:,:,pl.ds(j*fcols,fcols)],w1b.at[j%2],in_sem.at[0,j%2])
    b_load=lambda j: copy_now(outs[1].at[j//zb_rows,pl.ds(j%zb_rows*lows,lows)],w2b.at[j%2],in_sem.at[1,j%2])
    flight={}
    def u_expand(j):
        if j==0:
            ensure(0); flight["a",0]=a_load(0)
        if j+1<nf: flight["a",j+1]=a_load(j+1)
        flight.pop(("a",j)).wait()
        if j>=2: flight.pop(("o",j-2)).wait()
        hidden=mmv(h1[...],w1b[j%2].reshape(-1,fcols))
        ab[j%2]=hidden
        cols=pl.ds(j*fcols,fcols)
        sb[:,cols]=(hidden*jax.nn.sigmoid(hidden)).astype(jnp.bfloat16)
        flight["o",j]=copy_now(ab.at[j%2],a1_o.at[:,cols],out_sem.at[3+j%2])
        if j==nf-1:
            pending.extend((flight.pop(("o",j-1)),flight.pop(("o",j))))
            store(sb,s1_o,5)
    def u_shrink(j):
        if j==0:
            ensure(1); flight["b",0]=b_load(0)
        if j+1<nf: flight["b",j+1]=b_load(j+1)
        flight.pop(("b",j)).wait()
        acc[...]+=mmv(sb[:,j*fcols:j*fcols+fcols],w2b[j%2].reshape(fcols,-1))
    def u_norm1():
        gain,off=vec(1),vec(7)
        def f(j):
            at_rows=pl.ds(pl.multiple_of(j*quarter_rows,quarter_rows),quarter_rows)
            mid=x0[at_rows,:].astype(jnp.float32)+0.5*acc[at_rows,:]
            acc[at_rows,:]=mid
            ha[at_rows,:]=rows_norm(mid,gain,off).astype(jnp.bfloat16)
        loop(4,f)
        store(acc,x1_o,7); store(ha,ha_o,8)
    qcols=wqb.shape[-1]; nq=outs[2].shape[-1]//qcols
    q_load=lambda j: copy_now(outs[2].at[:,:,:,:,pl.ds(j*qcols,qcols)],wqb.at[j%2],in_sem.at[2,j%2])
    def u_qkv(j):
        if j==0:
            ensure(2); flight["q",0]=q_load(0)
        if j+1<nq: flight["q",j+1]=q_load(j+1)
        flight.pop(("q",j)).wait()
        qkv[:,j*qcols:j*qcols+qcols]=mmv(ha[...],wqb[j%2].reshape(-1,qcols)).astype(jnp.bfloat16)
        if j==nq-1:
            store(qkv,qkv_o,9)
            swap_kv().start()
    dim=x0.shape[1]
    swap_kv=lambda: rc(qkv.at[:,pl.ds(dim,2*dim)],kvo,kv_s.at[0],kv_r.at[0],(k["core"],z))
    def u_head(h):
        if h==0:
            swap_kv().wait()
            store(kvo,kvo_o,10)
        if h>=2: flight.pop(("p",h-2)).wait()
        col=lambda off: pl.ds(off+h*HD,HD)
        attn_head(c==0,length[0],qkv[:,col(0)],qkv[:,col(dim)],qkv[:,col(2*dim)],kvo[:,col(0)],kvo[:,col(dim)],
            pt.at[:,col(0)],pairv[0:2,col(0)],at.at[:,col(0)],pb.at[h%2])
        flight["p",h]=copy_now(pb.at[h%2],p_o.at[h],out_sem.at[11+h%2])
        if h==heads-1:
            store(at,at_o,13)
            pending.extend((flight.pop(("p",h-1)),flight.pop(("p",h))))
    pairv=x1b
    def u_pair():
        pairv[0:1,:]=vec(17); pairv[1:2,:]=vec(18)
    def loop(m,f):
        lax.fori_loop(0,m,lambda j,_: (f(j),0)[1],0)
    last_item=lambda w: max(i for i in range(ni) if items[i][0]==w)
    heads=at.shape[1]//HD
    ready=lambda w: last_item(w)+nz+SLACK
    units=[(nz-1,2,u_norm0),(0,0,u_pair),(0,4,u_table)]
    units+=[(ready(3),1.5,functools.partial(u_ptab,t)) for t in range(nz)]
    units+=[(ready(0),1,functools.partial(u_expand,j)) for j in range(nf)]
    units+=[(ready(1),1,functools.partial(u_shrink,j)) for j in range(nf)]+[(0,2,u_norm1)]
    units+=[(ready(2),1,functools.partial(u_qkv,j)) for j in range(nq)]
    units+=[(ready(2)+2,2.5,functools.partial(u_head,h)) for h in range(heads)]
    def run(s,budget):
        while budget>0 and units and units[0][0]<=s:
            _,cost,unit=units.pop(0)
            unit(); budget-=cost
    go(ni)
    for w in range(AHEAD): go(w)
    for w in order: load(w).start()
    local(nw).start()
    for s in range(ni+nz):
        if s<nw:
            load(order[s]).wait(); local(order[s]).start()
        if s+AHEAD<ni: go(s+AHEAD)
        if s<nz-1: at_(f1,ni,s+1)
        if s==ni//2: moves(1,lambda a,u:move(a,u).start(),lambda a:keep(a).start())
        for f,late in ((f3,1),(f2,0),(f1,-1)):
            for d in range(1,nz):
                if 0<=s-d-late<ni: at_(f,s-d-late,d)
            run(s,BUDGET)
    run(10**6,10**6)
    for cp in pending: cp.wait()
    def away(f):
        for d in range(1,nz):
            @pl.when(z-d>=0)
            def _(): f(z-d,True)
            @pl.when(z+d<nz)
            def _(): f(z+d,False)
    for w in range(nw+1):
        if w not in laid: local(w).wait()
    for w in range(ni+1):
        @pl.when(z<nz-1)
        def _(): zright(w,z,own(w)).wait_send()
        @pl.when(z>0)
        def _(): zleft(w,z,own(w)).wait_send()
        def f(t,fromleft):
            if fromleft:
                @pl.when(z<nz-1)
                def _(): zright(w,t).wait_send()
            else:
                @pl.when(z>0)
                def _(): zleft(w,t).wait_send()
            if w<ni:
                for g in (xsend,ysend,asend,bsend,csend): g(w,t).wait_send()
                if w not in got: csend(w,t).wait_recv()
        away(f)
    for a in range(2):
        moves(a,lambda a,u:move(a,u).wait_send(),lambda a:None)
    landed(1)

ITEM=2**21
BUDGET=2.0
SLACK=1
AHEAD=1
def gather(ws,vecs,fr,ct,length,tables,nz,cid=0):
    nw=len(ws); bf=jnp.bfloat16; f32=jnp.float32
    small=jax.ShapeDtypeStruct((32,vecs[0].shape[1]),bf)
    ins=[w.reshape(4,2,w.shape[0]//8,w.shape[1]) for w in ws]
    order=[3,0,1,2]+list(range(4,nw))
    items=[]
    for w in order:
        q,cc=ins[w].shape[2:]
        parts=max(1,nz*8*q*cc//ITEM)
        for j in range(parts): items.append((w,0,q,j*cc//parts,cc//parts) if q<64 else (w,j*q//parts,q//parts,0,cc))
    ni=len(items)
    rows=2*fr.shape[1]; dim=fr.shape[2]; ff=ws[0].shape[1]; heads=dim//HD; wide=ws[3].shape[1]
    any_=pl.BlockSpec(memory_space=pl.ANY); vm=pl.BlockSpec(memory_space=pltpu.VMEM); sm=pl.BlockSpec(memory_space=pltpu.SMEM)
    sd=jax.ShapeDtypeStruct; V=pltpu.VMEM
    shp=[sd((nz,)+w.shape,w.dtype) for w in ins]+[sd((nz,)+small.shape,small.dtype),sd(fr.shape,fr.dtype),sd(ct.shape,ct.dtype)]
    shp+=[sd((rows,dim),bf),sd((rows,ff),f32),sd((rows,ff),bf),sd((rows,dim),f32),sd((rows,dim),bf),sd((rows,3*dim),bf),sd((rows,2*dim),bf),
        sd((3*rows,dim),bf),sd((3*rows,dim),bf),sd((heads,rows,2*rows),bf),sd((rows,dim),bf)]
    S=pltpu.SemaphoreType.DMA
    cut=512
    q0=ins[0].shape[2]; q2=ins[1].shape[2]
    scratch=[V(w.shape,w.dtype) for w in ins]
    scratch+=[V((rows,dim),bf),V((nz,)+small.shape,bf),V((rows,dim),bf),V((rows,dim),f32),V((rows,dim),bf),V((rows,3*dim),bf),V((rows,2*dim),bf),
        V((3*rows,dim),bf),V((3*rows,dim),bf),V((rows,dim),bf),
        V((2,nz,4,2,q0,cut),bf),V((2,cut//(2*q2),2,q2,dim),bf),V((2,rows,cut),f32),V((rows,ff),bf),V((2,nz,4,2,q0,cut),bf),V((4,2,ins[3].shape[2],wide),bf),
        V((2,rows,2*rows),bf),V((8,dim),f32),V(small.shape,bf),V(small.shape,f32)]
    scratch+=[S((ni+1,nz))]+[S((ni,nz))]*5+[S((ni+1,nz))]*2+[S((ni,nz))]*5+[S((nw+3,)),S((nw,)),S((2,2)),S((2,2)),S((3,)),S((3,2)),S((14,)),S((1,)),S((1,))]
    o=pl.pallas_call(functools.partial(gather_kernel,items,order,nw,nz),out_shape=shp,
        in_specs=[any_]*nw+[vm]*4+[any_]*2+[sm]+[vm]*4,out_specs=[any_]*len(shp),
        scratch_shapes=scratch,
        compiler_params=pltpu.CompilerParams(collective_id=cid,has_side_effects=True,vmem_limit_bytes=60*2**20),
        cost_estimate=pl.CostEstimate(flops=25*10**9,bytes_accessed=2*48*2**20,transcendentals=0),
    )(*ins,*vecs,fr,ct,length,*tables)
    full=[x.reshape(nz*w.shape[0],w.shape[1]) for x,w in zip(o[:nw],ws)]
    return full,o[nw],o[nw+1],o[nw+2],o[nw+3:]

HD=128; SCALE=1.0/math.sqrt(128)
BLK=256
NT=(((1,),(1,)),((),()))
TN=(((0,),(0,)),((),()))
def dot(a,b,dims=(((1,),(0,)),((),()))):
    return lax.dot_general(a,b,dims,preferred_element_type=jnp.float32)

def order(first, own, oth):
    return jnp.concatenate([jnp.where(first, own, oth), jnp.where(first, oth, own)], axis=0)

def attn_head(first,length,q,k,v,ko,vo,pt_ref,pb,o_ref,p_ref):
    T=q.shape[0]; L2=2*T
    q=q.astype(jnp.float32)
    qu=(q+pb[0:1]).astype(jnp.bfloat16); qv=(q+pb[1:2]).astype(jnp.bfloat16)
    k=order(first,k,ko); v=order(first,v,vo)
    W=BLK+L2
    keep=lax.broadcasted_iota(jnp.int32,(BLK,L2),1)<length
    for b in range(T//BLK):
        i0=b*BLK; w0=T-i0-BLK
        s=dot(qu[i0:i0+BLK],k,NT)
        placed=dot(qv[i0:i0+BLK],pt_ref[w0:w0+W,:],NT)
        s=s+pltpu.roll(placed,W-(BLK-1),1,stride=1,stride_axis=0)[:,:L2]
        s=jnp.where(keep,s*SCALE,-1e9)
        m=jnp.max(s,axis=-1,keepdims=True)
        e=jnp.exp(s-m)
        p=(e*(1.0/jnp.sum(e,axis=-1,keepdims=True))).astype(jnp.bfloat16)
        p_ref[i0:i0+BLK,:]=p
        o_ref[i0:i0+BLK,:]=dot(p,v).astype(jnp.bfloat16)

def attn_bwd_kernel(sc_ref, q_ref, k_ref, v_ref, ko_ref, vo_ref, pt_ref, pb_ref, g_ref, at_ref, p_ref,
                    gq_ref, gk_ref, gv_ref, gko_ref, gvo_ref, gpt_ref, gb_ref, gpt_acc):
    T=q_ref.shape[0]; L2=2*T
    first=sc_ref[0]==0
    q=q_ref[...].astype(jnp.float32)
    pb=pb_ref[...].astype(jnp.float32)
    qu=(q+pb[0:1]).astype(jnp.bfloat16); qv=(q+pb[1:2]).astype(jnp.bfloat16)
    k=order(first,k_ref[...],ko_ref[...]); v=order(first,v_ref[...],vo_ref[...])
    W=BLK+L2
    flip=(lax.broadcasted_iota(jnp.int32,(BLK,BLK),0)+lax.broadcasted_iota(jnp.int32,(BLK,BLK),1)==BLK-1).astype(jnp.float32).astype(jnp.bfloat16)
    gpt_acc[...]=jnp.zeros_like(gpt_acc)
    gk=gv=None; su=sv=None
    low=lambda v: v.astype(jnp.bfloat16)
    for b in range(T//BLK):
        i0=b*BLK; w0=T-i0-BLK
        g0=g_ref[i0:i0+BLK,:]
        rows=jnp.concatenate([g0,qu[i0:i0+BLK],qv[i0:i0+BLK],p_ref[0,i0:i0+BLK,:]],axis=1)
        back=dot(flip,rows)
        g=low(back[:,:HD]); qur=low(back[:,HD:2*HD]); qvr=low(back[:,2*HD:3*HD]); p=back[:,3*HD:]
        pbf=low(p)
        delta=jnp.sum(g0.astype(jnp.float32)*at_ref[i0:i0+BLK,:].astype(jnp.float32),axis=-1,keepdims=True)
        delta=lax.dot_general(flip.astype(jnp.float32),jnp.broadcast_to(delta,(BLK,HD)),(((1,),(0,)),((),())),precision=lax.Precision.HIGHEST,preferred_element_type=jnp.float32)[:,:1]
        gr=p*((dot(g,v,NT)-delta)*SCALE)
        grb=low(gr)
        gvb=dot(pbf,g,TN); gkb=dot(grb,qur,TN)
        gv=gvb if gv is None else gv+gvb
        gk=gkb if gk is None else gk+gkb
        gqu=dot(grb,k)
        pad=jnp.concatenate([gr,jnp.zeros((BLK,BLK),jnp.float32)],axis=1)
        gp=low(pltpu.roll(pad,0,1,stride=1,stride_axis=0))
        gpt_acc[w0:w0+W,:]+=dot(gp,qvr,TN)
        gqv=dot(gp,pt_ref[w0:w0+W,:])
        gq_ref[i0:i0+BLK,:]=low(dot(flip,low(gqu+gqv)))
        a=jnp.sum(gqu,axis=0,keepdims=True); c=jnp.sum(gqv,axis=0,keepdims=True)
        su=a if su is None else su+a; sv=c if sv is None else sv+c
    gpt_ref[...]=gpt_acc[...].astype(jnp.bfloat16)
    gk_ref[...]=jnp.where(first,gk[:T],gk[T:]); gv_ref[...]=jnp.where(first,gv[:T],gv[T:])
    gko_ref[...]=jnp.where(first,gk[T:],gk[:T]).astype(jnp.bfloat16); gvo_ref[...]=jnp.where(first,gv[T:],gv[:T]).astype(jnp.bfloat16)
    gb_ref[...]=jnp.concatenate([su,sv,jnp.zeros((6,su.shape[1]),jnp.float32)],axis=0)

def col(rows,off=0): return pl.BlockSpec((rows,HD),lambda h,off=off:(0,h+off))
def attn_bwd(sc,qkv,kvo,pt,pb,g,at,p):
    T=qkv.shape[0]; D=qkv.shape[1]//3; H=D//HD
    f32=jnp.float32; bf=jnp.bfloat16
    return pl.pallas_call(attn_bwd_kernel,grid=(H,),
        in_specs=[pl.BlockSpec(memory_space=pltpu.SMEM),col(T),col(T,H),col(T,2*H),col(T),col(T,H),col(3*T),col(pb.shape[0]),col(T),col(T),pl.BlockSpec((1,T,2*T),lambda h:(h,0,0))],
        out_specs=[col(T)]*5+[col(3*T),col(8)],
        out_shape=[jax.ShapeDtypeStruct((T,D),bf),jax.ShapeDtypeStruct((T,D),f32),jax.ShapeDtypeStruct((T,D),f32),jax.ShapeDtypeStruct((T,D),bf),jax.ShapeDtypeStruct((T,D),bf),jax.ShapeDtypeStruct((3*T,D),bf),jax.ShapeDtypeStruct((8,D),f32)],
        scratch_shapes=[pltpu.VMEM((3*T,HD),f32)],
        compiler_params=pltpu.CompilerParams(vmem_limit_bytes=48*2**20),
        cost_estimate=pl.CostEstimate(flops=H*T*2*T*HD*2*6,bytes_accessed=30*2**20,transcendentals=0),
    )(sc,qkv,qkv,qkv,kvo,kvo,pt,pb,g,at,p)

def reduce_kernel(plan, zfirst, nz, nops, *refs):
    n=len(plan)
    refs=list(refs)
    take=lambda m: [refs.pop(0) for _ in range(m)]
    ops=take(nops); ready,small,gi=take(3)
    out,out_s,gi_o,far,far_s=take(5)
    tw,tsm,sw,ssm,cw,csm,ab,bb=take(8)
    x1=take(n); y1=take(n); x2=take(n); y2=take(n); zb=take(n)
    (cs,cr,x1s,x1r,y1s,y1r,x2s,x2r,y2s,y2r,axs,axr,ays,ayr,aas,aar,abs_,abr,acs,acr,zrs,zrr,zls,zlr,own,cld,loc,opsem,fs,frv,keeps)=refs
    k=place(); dp,z,c=k["dp"],k["z"],k["c"]
    bx=k["p"]%2; by=k["p"]//2
    tcore=z//2; tdp=dp-c+tcore
    bar=pltpu.get_barrier_semaphore()
    def sig(dev): pl.semaphore_signal(bar,inc=1,device_id=dev,device_id_type=MESH)
    for a in ("core","xn","yn"): sig((k[a],z))
    for ok,zz in ((z>0,z-1),(z<nz-1,z+1)):
        @pl.when(ok)
        def _(): sig((dp,zz))
    for u in range(2):
        @pl.when(jnp.logical_or(tcore!=c, 2*c+u!=z))
        def _(): sig((tdp,2*c+u))
    one=lambda b: jnp.where(b,1,0)
    pl.semaphore_wait(bar,3+one(z>0)+one(z<nz-1)+2-one(tcore==c))
    def rc(src,dst,s,r,dev):
        return pltpu.make_async_remote_copy(src_ref=src,dst_ref=dst,send_sem=s,recv_sem=r,device_id=dev,device_id_type=MESH)
    xn=(k["xn"],z); yn=(k["yn"],z); cn=(k["core"],z)
    nt=tw.shape[0]; nsnd=sw.shape[0]; nc=cw.shape[0]
    big=lambda i: len(plan[i])>0
    tb=lambda i: tw.at[i%nt] if big(i) else tsm
    sb=lambda i: sw.at[i%nsnd] if big(i) else ssm
    cb=lambda i: cw.at[i%nc] if big(i) else csm
    fb=lambda i: far.at[i] if big(i) else far_s
    ob=lambda i: out.at[i] if big(i) else out_s
    half=lambda i: 128 if big(i) else 16
    A=lambda i: pl.ds(0,half(i))
    B=lambda i: pl.ds(half(i),half(i))
    send_c=lambda i: rc(sb(i),fb(i),cs.at[i],cr.at[i],cn)
    load_c=lambda i: pltpu.make_async_copy(fb(i),cb(i),cld.at[i])
    zf=lambda i: i in zfirst
    def shard(i,r,*rest):
        return r.at[(z,)+rest] if zf(i) else r.at[(slice(None),)+rest]
    send_x1=lambda i: rc(shard(i,tb(i),slice(None),1-bx,A(i)),x1[i],x1s.at[i],x1r.at[i],xn)
    send_y1=lambda i: rc(shard(i,tb(i),1-by,slice(None),B(i)),y1[i],y1s.at[i],y1r.at[i],yn)
    send_x2=lambda i: rc(shard(i,tb(i),1-by,bx,A(i)),x2[i],x2s.at[i],x2r.at[i],yn)
    send_y2=lambda i: rc(shard(i,tb(i),by,1-bx,B(i)),y2[i],y2s.at[i],y2r.at[i],xn)
    line=lambda i,t: tb(i).at[t] if zf(i) else tb(i).at[t,by,bx]
    send_r=lambda i,t: rc(line(i,t),zb[i].at[t],zrs.at[i,t],zrr.at[i,t],(dp,z+1))
    send_l=lambda i,t,last: rc(line(i,t),zb[i].at[nz if last else t],zls.at[i,t],zlr.at[i,t],(dp,z-1))
    mine=lambda i: tb(i).at[z,by,bx]
    send_ax=lambda i: rc(mine(i),ob(i).at[by,bx,c],axs.at[i],axr.at[i],xn)
    send_ay=lambda i: rc(mine(i),ob(i).at[by,bx,c],ays.at[i],ayr.at[i],yn)
    keep_a=lambda i: pltpu.make_async_copy(mine(i),ob(i).at[by,bx,c],loc.at[i])
    send_aa=lambda i: rc(ob(i).at[by,1-bx,c,A(i)],ob(i).at[by,1-bx,c,A(i)],aas.at[i],aar.at[i],yn)
    send_ab=lambda i: rc(ob(i).at[1-by,bx,c,B(i)],ob(i).at[1-by,bx,c,B(i)],abs_.at[i],abr.at[i],xn)
    send_ac=lambda i: rc(ob(i).at[:,:,c],ob(i).at[:,:,c],acs.at[i],acr.at[i],cn)
    def add(dst,src):
        dst[...]=(dst[...].astype(jnp.float32)+src[...].astype(jnp.float32)).astype(jnp.bfloat16)
    def loop(m,f):
        lax.fori_loop(0,m,lambda j,_: (f(j),0)[1],0)
    def move(u): return rc(gi.at[u],gi_o.at[z%2],fs.at[u],frv.at[z%2],(tdp,2*c+u))
    keep=pltpu.make_async_copy(gi.at[z%2],gi_o.at[z%2],keeps.at[0])
    def operand(i):
        if len(plan[i])==5:
            l,r,zs,lo,ro=plan[i]; s=i%2
            cps=[pltpu.make_async_copy(ops[l].at[:,pl.ds(t*zs+lo,256)],ab.at[s,t],opsem.at[s,t]) for t in range(nz)]
            return cps+[pltpu.make_async_copy(ops[r].at[:,pl.ds(ro,1024)],bb.at[s],opsem.at[s,nz])]
        if big(i):
            q=[(yy,xx) for yy in range(2) for xx in range(2)]
            cols=lambda yy,xx,cc: pl.ds(pl.multiple_of((yy*4+xx*2+cc)*128,128),128)
            return ([pltpu.make_async_copy(ready.at[:,:,cols(yy,xx,c)],tb(i).at[:,yy,xx],opsem.at[i%2,yy*2+xx]) for yy,xx in q]
                +[pltpu.make_async_copy(ready.at[:,:,cols(yy,xx,1-c)],sb(i).at[:,yy,xx],opsem.at[i%2,4+yy*2+xx]) for yy,xx in q])
        return [pltpu.make_async_copy(small.at[:,:,:,c],tb(i),opsem.at[i%2,0]),pltpu.make_async_copy(small.at[:,:,:,1-c],sb(i),opsem.at[i%2,1])]
    def drain(i):
        for f in (send_x1,send_y1,send_x2,send_y2,send_ax,send_ay): f(i).wait_send()
        for t in range(nz):
            @pl.when(z<t)
            def _(): send_r(i,t).wait_send()
            @pl.when(z>t)
            def _(): send_l(i,t,False).wait_send()
    bigs=[i for i in range(n) if big(i)]
    def sl(i):
        if big(i) and i-nt in bigs: drain(i-nt)
        if big(i) and i-nsnd in bigs: send_c(i-nsnd).wait_send()
        for cp in operand(i): cp.start()
    def s0(i):
        for cp in operand(i): cp.wait()
        if len(plan[i])==5:
            s=i%2; T=tb(i); Sb=sb(i)
            cut=lambda cc: jnp.concatenate([bb[s,:,pl.ds(pl.multiple_of((2*q+cc)*128,128),128)] for q in range(4)],axis=1)
            def make(cc,dst):
                right=cut(cc)
                def f(t):
                    tile=lax.dot_general(ab[s,t],right,TN,preferred_element_type=jnp.float32).astype(jnp.bfloat16)
                    for q in range(4): dst[t,q//2,q%2]=tile[:,128*q:128*q+128]
                loop(nz,f)
            make(1-c,Sb)
            send_c(i).start()
            make(c,T)
        else:
            send_c(i).start()
    def s1a(i):
        send_c(i).wait_recv(); load_c(i).start()
    def s1(i):
        load_c(i).wait()
        T=tb(i); C=cb(i)
        loop(nz*4,lambda j: add(T.at[j//4,(j//2)%2,j%2],C.at[j//4,(j//2)%2,j%2]))
        if zf(i): line_start(i)
        else: xy_start(i)
    def xy_start(i):
        send_x1(i).start(); send_y1(i).start()
    def line_start(i):
        @pl.when(z==0)
        def _():
            for t in reversed(range(1,nz)): send_r(i,t).start()
        @pl.when(z==nz-1)
        def _():
            for t in range(nz-1): send_l(i,t,t==nz-2).start()
    def s2(i):
        T=tb(i)
        send_x1(i).wait_recv()
        if zf(i): loop(2,lambda j: add(T.at[z,j,bx,A(i)],x1[i].at[j]))
        else: loop(nz*2,lambda j: add(T.at[j//2,j%2,bx,A(i)],x1[i].at[j//2,j%2]))
        send_x2(i).start()
        send_y1(i).wait_recv()
        if zf(i): loop(2,lambda j: add(T.at[z,by,j,B(i)],y1[i].at[j]))
        else: loop(nz*2,lambda j: add(T.at[j//2,by,j%2,B(i)],y1[i].at[j//2,j%2]))
        send_y2(i).start()
    def s3(i):
        T=tb(i)
        send_x2(i).wait_recv()
        if zf(i): add(T.at[z,by,bx,A(i)],x2[i])
        else: loop(nz,lambda j: add(T.at[j,by,bx,A(i)],x2[i].at[j]))
        send_y2(i).wait_recv()
        if zf(i): add(T.at[z,by,bx,B(i)],y2[i])
        else: loop(nz,lambda j: add(T.at[j,by,bx,B(i)],y2[i].at[j]))
        if zf(i): spread_start(i)
        else: line_start(i)
    def add_line(i,t,slot):
        if zf(i): loop(4,lambda j: add(tb(i).at[t,j//2,j%2],zb[i].at[slot,j//2,j%2]))
        else: add(line(i,t),zb[i].at[slot])
    def hop(h,i):
        @pl.when(z==h)
        def _():
            for t in reversed(range(h+1,nz)):
                send_r(i,t).wait_recv()
                add_line(i,t,t)
                send_r(i,t).start()
        @pl.when(z==nz-1-h)
        def _():
            for t in range(nz-1-h):
                send_l(i,t,False).wait_recv()
                add_line(i,t,t)
                send_l(i,t,t==nz-2-h).start()
    def s6(i):
        @pl.when(z>0)
        def _():
            send_r(i,z).wait_recv()
            add_line(i,z,z)
        @pl.when(z<nz-1)
        def _():
            send_l(i,z,False).wait_recv()
            add_line(i,z,nz)
        if zf(i): xy_start(i)
        else: spread_start(i)
    def spread_start(i):
        send_ax(i).start(); send_ay(i).start(); keep_a(i).start()
    def s7(i):
        send_ax(i).wait_recv(); send_aa(i).start()
        send_ay(i).wait_recv(); send_ab(i).start()
    def s8(i):
        keep_a(i).wait()
        send_aa(i).wait_recv(); send_ab(i).wait_recv(); send_ac(i).start()
    def start_moves():
        for u in range(2):
            @pl.when(jnp.logical_or(tcore!=c,2*c+u!=z))
            def _(): move(u).start()
        @pl.when(tcore==c)
        def _(): keep.start()
    hops=[functools.partial(hop,h) for h in range(1,nz-1)]
    xy_stages=list(zip([sl,s0,s1a,s1,s2,s3]+hops+[s6,s7,s8],XY_LAGS))
    z_stages=list(zip([sl,s0,s1a,s1]+hops+[s6,s2,s3,s7,s8],Z_LAGS))
    for s in range(n+max(XY_LAGS+Z_LAGS)):
        if s==MOVE_AT: start_moves()
        todo=[(d,f,i) for i in range(n) for f,d in (z_stages if zf(i) else xy_stages) if i+d==s]
        for d,f,i in sorted(todo,key=lambda x:-x[0]): f(i)
    for i in range(n):
        if not (big(i) and i+nt in bigs): drain(i)
        if not (big(i) and i+nsnd in bigs): send_c(i).wait_send()
        send_aa(i).wait_send(); send_ab(i).wait_send()
        send_ac(i).wait()
    for u in range(2):
        @pl.when(jnp.logical_or(tcore!=c,2*c+u!=z))
        def _():
            move(u).wait_send()
            rc(gi.at[u],gi_o.at[u],fs.at[u],frv.at[u],(tdp,2*c+u)).wait_recv()
    @pl.when(tcore==c)
    def _(): keep.wait()

XY_LAGS=(0,1,2,3,5,6,7,8,9,10,11)
Z_LAGS=(0,1,2,3,5,6,8,9,10,11,12)
SLOTS=14
MOVE_AT=0
def reduce_call(ops,ready,small,gi,plan,zfirst,nz,cid):
    n=len(plan); nb=sum(len(x)>0 for x in plan); bf=jnp.bfloat16
    rows=ops[0].shape[0]
    any_=pl.BlockSpec(memory_space=pl.ANY)
    sd=jax.ShapeDtypeStruct
    outs=[sd((nb,2,2,2,256,128),bf),sd((2,2,2,32,128),bf),sd(gi.shape,gi.dtype),sd((nb,nz,2,2,256,128),bf),sd((nz,2,2,32,128),bf)]
    V=pltpu.VMEM; S=pltpu.SemaphoreType.DMA
    h=[128 if len(x) else 16 for x in plan]
    lead=lambda i: () if i in zfirst else (nz,)
    scratch=[V((SLOTS,nz,2,2,256,128),bf),V((nz,2,2,32,128),bf),V((2,nz,2,2,256,128),bf),V((nz,2,2,32,128),bf),V((2,nz,2,2,256,128),bf),V((nz,2,2,32,128),bf),
        V((2,nz,rows,256),bf),V((2,rows,1024),bf)]
    scratch+=[V(lead(i)+(2,h[i],128),bf) for i in range(n)]*2+[V(lead(i)+(h[i],128),bf) for i in range(n)]*2
    scratch+=[V((nz+1,)+((2,2) if i in zfirst else ())+(2*h[i],128),bf) for i in range(n)]
    scratch+=[S((n,))]*20+[S((n,nz))]*4+[S((1,)),S((n,)),S((n,)),S((2,8)),S((2,)),S((2,)),S((1,))]
    return pl.pallas_call(functools.partial(reduce_kernel,plan,zfirst,nz,len(ops)),out_shape=outs,in_specs=[any_]*(len(ops)+3),out_specs=[any_]*len(outs),
        scratch_shapes=scratch,
        compiler_params=pltpu.CompilerParams(collective_id=cid,has_side_effects=True,vmem_limit_bytes=58*2**20),
        cost_estimate=pl.CostEstimate(flops=2*n*rows*2**20,bytes_accessed=100*2**20,transcendentals=0),
    )(*ops,ready,small,gi)[:3]

def grad_plan(seq_count):
    plan, names = [], {}
    def weight(name, left, right, blocks, shrink):
        names[name] = len(plan), blocks
        for j in range(blocks):
            plan.append((left, right, 256 * blocks, 256 * j, 0) if shrink else (left, right, 256, 0, 1024 * j))
    weight("w4", 0, 1, 4, True)
    weight("w3", 2, 3, 4, False)
    weight("wco", 4, 5, 1, False)
    weight("wci", 6, 7, 2, False)
    weight("wo", 8, 9, 1, False)
    weight("wqkv", 10, 11, 3, False)
    names["wpos"] = len(plan), 1
    plan.append((0,))
    weight("w2", 12, 13, 4, True)
    weight("w1", 14, 15, 4, False)
    plan.append(())
    return plan, names

WIDEN_SLOTS = 4


def widen_kernel(spots, blocks_ref, *refs):
    outs, (narrow, wide, in_sem, out_sem) = refs[:-4], refs[-4:]
    count = len(spots)

    def fetch(i):
        return pltpu.make_async_copy(blocks_ref.at[i], narrow.at[i % WIDEN_SLOTS], in_sem.at[i % WIDEN_SLOTS])

    def put(i):
        which, row, column = spots[i]
        target = outs[which].at[pl.ds(row, 256), pl.ds(column, 1024)]
        return pltpu.make_async_copy(wide.at[i % WIDEN_SLOTS], target, out_sem.at[i % WIDEN_SLOTS])

    for i in range(WIDEN_SLOTS - 1):
        fetch(i).start()
    for i in range(count):
        if i + WIDEN_SLOTS - 1 < count:
            fetch(i + WIDEN_SLOTS - 1).start()
        fetch(i).wait()
        if i >= WIDEN_SLOTS:
            put(i - WIDEN_SLOTS).wait()
        slot = i % WIDEN_SLOTS

        def cast(piece, _):
            wide[slot, :, pl.ds(pl.multiple_of(128 * piece, 128), 128)] = narrow[slot, piece].astype(jnp.float32)
            return 0

        lax.fori_loop(0, 8, cast, 0, unroll=True)
        put(i).start()
    for i in range(count - WIDEN_SLOTS, count):
        put(i).wait()


def widen(blocks, names):
    spots, shapes = [], []
    for which, (name, (first, length)) in enumerate(names.items()):
        tall = name in ("w2", "w4")
        spots += [(which, 256 * j if tall else 0, 0 if tall else 1024 * j) for j in range(length)]
        shapes.append(jax.ShapeDtypeStruct((256 * length, 1024) if tall else (256, 1024 * length), jnp.float32))
    anywhere = pl.BlockSpec(memory_space=pl.ANY)
    wide = pl.pallas_call(
        functools.partial(widen_kernel, spots),
        in_specs=[anywhere],
        out_specs=[anywhere] * len(shapes),
        out_shape=shapes,
        scratch_shapes=[
            pltpu.VMEM((WIDEN_SLOTS, 8, 256, 128), jnp.bfloat16),
            pltpu.VMEM((WIDEN_SLOTS, 256, 1024), jnp.float32),
            pltpu.SemaphoreType.DMA((WIDEN_SLOTS,)),
            pltpu.SemaphoreType.DMA((WIDEN_SLOTS,)),
        ],
        compiler_params=pltpu.CompilerParams(vmem_limit_bytes=56 * 2**20),
        cost_estimate=pl.CostEstimate(flops=0, bytes_accessed=36 * 2**20, transcendentals=0),
    )(blocks)
    return dict(zip(names, wide))


def reduce_all(ops, ready, g_small, grad_input, seq_count):
    width = D // seq_count
    pieces = width // 128
    small = g_small.reshape(32, seq_count, pieces, 128).transpose(1, 2, 0, 3)
    small = jnp.pad(small, ((0, 0), (0, 8 - pieces), (0, 0), (0, 0))).reshape(seq_count, 2, 2, 2, 32, 128)
    plan, names = grad_plan(seq_count)
    by_line = {i for i in range(2, len(plan) - 1, 3)}
    blocks, small, grad_input = reduce_call(ops, ready, small, grad_input, plan, by_line, seq_count, 1)
    count = lax.axis_size("dp")
    if count > 8:
        groups = [[i + 8 * quad for quad in range(count // 8)] for i in range(8)]
        blocks, small = (lax.psum(x, "dp", axis_index_groups=groups) for x in (blocks, small))
    sums = widen(blocks.reshape(-1, 8, 256, 128), names)
    sums["wpos"] = sums["wpos"].T
    small = small.reshape(8, 32, 128)[:pieces].transpose(1, 0, 2).reshape(32, width).astype(jnp.float32)
    return sums, small, grad_input


def layer_norm(stream, gain, offset):
    average = jnp.mean(stream, axis=-1, keepdims=True)
    centred = stream - average
    spread = jnp.mean(centred * centred, axis=-1, keepdims=True)
    return centred * lax.rsqrt(spread + EPSILON) * gain + offset


def layer_norm_back(stream, gain, grad):
    average = jnp.mean(stream, axis=-1, keepdims=True)
    centred = stream - average
    spread = jnp.mean(centred * centred, axis=-1, keepdims=True)
    inverse = lax.rsqrt(spread + EPSILON)
    unit = centred * inverse
    scaled = grad * gain
    grad_stream = inverse * (
        scaled
        - jnp.mean(scaled, axis=-1, keepdims=True)
        - unit * jnp.mean(scaled * unit, axis=-1, keepdims=True)
    )
    return grad_stream, jnp.sum(grad * unit, axis=0), jnp.sum(grad, axis=0)


def swish(value):
    return value * jax.nn.sigmoid(value)


def swish_back(value, grad):
    gate = jax.nn.sigmoid(value)
    return grad * gate * (1.0 + value * (1.0 - gate))


def position_tables(first_row, rows, length, features):
    fine = 32
    column = lax.broadcasted_iota(jnp.int32, (1, features), 1)
    odd = column % 2 == 1
    frequency = jnp.exp((column // 2).astype(jnp.float32) * (-2.0 * math.log(10000.0) / features))
    coarse_at = (length - 1 - first_row - fine * jnp.arange(rows // fine, dtype=jnp.int32)).astype(jnp.float32)
    fine_at = jnp.arange(fine, dtype=jnp.int32).astype(jnp.float32)
    coarse = coarse_at[:, None] * frequency
    small = fine_at[:, None] * frequency
    coarse_sin, coarse_cos = jnp.sin(coarse), jnp.cos(coarse)
    return jnp.where(odd, coarse_cos, coarse_sin), jnp.where(odd, -coarse_sin, coarse_cos), jnp.cos(small), jnp.sin(small)


def mm(left, right):
    return jnp.dot(left, right, preferred_element_type=jnp.float32)


def mm_nt(left, right):
    return lax.dot_general(left, right, NT, preferred_element_type=jnp.float32)


def mm_tn(left, right):
    return lax.dot_general(left, right, TN, preferred_element_type=jnp.float32).astype(jnp.bfloat16)


def pair_swap(value):
    count = lax.axis_size("dp")
    return lax.ppermute(value, "dp", [(i, i + 1 - 2 * (i % 2)) for i in range(count)])


def redistribute(value):
    dp_count, seq_count = lax.axis_size("dp"), lax.axis_size("seq")
    z = lax.axis_index("seq")
    routes = ([], [])
    for dp in range(dp_count):
        for zz in range(seq_count):
            a, b, c = zz // 2, zz % 2, dp % 2
            for which in range(2):
                routes[which].append(
                    (dp * seq_count + zz, (dp - c + a) * seq_count + 2 * c + (b + which) % 2)
                )
    low = z % 2 == 0
    straight = lax.ppermute(jnp.where(low, value[0], value[1]), ("dp", "seq"), routes[0])
    crossed = lax.ppermute(jnp.where(low, value[1], value[0]), ("dp", "seq"), routes[1])
    return jnp.stack([jnp.where(low, straight, crossed), jnp.where(low, crossed, straight)])


def with_halo(rows, core):
    margin = (KERNEL - 1) // 2
    got = pair_swap(jnp.where(core == 0, rows[-margin:], rows[:margin]))
    none = jnp.zeros_like(got)
    return jnp.concatenate([jnp.where(core == 1, got, none), rows, jnp.where(core == 0, got, none)], axis=0)


def shards(
    frames, cotangent, lengths, assignment, norm_gains, norm_biases, expand_one, shrink_one, qkv_weight,
    pos_weight, pos_biases, attn_out, conv_in, conv_depth, conv_out, expand_two, shrink_two,
):
    seq_count = lax.axis_size("seq")
    dp, z = lax.axis_index("dp"), lax.axis_index("seq")
    core = dp % 2
    own_length = lengths[assignment[dp - core + z // 2], z % 2]
    rows = 2 * frames.shape[2]
    tables = position_tables((1 - core) * rows, 3 * rows, 2 * rows, D)
    weights, small_all, x_in, cot, first_part = gather(
        [expand_one, shrink_one, qkv_weight, pos_weight, attn_out, conv_in, conv_out, expand_two, shrink_two],
        [norm_gains, norm_biases, conv_depth, pos_biases], frames[0], cotangent[0], own_length.reshape(1), tables, seq_count,
    )
    w1, w2, wqkv, _, wo, wci, wco, w3, w4 = weights
    h1, a1, s1, x1, ha, qkv, kv_other, sinusoid, ptab, prob, attn = first_part
    vectors = small_all.transpose(1, 0, 2).reshape(32, D).astype(jnp.float32)
    gains, biases, depth, pos_pair = vectors[0:6], vectors[6:12], vectors[12:17], vectors[16:24]
    pos_pair = jnp.concatenate([vectors[17:19], jnp.zeros((6, D), jnp.float32)], axis=0)
    x0 = x_in.reshape(rows, D).astype(jnp.float32)
    cot = cot.reshape(rows, D).astype(jnp.float32)
    valid = (core * rows + jnp.arange(rows, dtype=jnp.int32) < own_length).astype(jnp.float32)[:, None]

    scalars = jnp.stack([core, own_length]).astype(jnp.int32)
    x2 = x1 + mm(attn, wo)
    hc = layer_norm(x2, gains[2], biases[2]).astype(jnp.bfloat16)
    dbl = mm(hc, wci)
    gate = jax.nn.sigmoid(dbl[:, D:])
    m = (dbl[:, :D] * gate * valid).astype(jnp.bfloat16)
    rim = with_halo(m, core)
    cv = depth[0] * rim[0:rows]
    for tap in range(1, KERNEL):
        cv = cv + depth[tap] * rim[tap : tap + rows]
    sc = swish(layer_norm(cv, gains[3], biases[3])).astype(jnp.bfloat16)
    x3 = x2 + mm(sc, wco)
    h2 = layer_norm(x3, gains[4], biases[4]).astype(jnp.bfloat16)
    a2 = mm(h2, w3)
    s2 = swish(a2).astype(jnp.bfloat16)
    x4 = x3 + 0.5 * mm(s2, w4)
    encoded = layer_norm(x4, gains[5], biases[5]).astype(jnp.bfloat16)
    encoded = redistribute(encoded.reshape(2, rows // 2, D))

    gx4, gg5, gb5 = layer_norm_back(x4, gains[5], cot)
    go2 = (0.5 * gx4).astype(jnp.bfloat16)
    ga2 = swish_back(a2, mm_nt(go2, w4)).astype(jnp.bfloat16)
    back, gg4, gb4 = layer_norm_back(x3, gains[4], mm_nt(ga2, w3))
    gx3 = gx4 + back
    gco = gx3.astype(jnp.bfloat16)
    inner = layer_norm(cv, gains[3], biases[3])
    gcv, gg3, gb3 = layer_norm_back(cv, gains[3], swish_back(inner, mm_nt(gco, wco)))
    gcv = gcv.astype(jnp.bfloat16)
    grim = with_halo(gcv, core)
    gm = depth[0] * grim[KERNEL - 1 : KERNEL - 1 + rows]
    for tap in range(1, KERNEL):
        gm = gm + depth[tap] * grim[KERNEL - 1 - tap : KERNEL - 1 - tap + rows]
    g_depth = jnp.stack([
        jnp.sum(gcv.astype(jnp.float32) * rim[tap : tap + rows].astype(jnp.float32), axis=0) for tap in range(KERNEL)
    ])
    gm = gm * valid
    gdbl = jnp.concatenate(
        [(gm * gate).astype(jnp.bfloat16), (gm * dbl[:, :D] * gate * (1.0 - gate)).astype(jnp.bfloat16)], axis=1
    )
    back, gg2, gb2 = layer_norm_back(x2, gains[2], mm_nt(gdbl, wci))
    gx2 = gx3 + back
    gao = gx2.astype(jnp.bfloat16)
    gattn = mm_nt(gao, wo).astype(jnp.bfloat16)
    gq, gk, gv, gk_other, gv_other, gptab, g_pair = attn_bwd(scalars, qkv, kv_other, ptab, pos_pair, gattn, attn, prob)
    got = pair_swap(jnp.concatenate([gk_other, gv_other], axis=1))
    gk = (gk + got[:, :D]).astype(jnp.bfloat16)
    gv = (gv + got[:, D:]).astype(jnp.bfloat16)
    gqkv = jnp.concatenate([gq, gk, gv], axis=1)
    g_wpos = mm_tn(gptab, sinusoid).reshape(seq_count, D // seq_count, D)
    back, gg1, gb1 = layer_norm_back(x1, gains[1], mm_nt(gqkv, wqkv))
    gx1 = gx2 + back
    go1 = (0.5 * gx1).astype(jnp.bfloat16)
    ga1 = swish_back(a1, mm_nt(go1, w2)).astype(jnp.bfloat16)
    back, gg0, gb0 = layer_norm_back(x0, gains[0], mm_nt(ga1, w1))
    gx0 = gx1 + back
    g_small = jnp.concatenate(
        [jnp.stack([gg0, gg1, gg2, gg3, gg4, gg5, gb0, gb1, gb2, gb3, gb4, gb5]), g_depth, g_pair[:2], jnp.zeros((13, D), jnp.float32)],
        axis=0,
    ).astype(jnp.bfloat16)
    sums, s_small, grad_input = reduce_all(
        [s2, go2, h2, ga2, sc, gco, hc, gdbl, attn, gao, ha, gqkv, s1, go1, h1, ga1],
        g_wpos, g_small, gx0.astype(jnp.bfloat16).reshape(2, rows // 2, D), seq_count,
    )
    grad_input = grad_input.astype(jnp.float32)
    return (
        encoded[None], grad_input[None], s_small[0:6], s_small[6:12], sums["w1"], sums["w2"], sums["wqkv"],
        sums["wpos"], s_small[17:19], sums["wo"], sums["wci"], s_small[12:17], sums["wco"], sums["w3"], sums["w4"],
    )


def solution(mesh):
    rows, columns = P("seq", None), P(None, "seq")
    act = P("dp", None, "seq", None)
    return jax.shard_map(
        shards,
        mesh=mesh,
        in_specs=(act, act, P(), P(), columns, columns, rows, rows, rows, columns, columns, rows, rows, columns, rows, rows, rows),
        out_specs=(act, act, columns, columns, rows, rows, rows, columns, columns, rows, rows, columns, rows, rows, rows),
        check_vma=False,
    )
```

time: 1830 us -> 695 us (0.38)
  waiting for transfers between devices: 1170 us -> 3.3 us
  Pallas kernels: 271 us -> 536 us
  matrix products: 174 us -> 79.9 us
  blocking collectives: 76.1 us -> 0 us
  local copies, waits for them, and re-layouts: 46.9 us -> 17.7 us
    reduce_scatter x9 -> x0, waiting for transfers between devices: 1010 us -> none  [reduce_all(): part = lax.psum_scatter(g, ('seq', 'dp'), scatter_dimension=0, tiled=True)]
    pallas_call x2 -> x3, Pallas kernels: 236 us -> 503 us  [the longest x1 276 us: reduce_call(): pl.pallas_call(functools.partial(reduce_kernel, plan, zfirst, nz, len(ops...]
    all_gather x6 -> x0, waiting for transfers between devices: 137 us -> none  [reduce_all(): lax.all_gather(part, 'dp', axis=0, tiled=True).astype(jnp.float32)]
    dot_general x9 -> x1, matrix products: 67.3 us -> 7.82 us  [mm_tn(): lax.dot_general(left, right, TN, preferred_element_type=jnp.float32)]
    psum x1 -> x0, blocking collectives: 46.9 us -> none  [reduce_all(): lax.psum(g_small.astype(jnp.bfloat16), ('dp', 'seq')).astype(jnp.float32)]
    all_gather x3 -> x0, blocking collectives: 29.1 us -> none  [reduce_all(): lax.all_gather(part, 'dp', axis=0, tiled=True).astype(jnp.float32)]
    dot_general x9 -> x5, matrix products: 46.5 us -> 23.6 us  [mm(): return jnp.dot(left, right, preferred_element_type=jnp.float32)]
    convert_element_type x15 -> x10, other arithmetic: 28.9 us -> 7.68 us  [the longest x1 2.06 us: shards(): gao = gx2.astype(jnp.bfloat16)]
  transfers between devices with their start and end apart: 23 -> 5, of which waited for: 18 -> 2; matrix products, arithmetic and copies ran while one was open for 8% -> 2% of each run, Pallas kernels for 2% -> 0%
where the time goes in v3:
time: 695 us; the launch traced here: 690 us
  Pallas kernels  536 us (77%)
  matrix products  79.9 us (11%)
  other arithmetic  47 us (7%)
  local copies, waits for them, and re-layouts  17.7 us (3%)
    pallas_call x1, Pallas kernels, reduce_call(): pl.pallas_call(functools.partial(reduce_kernel, plan, zfirst, nz, len(ops...  276 us
    pallas_call x1, Pallas kernels, gather(): pl.pallas_call(functools.partial(gather_kernel, items, order, nw, nz), ou...  214 us
    dot_general x8, matrix products, mm_nt(): return lax.dot_general(left, right, NT, preferred_element_type=jnp.float32)  48.4 us
    pallas_call x1, Pallas kernels, attn_bwd(): pl.pallas_call(attn_bwd_kernel, grid=(H,), in_specs=[pl.BlockSpec(memory_...  33 us
    dot_general x5, matrix products, mm(): return jnp.dot(left, right, preferred_element_type=jnp.float32)  23.6 us
  transfers between devices with their start and end apart: 5, of which 2 were waited for; matrix products, arithmetic and copies ran while one was open for 2% of the time, Pallas kernels for 0%

profile of v3, /device:TPU:0, one launch (start us, length us, event | category | flops | bytes accessed | tf_op | source)
XLA Modules:
  0.0 690.0 jit_solution(17196632068123269821)
XLA Ops:
  0.7 1.2 dynamic_slice.6
  3.9 1.2 multiply_sine_fusion.1
  5.2 1.5 fusion.28
  6.7 1.3 dynamic_slice.7
  8.0 213.7 %shard_map.280 = (bf16[4,4,2,32,4096]{4,3,2,1,0:T(8,128)(2,1)}, bf16[4,4,2,128,1024]{4,3,2,1,0:T(8,128)(2,1)}, bf16[4,4,2,32,3072]{4,3,2,1,0:T(8,128)(2,1)}, bf1...) custom-call(bf16[4,2,32,4096]{3,2,1,0:T(8,128)(2,1)} %bitcast.213, ...), custom_call_target="tpu_custom_call" | custom-call | flops 24999999488 | bytes 100663296 | tf_op jit(solution)/shard_map/pallas_call | solution.py:325
  221.6 0.9 convert_bitcast_fusion
  222.5 3.9 fusion.50
  226.8 1.6 fusion.40
  228.4 0.4 add_convert_fusion.5.refs_6_
  228.9 1.0 copy-done.23
  229.9 2.3 fusion.53
  232.3 0.6 multiply_convert_fusion.9
  232.8 1.5 copy-done.2
  234.4 1.0 copy-done.8
  236.3 1.8 fusion.22
  238.1 5.4 fusion.47
  244.0 0.8 multiply_convert_fusion.8.refs_4_
  244.8 0.4 copy-done.29
  245.2 0.9 copy-done.7
  246.1 1.4 fusion.51
  247.8 0.4 add_convert_fusion.4.refs_2_
  248.2 0.5 slice-done.3
  248.8 7.5 %multiply_convert_fusion.2 = (bf16[512,4096]{1,0:T(8,128)(2,1)S(1)}, f32[512,4096]{1,0:T(8,128)}) fusion(bf16[512,1024]{1,0:T(8,128)(2,1)S(1)} %add_convert_fusion.4.refs_2_, bf16[1024,4096]{1,0:T(8,128)(2,1)S(1)} %bitcast.231), kind=kOutput, calls=%fused_computation.2 | convolution fusion | flops 4305453056 | bytes 22020096 | tf_op jit(solution)/shard_map/dot_general | solution.py:779
  256.3 8.5 %fusion.52 = (f32[512]{0:T(512)S(1)}, f32[512,1024]{1,0:T(8,128)S(1)}) fusion(f32[512,1024]{1,0:T(8,128)S(1)} %get-tuple-element.204, bf16[512,4096]{1,0:T(8,128)(2,1)S(1)} %get-tuple-element.205.refs_0_, bf16[4096,1024]{1,0:T(8,128)(2,1)} %bitcast.232), kind=kOutput, calls=%fused_computation.192 | convolution fusion | flops 4296539648 | bytes 16779264 | tf_op jit(solution)/shard_map/dot_general | solution.py:779
  265.2 1.0 fusion.23
  266.3 0.7 multiply_convert_fusion.7.refs_1_
  267.0 1.0 copy-done.19
  268.0 11.7 %multiply_convert_fusion.1.refs_3_ = bf16[512,4096]{1,0:T(8,128)(2,1)} fusion(f32[512,4096]{1,0:T(8,128)} %get-tuple-element.206, bf16[512,1024]{1,0:T(8,128)(2,1)S(1)} %multiply_convert_fusion.7.refs_1_, bf16[4096,1024]{1,0:T(8,128)(2,1)} %bitcast.233), kind=kOutput, calls=%fused_computation.1 | convolution fusion | flops 4313841664 | bytes 22020096 | tf_op jit(solution)/shard_map/dot_general | solution.py:783
  279.7 8.8 %multiply_reduce_fusion.1 = (bf16[1024]{0:T(1024)(128)(2,1)S(1)}, f32[512]{0:T(512)S(1)}, f32[512]{0:T(512)S(1)}, bf16[1024]{0:T(1024)(128)(2,1)S(1)}, f32[512,1024]{1,0:T(8,128)S(1)}) fusion(f32[512,1024]{1,0:T(8,128)S(1)} %get-tuple-element.204, f32[512]{0:T(512)S(1)} %add_rsqrt_fusion.2, f32[512]{0:T(512)S(1)} %broadcast_multiply_fusion.14, ...), kind=kOutput, calls=%fused_computation.49 | convolution fusion | flops 4299682816 | bytes 16793600 | tf_op jit(solution)/shard_map/dot_general | solution.py:783
  288.6 1.7 fusion.46
  290.3 2.4 multiply_reduce_fusion.2
  292.7 3.6 fusion.12
  296.4 0.4 collective-permute-start.3
  296.8 0.7 pad_add_fusion.sc_ref
  297.7 3.3 multiply_convert_fusion.5
  301.0 0.8 multiply_convert_fusion.4
  301.9 2.0 copy-done.27
  303.9 2.9 multiply_reduce_fusion.3
  306.8 2.1 fusion.44
  308.9 1.3 convolution_convert_fusion.1.g_ref
  310.5 33.0 %shard_map.281 = (bf16[512,1024]{1,0:T(8,128)(2,1)S(1)}, f32[512,1024]{1,0:T(8,128)}, f32[512,1024]{1,0:T(8,128)}, bf16[512,1024]{1,0:T(8,128)(2,1)S(1)}, bf16[5...) custom-call(s32[2]{0:T(128)S(1)} %pad_add_fusion.sc_ref, ...), custom_call_target="tpu_custom_call" | custom-call | flops 6442450944 | bytes 31457280 | tf_op jit(solution)/shard_map/pallas_call | solution.py:407
  343.5 1.5 pad_maximum_fusion.2
  345.8 0.7 collective-permute-start.1
  346.6 7.8 %convolution_convert_fusion = bf16[1024,1024]{1,0:T(8,128)(2,1)} fusion(bf16[1536,1024]{1,0:T(8,128)(2,1)} %get-tuple-element.80, bf16[1536,1024]{1,0:T(8,128)(2,1)} %get-tuple-element.81), kind=kOutput, calls=%fused_computation.88 | convolution fusion | flops 3222274048 | bytes 8388608 | tf_op jit(solution)/shard_map/dot_general | solution.py:787
  354.5 1.5 pad_maximum_fusion.1.refs_7_
  356.0 3.2 collective-permute-done.2
  359.3 1.1 maximum_bitcast_fusion
  360.4 2.4 add_convert_fusion.2
  362.8 2.0 pad_maximum_fusion.refs_11_
  365.1 4.0 multiply_reduce_fusion.4
  369.2 0.8 multiply_convert_fusion.3
  370.1 11.1 %multiply_convert_fusion.refs_15_ = bf16[512,4096]{1,0:T(8,128)(2,1)S(1)} fusion(f32[512,4096]{1,0:T(8,128)} %get-tuple-element.79, bf16[512,1024]{1,0:T(8,128)(2,1)S(1)} %get-tuple-element.157.refs_13_, bf16[4096,1024]{1,0:T(8,128)(2,1)} %bitcast.227), kind=kOutput, calls=%fused_computation | convolution fusion | flops 4313841664 | bytes 22020096 | tf_op jit(solution)/shard_map/dot_general | solution.py:783
  381.2 6.3 multiply_reduce_fusion
  387.5 0.5 concatenate.97
  388.1 0.8 pad.5
  388.8 3.3 add_convert_fusion
  392.2 276.1 %shard_map.282 = (bf16[24,2,2,2,256,128]{5,4,3,2,1,0:T(8,128)(2,1)}, bf16[2,2,2,32,128]{4,3,2,1,0:T(8,128)(2,1)}, bf16[2,256,1024]{2,1,0:T(8,128)(2,1)}, bf16[24...) custom-call(bf16[512,4096]{1,0:T(8,128)(2,1)} %copy-done.31, bf16[512,1024]{1,0:T(8,128)(2,1)} %copy-done.19, ...), custom_call_target="tpu_custom_call" | custom-call | flops 26843545600 | bytes 104857600 | tf_op jit(solution)/shard_map/pallas_call | solution.py:632
  668.3 0.7 convert_bitcast_fusion.1
  669.0 0.6 slice_bitcast_fusion.3
  669.6 0.6 slice_bitcast_fusion
  670.2 0.6 slice_bitcast_fusion.1
  670.8 2.8 bitcast_convert_fusion
  673.6 13.6 %shard_map.283 = (f32[1024,1024]{1,0:T(8,128)}, f32[256,4096]{1,0:T(8,128)}, f32[256,1024]{1,0:T(8,128)}, f32[256,2048]{1,0:T(8,128)}, f32[256,1024]{1,0:T(8,128...) custom-call(bf16[24,8,256,128]{3,2,1,0:T(8,128)(2,1)} %bitcast.150), custom_call_target="tpu_custom_call" | custom-call | bytes 37748736 | tf_op jit(solution)/shard_map/pallas_call | solution.py:699
  687.3 2.5 copy.54
  (144 shorter events, 4.4 us)
Async XLA Ops:
  226.4 2.4 copy-start.6
  226.4 3.4 copy-start.26
  228.8 1.0 copy-start.23
  232.2 2.1 copy-start.2
  232.2 3.5 copy-start.10
  232.3 3.8 copy-start.4
  234.4 1.0 copy-start.8
  234.4 1.9 copy-start.1
  235.3 2.8 collective-permute-start
  243.6 1.6 copy-start.29
  243.9 2.1 copy-start.7
  244.0 4.3 slice-start.2
  244.8 2.7 copy-start.24
  246.1 2.7 slice-start.3
  248.2 8.1 %copy-start.25 = (bf16[512,1024]{1,0:T(8,128)(2,1)}, bf16[512,1024]{1,0:T(8,128)(2,1)S(1)}, u32[]{:S(2)}) copy-start(bf16[512,1024]{1,0:T(8,128)(2,1)S(1)} %add_convert_fusion.4.refs_2_) | copy-start | bytes 3145732
  256.3 8.5 %copy-start.31 = (bf16[512,4096]{1,0:T(8,128)(2,1)}, bf16[512,4096]{1,0:T(8,128)(2,1)S(1)}, u32[]{:S(2)}) copy-start(bf16[512,4096]{1,0:T(8,128)(2,1)S(1)} %get-tuple-element.205.refs_0_) | copy-start | bytes 12582916
  267.0 1.0 copy-start.19
  290.3 2.4 copy-start.20
  290.3 2.4 copy-start.9
  292.7 4.9 copy-start.3
  296.4 1.3 collective-permute-start.3
  301.0 1.0 copy-start.13
  301.0 2.9 copy-start.27
  301.8 5.0 copy-start.15
  306.8 2.1 copy-start.28
  308.9 1.3 copy-start.21
  308.9 1.6 copy-start
  345.0 15.3 %collective-permute-start.4 = (bf16[512,2048]{1,0:T(8,128)(2,1)}, bf16[512,2048]{1,0:T(8,128)(2,1)}, u32[]{:S(2)}, u32[]{:S(2)}) collective-permute-start(bf16[512,2048]{1,0:T(8,128)(2,1)} %pad_maximum_fusion.2), channel_id=1, source_target_pairs={{0,4},{4,0},{8,12},{12,8},{16,20},{20,16},{24,28},{28,24},{1,5},{5... | collective-permute-start | bytes 6291464 | tf_op jit(solution)/shard_map/ppermute | solution.py:792
  345.8 10.2 %collective-permute-start.1 = (bf16[256,1024]{1,0:T(8,128)(2,1)S(1)}, bf16[256,1024]{1,0:T(8,128)(2,1)S(1)}, u32[]{:S(2)}, u32[]{:S(2)}) collective-permute-start(bf16[256,1024]{1,0:T(8,128)(2,1)S(1)} %get-tuple-element.172), channel_id=1, source_target_pairs={{0,0},{1,1},{2,4},{3,5},{4,2},{5,3},{6,6},{7,7},{8,8},{9,9},{10,12... | collective-permute-start | bytes 1572872 | tf_op jit(solution)/shard_map/ppermute | solution.py:807
  346.5 12.7 %collective-permute-start.2 = (bf16[256,1024]{1,0:T(8,128)(2,1)S(1)}, bf16[256,1024]{1,0:T(8,128)(2,1)S(1)}, u32[]{:S(2)}, u32[]{:S(2)}) collective-permute-start(bf16[256,1024]{1,0:T(8,128)(2,1)S(1)} %get-tuple-element.173), channel_id=1, source_target_pairs={{0,1},{1,0},{2,5},{3,4},{4,3},{5,2},{6,7},{7,6},{8,9},{9,8},{10,13... | collective-permute-start | bytes 1572872 | tf_op jit(solution)/shard_map/ppermute | solution.py:808
  346.6 7.9 %copy-start.14 = (bf16[512,1024]{1,0:T(8,128)(2,1)S(1)}, bf16[512,1024]{1,0:T(8,128)(2,1)}, u32[]{:S(2)}) copy-start(bf16[512,1024]{1,0:T(8,128)(2,1)} %copy-done.13) | copy-start | bytes 3145732
  346.6 7.9 %copy-start.16 = (bf16[512,1024]{1,0:T(8,128)(2,1)S(1)}, bf16[512,1024]{1,0:T(8,128)(2,1)}, u32[]{:S(2)}) copy-start(bf16[512,1024]{1,0:T(8,128)(2,1)} %copy-done.15) | copy-start | bytes 3145732
  346.6 18.1 %slice-start.4 = ((s8[6291456]{0:T(1024)(128)(4,1)}), s8[4194304]{0:T(1024)(128)(4,1)S(1)}, s32[]{:S(2)}) async-start(s8[6291456]{0:T(1024)(128)(4,1)} %bitcast.234), calls=%async_computation.4 | async-start | bytes 8388608
  356.0 4.4 copy-start.17
  356.0 4.4 copy-start.18
  356.0 8.7 %slice-start.5 = ((s8[6291456]{0:T(1024)(128)(4,1)}), s8[2097152]{0:T(1024)(128)(4,1)S(1)}, s32[]{:S(2)}) async-start(s8[6291456]{0:T(1024)(128)(4,1)} %bitcast.234), calls=%async_computation.5 | async-start | bytes 4194304
  362.8 2.4 copy-start.5
  365.1 4.1 copy-start.12
  369.2 12.0 %slice-start = ((s8[8388608]{0:T(1024)(128)(4,1)}), s8[4194304]{0:T(1024)(128)(4,1)S(1)}, s32[]{:S(2)}) async-start(s8[8388608]{0:T(1024)(128)(4,1)} %bitcast.224), calls=%async_computation | async-start | bytes 8388608
  370.0 11.1 %copy-start.22 = (bf16[512,1024]{1,0:T(8,128)(2,1)}, bf16[512,1024]{1,0:T(8,128)(2,1)S(1)}, u32[]{:S(2)}) copy-start(bf16[512,1024]{1,0:T(8,128)(2,1)S(1)} %get-tuple-element.157.refs_13_) | copy-start | bytes 3145732
  370.1 11.1 %copy-start.11 = (bf16[2,256,1024]{2,1,0:T(8,128)(2,1)S(1)}, bf16[2,256,1024]{2,1,0:T(8,128)(2,1)}, u32[]{:S(2)}) copy-start(bf16[2,256,1024]{2,1,0:T(8,128)(2,1)} %get-tuple-element.83) | copy-start | bytes 3145732
  370.1 11.1 %slice-start.1 = ((s8[8388608]{0:T(1024)(128)(4,1)}), s8[4194304]{0:T(1024)(128)(4,1)S(1)}, s32[]{:S(2)}) async-start(s8[8388608]{0:T(1024)(128)(4,1)} %bitcast.224), calls=%async_computation.1 | async-start | bytes 8388608
  381.2 6.3 copy-start.30

commit v4 on v3

--- a/solution.py
+++ b/solution.py
@@ -257,7 +257,7 @@
             load(order[s]).wait(); local(order[s]).start()
         if s+AHEAD<ni: go(s+AHEAD)
         if s<nz-1: at_(f1,ni,s+1)
-        if s==ni//2: moves(1,lambda a,u:move(a,u).start(),lambda a:keep(a).start())
+        if s==ni-1: moves(1,lambda a,u:move(a,u).start(),lambda a:keep(a).start())
         for f,late in ((f3,1),(f2,0),(f1,-1)):
             for d in range(1,nz):
                 if 0<=s-d-late<ni: at_(f,s-d-late,d)
@@ -293,9 +293,9 @@
     landed(1)
 
 ITEM=2**21
-BUDGET=2.0
+BUDGET=1.5
 SLACK=1
-AHEAD=1
+AHEAD=2
 def gather(ws,vecs,fr,ct,length,tables,nz,cid=0):
     nw=len(ws); bf=jnp.bfloat16; f32=jnp.float32
     small=jax.ShapeDtypeStruct((32,vecs[0].shape[1]),bf)
@@ -719,7 +719,7 @@
     small = g_small.reshape(32, seq_count, pieces, 128).transpose(1, 2, 0, 3)
     small = jnp.pad(small, ((0, 0), (0, 8 - pieces), (0, 0), (0, 0))).reshape(seq_count, 2, 2, 2, 32, 128)
     plan, names = grad_plan(seq_count)
-    by_line = {i for i in range(2, len(plan) - 1, 3)}
+    by_line = {i for i in range(1, len(plan) - 1, 3)}
     blocks, small, grad_input = reduce_call(ops, ready, small, grad_input, plan, by_line, seq_count, 1)
     count = lax.axis_size("dp")
     if count > 8:

time: 695 us -> 684 us (0.984)
  Pallas kernels: 536 us -> 525 us
where the time goes in v4:
time: 684 us; the launch traced here: 679 us
  Pallas kernels  525 us (77%)
  matrix products  79.9 us (12%)
  other arithmetic  47 us (7%)
  local copies, waits for them, and re-layouts  17.7 us (3%)
    pallas_call x1, Pallas kernels, reduce_call(): pl.pallas_call(functools.partial(reduce_kernel, plan, zfirst, nz, len(ops...  271 us
    pallas_call x1, Pallas kernels, gather(): pl.pallas_call(functools.partial(gather_kernel, items, order, nw, nz), ou...  208 us
    dot_general x8, matrix products, mm_nt(): return lax.dot_general(left, right, NT, preferred_element_type=jnp.float32)  48.5 us
    pallas_call x1, Pallas kernels, attn_bwd(): pl.pallas_call(attn_bwd_kernel, grid=(H,), in_specs=[pl.BlockSpec(memory_...  33 us
    dot_general x5, matrix products, mm(): return jnp.dot(left, right, preferred_element_type=jnp.float32)  23.6 us
  transfers between devices with their start and end apart: 5, of which 2 were waited for; matrix products, arithmetic and copies ran while one was open for 2% of the time, Pallas kernels for 0%

profile of v4, /device:TPU:0, one launch (start us, length us, event | category | flops | bytes accessed | tf_op | source)
XLA Modules:
  0.0 679.2 jit_solution(5003613482432943942)
XLA Ops:
  0.7 1.2 dynamic_slice.6
  3.9 1.2 multiply_sine_fusion.1
  5.2 1.5 fusion.28
  6.7 1.3 dynamic_slice.7
  8.0 208.1 %shard_map.280 = (bf16[4,4,2,32,4096]{4,3,2,1,0:T(8,128)(2,1)}, bf16[4,4,2,128,1024]{4,3,2,1,0:T(8,128)(2,1)}, bf16[4,4,2,32,3072]{4,3,2,1,0:T(8,128)(2,1)}, bf1...) custom-call(bf16[4,2,32,4096]{3,2,1,0:T(8,128)(2,1)} %bitcast.213, ...), custom_call_target="tpu_custom_call" | custom-call | flops 24999999488 | bytes 100663296 | tf_op jit(solution)/shard_map/pallas_call | solution.py:325
  216.0 0.9 convert_bitcast_fusion
  216.9 3.9 fusion.50
  221.2 1.6 fusion.40
  222.8 0.4 add_convert_fusion.5.refs_6_
  223.3 1.0 copy-done.23
  224.3 2.3 fusion.53
  226.7 0.6 multiply_convert_fusion.9
  227.2 1.5 copy-done.2
  228.8 1.0 copy-done.8
  230.7 1.8 fusion.22
  232.5 5.4 fusion.47
  238.4 0.8 multiply_convert_fusion.8.refs_4_
  239.2 0.4 copy-done.29
  239.6 0.9 copy-done.7
  240.5 1.4 fusion.51
  242.2 0.4 add_convert_fusion.4.refs_2_
  242.6 0.5 slice-done.3
  243.2 7.5 %multiply_convert_fusion.2 = (bf16[512,4096]{1,0:T(8,128)(2,1)S(1)}, f32[512,4096]{1,0:T(8,128)}) fusion(bf16[512,1024]{1,0:T(8,128)(2,1)S(1)} %add_convert_fusion.4.refs_2_, bf16[1024,4096]{1,0:T(8,128)(2,1)S(1)} %bitcast.231), kind=kOutput, calls=%fused_computation.2 | convolution fusion | flops 4305453056 | bytes 22020096 | tf_op jit(solution)/shard_map/dot_general | solution.py:779
  250.7 8.5 %fusion.52 = (f32[512]{0:T(512)S(1)}, f32[512,1024]{1,0:T(8,128)S(1)}) fusion(f32[512,1024]{1,0:T(8,128)S(1)} %get-tuple-element.204, bf16[512,4096]{1,0:T(8,128)(2,1)S(1)} %get-tuple-element.205.refs_0_, bf16[4096,1024]{1,0:T(8,128)(2,1)} %bitcast.232), kind=kOutput, calls=%fused_computation.192 | convolution fusion | flops 4296539648 | bytes 16779264 | tf_op jit(solution)/shard_map/dot_general | solution.py:779
  259.6 1.0 fusion.23
  260.7 0.7 multiply_convert_fusion.7.refs_1_
  261.4 1.0 copy-done.19
  262.4 11.8 %multiply_convert_fusion.1.refs_3_ = bf16[512,4096]{1,0:T(8,128)(2,1)} fusion(f32[512,4096]{1,0:T(8,128)} %get-tuple-element.206, bf16[512,1024]{1,0:T(8,128)(2,1)S(1)} %multiply_convert_fusion.7.refs_1_, bf16[4096,1024]{1,0:T(8,128)(2,1)} %bitcast.233), kind=kOutput, calls=%fused_computation.1 | convolution fusion | flops 4313841664 | bytes 22020096 | tf_op jit(solution)/shard_map/dot_general | solution.py:783
  274.1 8.8 %multiply_reduce_fusion.1 = (bf16[1024]{0:T(1024)(128)(2,1)S(1)}, f32[512]{0:T(512)S(1)}, f32[512]{0:T(512)S(1)}, bf16[1024]{0:T(1024)(128)(2,1)S(1)}, f32[512,1024]{1,0:T(8,128)S(1)}) fusion(f32[512,1024]{1,0:T(8,128)S(1)} %get-tuple-element.204, f32[512]{0:T(512)S(1)} %add_rsqrt_fusion.2, f32[512]{0:T(512)S(1)} %broadcast_multiply_fusion.14, ...), kind=kOutput, calls=%fused_computation.49 | convolution fusion | flops 4299682816 | bytes 16793600 | tf_op jit(solution)/shard_map/dot_general | solution.py:783
  283.0 1.7 fusion.46
  284.7 2.4 multiply_reduce_fusion.2
  287.2 3.6 fusion.12
  290.8 0.4 collective-permute-start.3
  291.2 0.7 pad_add_fusion.sc_ref
  292.1 3.3 multiply_convert_fusion.5
  295.4 0.8 multiply_convert_fusion.4
  296.3 2.0 copy-done.27
  298.3 2.9 multiply_reduce_fusion.3
  301.2 2.1 fusion.44
  303.3 1.3 convolution_convert_fusion.1.g_ref
  304.9 33.0 %shard_map.281 = (bf16[512,1024]{1,0:T(8,128)(2,1)S(1)}, f32[512,1024]{1,0:T(8,128)}, f32[512,1024]{1,0:T(8,128)}, bf16[512,1024]{1,0:T(8,128)(2,1)S(1)}, bf16[5...) custom-call(s32[2]{0:T(128)S(1)} %pad_add_fusion.sc_ref, ...), custom_call_target="tpu_custom_call" | custom-call | flops 6442450944 | bytes 31457280 | tf_op jit(solution)/shard_map/pallas_call | solution.py:407
  337.9 1.5 pad_maximum_fusion.2
  340.2 0.7 collective-permute-start.1
  341.0 7.8 %convolution_convert_fusion = bf16[1024,1024]{1,0:T(8,128)(2,1)} fusion(bf16[1536,1024]{1,0:T(8,128)(2,1)} %get-tuple-element.80, bf16[1536,1024]{1,0:T(8,128)(2,1)} %get-tuple-element.81), kind=kOutput, calls=%fused_computation.88 | convolution fusion | flops 3222274048 | bytes 8388608 | tf_op jit(solution)/shard_map/dot_general | solution.py:787
  348.9 1.5 pad_maximum_fusion.1.refs_7_
  350.4 3.6 collective-permute-done.2
  354.1 1.1 maximum_bitcast_fusion
  355.2 2.4 add_convert_fusion.2
  357.6 2.0 pad_maximum_fusion.refs_11_
  359.9 4.0 multiply_reduce_fusion.4
  364.0 0.8 multiply_convert_fusion.3
  364.9 11.1 %multiply_convert_fusion.refs_15_ = bf16[512,4096]{1,0:T(8,128)(2,1)S(1)} fusion(f32[512,4096]{1,0:T(8,128)} %get-tuple-element.79, bf16[512,1024]{1,0:T(8,128)(2,1)S(1)} %get-tuple-element.157.refs_13_, bf16[4096,1024]{1,0:T(8,128)(2,1)} %bitcast.227), kind=kOutput, calls=%fused_computation | convolution fusion | flops 4313841664 | bytes 22020096 | tf_op jit(solution)/shard_map/dot_general | solution.py:783
  376.0 6.3 multiply_reduce_fusion
  382.3 0.5 concatenate.97
  382.9 0.8 pad.5
  383.6 3.3 add_convert_fusion
  387.0 270.5 %shard_map.282 = (bf16[24,2,2,2,256,128]{5,4,3,2,1,0:T(8,128)(2,1)}, bf16[2,2,2,32,128]{4,3,2,1,0:T(8,128)(2,1)}, bf16[2,256,1024]{2,1,0:T(8,128)(2,1)}, bf16[24...) custom-call(bf16[512,4096]{1,0:T(8,128)(2,1)} %copy-done.31, bf16[512,1024]{1,0:T(8,128)(2,1)} %copy-done.19, ...), custom_call_target="tpu_custom_call" | custom-call | flops 26843545600 | bytes 104857600 | tf_op jit(solution)/shard_map/pallas_call | solution.py:632
  657.5 0.7 convert_bitcast_fusion.1
  658.2 0.6 slice_bitcast_fusion.3
  658.8 0.6 slice_bitcast_fusion
  659.4 0.6 slice_bitcast_fusion.1
  660.0 2.8 bitcast_convert_fusion
  662.8 13.6 %shard_map.283 = (f32[1024,1024]{1,0:T(8,128)}, f32[256,4096]{1,0:T(8,128)}, f32[256,1024]{1,0:T(8,128)}, f32[256,2048]{1,0:T(8,128)}, f32[256,1024]{1,0:T(8,128...) custom-call(bf16[24,8,256,128]{3,2,1,0:T(8,128)(2,1)} %bitcast.150), custom_call_target="tpu_custom_call" | custom-call | bytes 37748736 | tf_op jit(solution)/shard_map/pallas_call | solution.py:699
  676.5 2.5 copy.54
  (144 shorter events, 4.4 us)
Async XLA Ops:
  220.8 2.4 copy-start.6
  220.8 3.4 copy-start.26
  223.2 1.0 copy-start.23
  226.6 2.1 copy-start.2
  226.6 3.5 copy-start.10
  226.7 3.8 copy-start.4
  228.8 1.0 copy-start.8
  228.8 1.9 copy-start.1
  229.7 2.8 collective-permute-start
  238.0 1.6 copy-start.29
  238.3 2.1 copy-start.7
  238.4 4.3 slice-start.2
  239.2 2.7 copy-start.24
  240.5 2.7 slice-start.3
  242.6 8.1 %copy-start.25 = (bf16[512,1024]{1,0:T(8,128)(2,1)}, bf16[512,1024]{1,0:T(8,128)(2,1)S(1)}, u32[]{:S(2)}) copy-start(bf16[512,1024]{1,0:T(8,128)(2,1)S(1)} %add_convert_fusion.4.refs_2_) | copy-start | bytes 3145732
  250.7 8.5 %copy-start.31 = (bf16[512,4096]{1,0:T(8,128)(2,1)}, bf16[512,4096]{1,0:T(8,128)(2,1)S(1)}, u32[]{:S(2)}) copy-start(bf16[512,4096]{1,0:T(8,128)(2,1)S(1)} %get-tuple-element.205.refs_0_) | copy-start | bytes 12582916
  261.4 1.0 copy-start.19
  284.7 2.4 copy-start.20
  284.7 2.4 copy-start.9
  287.1 4.9 copy-start.3
  290.8 1.3 collective-permute-start.3
  295.3 1.0 copy-start.13
  295.4 2.9 copy-start.27
  296.2 5.0 copy-start.15
  301.2 2.1 copy-start.28
  303.3 1.3 copy-start.21
  303.3 1.6 copy-start
  339.4 15.8 %collective-permute-start.4 = (bf16[512,2048]{1,0:T(8,128)(2,1)}, bf16[512,2048]{1,0:T(8,128)(2,1)}, u32[]{:S(2)}, u32[]{:S(2)}) collective-permute-start(bf16[512,2048]{1,0:T(8,128)(2,1)} %pad_maximum_fusion.2), channel_id=1, source_target_pairs={{0,4},{4,0},{8,12},{12,8},{16,20},{20,16},{24,28},{28,24},{1,5},{5... | collective-permute-start | bytes 6291464 | tf_op jit(solution)/shard_map/ppermute | solution.py:792
  340.2 10.2 %collective-permute-start.1 = (bf16[256,1024]{1,0:T(8,128)(2,1)S(1)}, bf16[256,1024]{1,0:T(8,128)(2,1)S(1)}, u32[]{:S(2)}, u32[]{:S(2)}) collective-permute-start(bf16[256,1024]{1,0:T(8,128)(2,1)S(1)} %get-tuple-element.172), channel_id=1, source_target_pairs={{0,0},{1,1},{2,4},{3,5},{4,2},{5,3},{6,6},{7,7},{8,8},{9,9},{10,12... | collective-permute-start | bytes 1572872 | tf_op jit(solution)/shard_map/ppermute | solution.py:807
  340.9 13.1 %collective-permute-start.2 = (bf16[256,1024]{1,0:T(8,128)(2,1)S(1)}, bf16[256,1024]{1,0:T(8,128)(2,1)S(1)}, u32[]{:S(2)}, u32[]{:S(2)}) collective-permute-start(bf16[256,1024]{1,0:T(8,128)(2,1)S(1)} %get-tuple-element.173), channel_id=1, source_target_pairs={{0,1},{1,0},{2,5},{3,4},{4,3},{5,2},{6,7},{7,6},{8,9},{9,8},{10,13... | collective-permute-start | bytes 1572872 | tf_op jit(solution)/shard_map/ppermute | solution.py:808
  341.0 7.9 %copy-start.14 = (bf16[512,1024]{1,0:T(8,128)(2,1)S(1)}, bf16[512,1024]{1,0:T(8,128)(2,1)}, u32[]{:S(2)}) copy-start(bf16[512,1024]{1,0:T(8,128)(2,1)} %copy-done.13) | copy-start | bytes 3145732
  341.0 7.9 %copy-start.16 = (bf16[512,1024]{1,0:T(8,128)(2,1)S(1)}, bf16[512,1024]{1,0:T(8,128)(2,1)}, u32[]{:S(2)}) copy-start(bf16[512,1024]{1,0:T(8,128)(2,1)} %copy-done.15) | copy-start | bytes 3145732
  341.0 18.5 %slice-start.4 = ((s8[6291456]{0:T(1024)(128)(4,1)}), s8[4194304]{0:T(1024)(128)(4,1)S(1)}, s32[]{:S(2)}) async-start(s8[6291456]{0:T(1024)(128)(4,1)} %bitcast.234), calls=%async_computation.4 | async-start | bytes 8388608
  350.4 4.8 copy-start.17
  350.4 4.8 copy-start.18
  350.4 9.1 %slice-start.5 = ((s8[6291456]{0:T(1024)(128)(4,1)}), s8[2097152]{0:T(1024)(128)(4,1)S(1)}, s32[]{:S(2)}) async-start(s8[6291456]{0:T(1024)(128)(4,1)} %bitcast.234), calls=%async_computation.5 | async-start | bytes 4194304
  357.6 2.4 copy-start.5
  359.9 4.1 copy-start.12
  364.0 12.0 %slice-start = ((s8[8388608]{0:T(1024)(128)(4,1)}), s8[4194304]{0:T(1024)(128)(4,1)S(1)}, s32[]{:S(2)}) async-start(s8[8388608]{0:T(1024)(128)(4,1)} %bitcast.224), calls=%async_computation | async-start | bytes 8388608
  364.8 11.1 %copy-start.22 = (bf16[512,1024]{1,0:T(8,128)(2,1)}, bf16[512,1024]{1,0:T(8,128)(2,1)S(1)}, u32[]{:S(2)}) copy-start(bf16[512,1024]{1,0:T(8,128)(2,1)S(1)} %get-tuple-element.157.refs_13_) | copy-start | bytes 3145732
  364.9 11.1 %copy-start.11 = (bf16[2,256,1024]{2,1,0:T(8,128)(2,1)S(1)}, bf16[2,256,1024]{2,1,0:T(8,128)(2,1)}, u32[]{:S(2)}) copy-start(bf16[2,256,1024]{2,1,0:T(8,128)(2,1)} %get-tuple-element.83) | copy-start | bytes 3145732
  364.9 11.1 %slice-start.1 = ((s8[8388608]{0:T(1024)(128)(4,1)}), s8[4194304]{0:T(1024)(128)(4,1)S(1)}, s32[]{:S(2)}) async-start(s8[8388608]{0:T(1024)(128)(4,1)} %bitcast.224), calls=%async_computation.1 | async-start | bytes 8388608
  376.0 6.3 copy-start.30

commit v5 on v4

--- a/solution.py
+++ b/solution.py
@@ -295,7 +295,7 @@
 ITEM=2**21
 BUDGET=1.5
 SLACK=1
-AHEAD=2
+AHEAD=3
 def gather(ws,vecs,fr,ct,length,tables,nz,cid=0):
     nw=len(ws); bf=jnp.bfloat16; f32=jnp.float32
     small=jax.ShapeDtypeStruct((32,vecs[0].shape[1]),bf)

time: 684 us -> 688 us (level)
  no operation moved by 1% of the time
where the time goes in v5:
time: 688 us; the launch traced here: 683 us
  Pallas kernels  530 us (77%)
  matrix products  79.9 us (12%)
  other arithmetic  47 us (7%)
  local copies, waits for them, and re-layouts  17.7 us (3%)
    pallas_call x1, Pallas kernels, reduce_call(): pl.pallas_call(functools.partial(reduce_kernel, plan, zfirst, nz, len(ops...  270 us
    pallas_call x1, Pallas kernels, gather(): pl.pallas_call(functools.partial(gather_kernel, items, order, nw, nz), ou...  213 us
    dot_general x8, matrix products, mm_nt(): return lax.dot_general(left, right, NT, preferred_element_type=jnp.float32)  48.4 us
    pallas_call x1, Pallas kernels, attn_bwd(): pl.pallas_call(attn_bwd_kernel, grid=(H,), in_specs=[pl.BlockSpec(memory_...  33 us
    dot_general x5, matrix products, mm(): return jnp.dot(left, right, preferred_element_type=jnp.float32)  23.6 us
  transfers between devices with their start and end apart: 5, of which 2 were waited for; matrix products, arithmetic and copies ran while one was open for 2% of the time, Pallas kernels for 0%

profile of v5, /device:TPU:0, one launch (start us, length us, event | category | flops | bytes accessed | tf_op | source)
XLA Modules:
  0.0 682.8 jit_solution(9775763146588916054)
XLA Ops:
  0.7 1.2 dynamic_slice.6
  3.9 1.2 multiply_sine_fusion.1
  5.2 1.5 fusion.28
  6.7 1.3 dynamic_slice.7
  8.0 213.1 %shard_map.280 = (bf16[4,4,2,32,4096]{4,3,2,1,0:T(8,128)(2,1)}, bf16[4,4,2,128,1024]{4,3,2,1,0:T(8,128)(2,1)}, bf16[4,4,2,32,3072]{4,3,2,1,0:T(8,128)(2,1)}, bf1...) custom-call(bf16[4,2,32,4096]{3,2,1,0:T(8,128)(2,1)} %bitcast.213, ...), custom_call_target="tpu_custom_call" | custom-call | flops 24999999488 | bytes 100663296 | tf_op jit(solution)/shard_map/pallas_call | solution.py:325
  221.1 0.9 convert_bitcast_fusion
  222.0 3.9 fusion.50
  226.3 1.6 fusion.40
  227.9 0.4 add_convert_fusion.5.refs_6_
  228.3 1.0 copy-done.23
  229.3 2.3 fusion.53
  231.7 0.6 multiply_convert_fusion.9
  232.3 1.5 copy-done.2
  233.8 1.0 copy-done.8
  235.8 1.8 fusion.22
  237.6 5.4 fusion.47
  243.4 0.8 multiply_convert_fusion.8.refs_4_
  244.2 0.4 copy-done.29
  244.6 0.9 copy-done.7
  245.5 1.4 fusion.51
  247.3 0.4 add_convert_fusion.4.refs_2_
  247.7 0.5 slice-done.3
  248.2 7.5 %multiply_convert_fusion.2 = (bf16[512,4096]{1,0:T(8,128)(2,1)S(1)}, f32[512,4096]{1,0:T(8,128)}) fusion(bf16[512,1024]{1,0:T(8,128)(2,1)S(1)} %add_convert_fusion.4.refs_2_, bf16[1024,4096]{1,0:T(8,128)(2,1)S(1)} %bitcast.231), kind=kOutput, calls=%fused_computation.2 | convolution fusion | flops 4305453056 | bytes 22020096 | tf_op jit(solution)/shard_map/dot_general | solution.py:779
  255.7 8.5 %fusion.52 = (f32[512]{0:T(512)S(1)}, f32[512,1024]{1,0:T(8,128)S(1)}) fusion(f32[512,1024]{1,0:T(8,128)S(1)} %get-tuple-element.204, bf16[512,4096]{1,0:T(8,128)(2,1)S(1)} %get-tuple-element.205.refs_0_, bf16[4096,1024]{1,0:T(8,128)(2,1)} %bitcast.232), kind=kOutput, calls=%fused_computation.192 | convolution fusion | flops 4296539648 | bytes 16779264 | tf_op jit(solution)/shard_map/dot_general | solution.py:779
  264.7 1.0 fusion.23
  265.7 0.7 multiply_convert_fusion.7.refs_1_
  266.5 1.0 copy-done.19
  267.4 11.7 %multiply_convert_fusion.1.refs_3_ = bf16[512,4096]{1,0:T(8,128)(2,1)} fusion(f32[512,4096]{1,0:T(8,128)} %get-tuple-element.206, bf16[512,1024]{1,0:T(8,128)(2,1)S(1)} %multiply_convert_fusion.7.refs_1_, bf16[4096,1024]{1,0:T(8,128)(2,1)} %bitcast.233), kind=kOutput, calls=%fused_computation.1 | convolution fusion | flops 4313841664 | bytes 22020096 | tf_op jit(solution)/shard_map/dot_general | solution.py:783
  279.2 8.8 %multiply_reduce_fusion.1 = (bf16[1024]{0:T(1024)(128)(2,1)S(1)}, f32[512]{0:T(512)S(1)}, f32[512]{0:T(512)S(1)}, bf16[1024]{0:T(1024)(128)(2,1)S(1)}, f32[512,1024]{1,0:T(8,128)S(1)}) fusion(f32[512,1024]{1,0:T(8,128)S(1)} %get-tuple-element.204, f32[512]{0:T(512)S(1)} %add_rsqrt_fusion.2, f32[512]{0:T(512)S(1)} %broadcast_multiply_fusion.14, ...), kind=kOutput, calls=%fused_computation.49 | convolution fusion | flops 4299682816 | bytes 16793600 | tf_op jit(solution)/shard_map/dot_general | solution.py:783
  288.0 1.7 fusion.46
  289.8 2.4 multiply_reduce_fusion.2
  292.2 3.6 fusion.12
  295.8 0.4 collective-permute-start.3
  296.3 0.7 pad_add_fusion.sc_ref
  297.1 3.3 multiply_convert_fusion.5
  300.4 0.8 multiply_convert_fusion.4
  301.4 2.0 copy-done.27
  303.4 2.9 multiply_reduce_fusion.3
  306.3 2.1 fusion.44
  308.3 1.3 convolution_convert_fusion.1.g_ref
  309.9 33.0 %shard_map.281 = (bf16[512,1024]{1,0:T(8,128)(2,1)S(1)}, f32[512,1024]{1,0:T(8,128)}, f32[512,1024]{1,0:T(8,128)}, bf16[512,1024]{1,0:T(8,128)(2,1)S(1)}, bf16[5...) custom-call(s32[2]{0:T(128)S(1)} %pad_add_fusion.sc_ref, ...), custom_call_target="tpu_custom_call" | custom-call | flops 6442450944 | bytes 31457280 | tf_op jit(solution)/shard_map/pallas_call | solution.py:407
  342.9 1.5 pad_maximum_fusion.2
  345.3 0.7 collective-permute-start.1
  346.1 7.8 %convolution_convert_fusion = bf16[1024,1024]{1,0:T(8,128)(2,1)} fusion(bf16[1536,1024]{1,0:T(8,128)(2,1)} %get-tuple-element.80, bf16[1536,1024]{1,0:T(8,128)(2,1)} %get-tuple-element.81), kind=kOutput, calls=%fused_computation.88 | convolution fusion | flops 3222274048 | bytes 8388608 | tf_op jit(solution)/shard_map/dot_general | solution.py:787
  353.9 1.5 pad_maximum_fusion.1.refs_7_
  355.5 2.8 collective-permute-done.2
  358.4 1.1 maximum_bitcast_fusion
  359.5 2.4 add_convert_fusion.2
  361.9 2.0 pad_maximum_fusion.refs_11_
  364.2 4.0 multiply_reduce_fusion.4
  368.3 0.8 multiply_convert_fusion.3
  369.2 11.1 %multiply_convert_fusion.refs_15_ = bf16[512,4096]{1,0:T(8,128)(2,1)S(1)} fusion(f32[512,4096]{1,0:T(8,128)} %get-tuple-element.79, bf16[512,1024]{1,0:T(8,128)(2,1)S(1)} %get-tuple-element.157.refs_13_, bf16[4096,1024]{1,0:T(8,128)(2,1)} %bitcast.227), kind=kOutput, calls=%fused_computation | convolution fusion | flops 4313841664 | bytes 22020096 | tf_op jit(solution)/shard_map/dot_general | solution.py:783
  380.3 6.3 multiply_reduce_fusion
  386.6 0.5 concatenate.97
  387.2 0.8 pad.5
  387.9 3.3 add_convert_fusion
  391.3 269.8 %shard_map.282 = (bf16[24,2,2,2,256,128]{5,4,3,2,1,0:T(8,128)(2,1)}, bf16[2,2,2,32,128]{4,3,2,1,0:T(8,128)(2,1)}, bf16[2,256,1024]{2,1,0:T(8,128)(2,1)}, bf16[24...) custom-call(bf16[512,4096]{1,0:T(8,128)(2,1)} %copy-done.31, bf16[512,1024]{1,0:T(8,128)(2,1)} %copy-done.19, ...), custom_call_target="tpu_custom_call" | custom-call | flops 26843545600 | bytes 104857600 | tf_op jit(solution)/shard_map/pallas_call | solution.py:632
  661.1 0.7 convert_bitcast_fusion.1
  661.8 0.6 slice_bitcast_fusion.3
  662.4 0.6 slice_bitcast_fusion
  663.0 0.6 slice_bitcast_fusion.1
  663.6 2.8 bitcast_convert_fusion
  666.4 13.6 %shard_map.283 = (f32[1024,1024]{1,0:T(8,128)}, f32[256,4096]{1,0:T(8,128)}, f32[256,1024]{1,0:T(8,128)}, f32[256,2048]{1,0:T(8,128)}, f32[256,1024]{1,0:T(8,128...) custom-call(bf16[24,8,256,128]{3,2,1,0:T(8,128)(2,1)} %bitcast.150), custom_call_target="tpu_custom_call" | custom-call | bytes 37748736 | tf_op jit(solution)/shard_map/pallas_call | solution.py:699
  680.1 2.5 copy.54
  (144 shorter events, 4.4 us)
Async XLA Ops:
  225.9 2.4 copy-start.6
  225.9 3.4 copy-start.26
  228.3 1.0 copy-start.23
  231.7 2.1 copy-start.2
  231.7 3.5 copy-start.10
  231.7 3.8 copy-start.4
  233.8 1.0 copy-start.8
  233.8 1.9 copy-start.1
  234.8 2.8 collective-permute-start
  243.0 1.6 copy-start.29
  243.4 2.1 copy-start.7
  243.4 4.3 slice-start.2
  244.2 2.7 copy-start.24
  245.5 2.7 slice-start.3
  247.7 8.1 %copy-start.25 = (bf16[512,1024]{1,0:T(8,128)(2,1)}, bf16[512,1024]{1,0:T(8,128)(2,1)S(1)}, u32[]{:S(2)}) copy-start(bf16[512,1024]{1,0:T(8,128)(2,1)S(1)} %add_convert_fusion.4.refs_2_) | copy-start | bytes 3145732
  255.7 8.5 %copy-start.31 = (bf16[512,4096]{1,0:T(8,128)(2,1)}, bf16[512,4096]{1,0:T(8,128)(2,1)S(1)}, u32[]{:S(2)}) copy-start(bf16[512,4096]{1,0:T(8,128)(2,1)S(1)} %get-tuple-element.205.refs_0_) | copy-start | bytes 12582916
  266.5 1.0 copy-start.19
  289.7 2.4 copy-start.20
  289.8 2.4 copy-start.9
  292.2 4.9 copy-start.3
  295.8 1.3 collective-permute-start.3
  300.4 1.0 copy-start.13
  300.4 2.9 copy-start.27
  301.3 5.0 copy-start.15
  306.3 2.1 copy-start.28
  308.3 1.3 copy-start.21
  308.3 1.6 copy-start
  344.5 15.0 %collective-permute-start.4 = (bf16[512,2048]{1,0:T(8,128)(2,1)}, bf16[512,2048]{1,0:T(8,128)(2,1)}, u32[]{:S(2)}, u32[]{:S(2)}) collective-permute-start(bf16[512,2048]{1,0:T(8,128)(2,1)} %pad_maximum_fusion.2), channel_id=1, source_target_pairs={{0,4},{4,0},{8,12},{12,8},{16,20},{20,16},{24,28},{28,24},{1,5},{5... | collective-permute-start | bytes 6291464 | tf_op jit(solution)/shard_map/ppermute | solution.py:792
  345.3 10.2 %collective-permute-start.1 = (bf16[256,1024]{1,0:T(8,128)(2,1)S(1)}, bf16[256,1024]{1,0:T(8,128)(2,1)S(1)}, u32[]{:S(2)}, u32[]{:S(2)}) collective-permute-start(bf16[256,1024]{1,0:T(8,128)(2,1)S(1)} %get-tuple-element.172), channel_id=1, source_target_pairs={{0,0},{1,1},{2,4},{3,5},{4,2},{5,3},{6,6},{7,7},{8,8},{9,9},{10,12... | collective-permute-start | bytes 1572872 | tf_op jit(solution)/shard_map/ppermute | solution.py:807
  346.0 12.4 %collective-permute-start.2 = (bf16[256,1024]{1,0:T(8,128)(2,1)S(1)}, bf16[256,1024]{1,0:T(8,128)(2,1)S(1)}, u32[]{:S(2)}, u32[]{:S(2)}) collective-permute-start(bf16[256,1024]{1,0:T(8,128)(2,1)S(1)} %get-tuple-element.173), channel_id=1, source_target_pairs={{0,1},{1,0},{2,5},{3,4},{4,3},{5,2},{6,7},{7,6},{8,9},{9,8},{10,13... | collective-permute-start | bytes 1572872 | tf_op jit(solution)/shard_map/ppermute | solution.py:808
  346.0 7.9 %copy-start.14 = (bf16[512,1024]{1,0:T(8,128)(2,1)S(1)}, bf16[512,1024]{1,0:T(8,128)(2,1)}, u32[]{:S(2)}) copy-start(bf16[512,1024]{1,0:T(8,128)(2,1)} %copy-done.13) | copy-start | bytes 3145732
  346.1 7.9 %copy-start.16 = (bf16[512,1024]{1,0:T(8,128)(2,1)S(1)}, bf16[512,1024]{1,0:T(8,128)(2,1)}, u32[]{:S(2)}) copy-start(bf16[512,1024]{1,0:T(8,128)(2,1)} %copy-done.15) | copy-start | bytes 3145732
  346.1 17.8 %slice-start.4 = ((s8[6291456]{0:T(1024)(128)(4,1)}), s8[4194304]{0:T(1024)(128)(4,1)S(1)}, s32[]{:S(2)}) async-start(s8[6291456]{0:T(1024)(128)(4,1)} %bitcast.234), calls=%async_computation.4 | async-start | bytes 8388608
  355.5 4.0 copy-start.17
  355.5 4.0 copy-start.18
  355.5 8.4 %slice-start.5 = ((s8[6291456]{0:T(1024)(128)(4,1)}), s8[2097152]{0:T(1024)(128)(4,1)S(1)}, s32[]{:S(2)}) async-start(s8[6291456]{0:T(1024)(128)(4,1)} %bitcast.234), calls=%async_computation.5 | async-start | bytes 4194304
  361.9 2.4 copy-start.5
  364.2 4.1 copy-start.12
  368.3 12.0 %slice-start = ((s8[8388608]{0:T(1024)(128)(4,1)}), s8[4194304]{0:T(1024)(128)(4,1)S(1)}, s32[]{:S(2)}) async-start(s8[8388608]{0:T(1024)(128)(4,1)} %bitcast.224), calls=%async_computation | async-start | bytes 8388608
  369.1 11.1 %copy-start.22 = (bf16[512,1024]{1,0:T(8,128)(2,1)}, bf16[512,1024]{1,0:T(8,128)(2,1)S(1)}, u32[]{:S(2)}) copy-start(bf16[512,1024]{1,0:T(8,128)(2,1)S(1)} %get-tuple-element.157.refs_13_) | copy-start | bytes 3145732
  369.1 11.1 %copy-start.11 = (bf16[2,256,1024]{2,1,0:T(8,128)(2,1)S(1)}, bf16[2,256,1024]{2,1,0:T(8,128)(2,1)}, u32[]{:S(2)}) copy-start(bf16[2,256,1024]{2,1,0:T(8,128)(2,1)} %get-tuple-element.83) | copy-start | bytes 3145732
  369.1 11.1 %slice-start.1 = ((s8[8388608]{0:T(1024)(128)(4,1)}), s8[4194304]{0:T(1024)(128)(4,1)S(1)}, s32[]{:S(2)}) async-start(s8[8388608]{0:T(1024)(128)(4,1)} %bitcast.224), calls=%async_computation.1 | async-start | bytes 8388608
  380.2 6.3 copy-start.30
